TPU v7x, 256 devices: a whole 4x4x8 slice. The times are simulated.
256 devices in a mesh: blk: 32 (over x_lo, z, core), aux: 8 (over y, x_hi).
Axes of the slice: x: 4 (x_hi: 2, x_lo: 2; x = x_hi * 2 + x_lo), y: 4, z: 8, core: 2. Of those that a mesh axis runs over, the one named last changes fastest.
Arguments:
- factors: bfloat16 [128, 8192, 1024], P('aux', 'blk'), may hold values from -0.31445312 to 0.31445312
Outputs:
- exchange_band: float32 [8192, 4, 256], P('blk', None, 'aux')
All inputs are finite; a program needn't handle non-finite values.
Results may differ from a plain program's by a relative error of at most 0.0003.
Values may be sent and summed in bfloat16 or wider, within the bound.
No kernel may reach another device: no remote copies, remote signals or barrier semaphores. Data moves between devices by JAX's collectives and lax.ppermute only.
A program may use at most 128 MiB of HBM per device.

v0:
```python
import jax
import jax.numpy as jnp
from jax import lax
from jax.sharding import PartitionSpec as P

STEPS = 4


def from_behind(value, axis, steps):
    count = lax.axis_size(axis)
    pairs = [(source, (source + steps) % count) for source in range(count)]
    return lax.ppermute(value, axis, pairs)


def contract(own, other):
    return lax.dot_general(
        own, other, (((0, 2), (0, 2)), ((), ())), preferred_element_type=jnp.float32
    )


def local(factors):
    tiles = []
    current = factors
    for step in range(STEPS):
        if step == 0:
            other = factors
        else:
            current = from_behind(current, "blk", 1)
            other = current
        tile = contract(factors, other)
        tiles.append(tile)
    stacked = jnp.stack(tiles, axis=1)
    stacked = lax.psum_scatter(stacked, "aux", scatter_dimension=2, tiled=True)
    return stacked


def solution(mesh):
    placed = (P("aux", "blk", None),)
    return jax.shard_map(
        local, mesh=mesh, in_specs=placed, out_specs=P("blk", None, "aux"), check_vma=False
    )
```

profile of v0, /device:TPU:16, one launch (start us, length us, event | category | flops | bytes accessed | tf_op | source)
XLA Modules:
  0.0 401.2 jit_solution(14259979675084593338)
XLA Ops:
  6.5 0.0 all-reduce.3.cloned.1.call-start
  6.5 0.0 copy-start
  6.5 0.0 collective-permute-start
  6.5 97.6 %collective-permute-done = bf16[16,256,1024]{2,1,0:T(8,128)(2,1)S(1)} collective-permute-done((bf16[16,256,1024]{2,1,0:T(8,128)(2,1)}, bf16[16,256,1024]{2,1,0:T(8,128)(2,1)S(1)}, u32[]{:S(2)}, u32[]{:S(2)}) %collective-permute-start) | collective-permute-done | bytes 8388640 | tf_op jit(solution)/shard_map/ppermute | solution.py:12
  104.2 0.0 collective-permute-start.1
  104.2 95.1 %collective-permute-done.1 = bf16[16,256,1024]{2,1,0:T(8,128)(2,1)} collective-permute-done((bf16[16,256,1024]{2,1,0:T(8,128)(2,1)S(1)}, bf16[16,256,1024]{2,1,0:T(8,128)(2,1)}, u32[]{:S(2)}, u32[]{:S(2)}) %collective-permute-start.1) | collective-permute-done | bytes 8388640 | tf_op jit(solution)/shard_map/ppermute | solution.py:12
  199.3 0.0 collective-permute-start.2
  199.3 8.1 %convolution_bitcast_fusion.3 = f32[256,1,256]{2,0,1:T(8,128)S(1)} fusion(bf16[16,256,1024]{2,1,0:T(8,128)(2,1)} %param.1), kind=kOutput, calls=%fused_computation.3 | convolution fusion | flops 2147483648 | bytes 8650752 | tf_op jit(solution)/shard_map/dot_general | solution.py:16
  207.4 0.0 copy-done
  207.4 2.4 convolution_bitcast_fusion.2
  209.8 5.7 %convolution_bitcast_fusion.1 = f32[256,1,256]{2,0,1:T(8,128)S(1)} fusion(bf16[16,256,1024]{2,1,0:T(8,128)(2,1)S(1)} %copy-done, bf16[16,256,1024]{2,1,0:T(8,128)(2,1)} %collective-permute-done.1), kind=kOutput, calls=%fused_computation.1 | convolution fusion | flops 2147483648 | bytes 17039360 | tf_op jit(solution)/shard_map/dot_general | solution.py:16
  215.5 0.0 copy-start.1
  215.5 79.0 %collective-permute-done.2 = bf16[16,256,1024]{2,1,0:T(8,128)(2,1)} collective-permute-done((bf16[16,256,1024]{2,1,0:T(8,128)(2,1)}, bf16[16,256,1024]{2,1,0:T(8,128)(2,1)}, u32[]{:S(2)}, u32[]{:S(2)}) %collective-permute-start.2) | collective-permute-done | bytes 8388640 | tf_op jit(solution)/shard_map/ppermute | solution.py:12
  294.6 5.7 %convolution_bitcast_fusion = f32[256,1,256]{2,0,1:T(8,128)S(1)} fusion(bf16[16,256,1024]{2,1,0:T(8,128)(2,1)S(1)} %copy-done, bf16[16,256,1024]{2,1,0:T(8,128)(2,1)} %collective-permute-done.2), kind=kOutput, calls=%fused_computation | convolution fusion | flops 2147483648 | bytes 17039360 | tf_op jit(solution)/shard_map/dot_general | solution.py:16
  300.3 0.1 pad_maximum_fusion
  300.4 1.4 copy.3
  301.7 0.0 all-reduce.3.cloned.1.call-update
  301.8 0.0 copy-done.1
  301.8 0.6 dynamic-slice
  303.0 89.7 %all-reduce.3.cloned.1.call-done = f32[256,4,256]{0,1,2:T(4,128)} async-done(((f32[256,4,256]{0,1,2:T(4,128)}), f32[256,4,256]{0,1,2:T(4,128)}) %all-reduce.3.cloned.1.call-update) | async-done | bytes 1048592
  392.7 0.9 constant_dynamic-slice_fusion
  393.6 0.7 copy.4
Async XLA Ops:
  6.5 386.2 %all-reduce.3.cloned.1.call-start = ((), (), s32[]{:S(2)}) async-start(), calls=%async_computation | async-start | bytes 2097152
  6.5 200.9 %copy-start = (bf16[16,256,1024]{2,1,0:T(8,128)(2,1)S(1)}, bf16[16,256,1024]{2,1,0:T(8,128)(2,1)}, u32[]{:S(2)}) copy-start(bf16[16,256,1024]{2,1,0:T(8,128)(2,1)} %param.1) | copy-start | bytes 25165828
  6.5 97.6 %collective-permute-start = (bf16[16,256,1024]{2,1,0:T(8,128)(2,1)}, bf16[16,256,1024]{2,1,0:T(8,128)(2,1)S(1)}, u32[]{:S(2)}, u32[]{:S(2)}) collective-permute-start(bf16[16,256,1024]{2,1,0:T(8,128)(2,1)} %param.1), channel_id=1, source_target_pairs={{0,8},{8,16},{16,24},{24,32},{32,40},{40,48},{48,56},{56,64},{64,7... | collective-permute-start | bytes 25165832 | tf_op jit(solution)/shard_map/ppermute | solution.py:12
  104.2 95.1 %collective-permute-start.1 = (bf16[16,256,1024]{2,1,0:T(8,128)(2,1)S(1)}, bf16[16,256,1024]{2,1,0:T(8,128)(2,1)}, u32[]{:S(2)}, u32[]{:S(2)}) collective-permute-start(bf16[16,256,1024]{2,1,0:T(8,128)(2,1)S(1)} %collective-permute-done), channel_id=1, source_target_pairs={{0,8},{8,16},{16,24},{24,32},{32,40},{40,48},{48,56},{56,64},{64,7... | collective-permute-start | bytes 25165832 | tf_op jit(solution)/shard_map/ppermute | solution.py:12
  199.3 95.3 %collective-permute-start.2 = (bf16[16,256,1024]{2,1,0:T(8,128)(2,1)}, bf16[16,256,1024]{2,1,0:T(8,128)(2,1)}, u32[]{:S(2)}, u32[]{:S(2)}) collective-permute-start(bf16[16,256,1024]{2,1,0:T(8,128)(2,1)} %collective-permute-done.1), channel_id=1, source_target_pairs={{0,8},{8,16},{16,24},{24,32},{32,40},{40,48},{48,56},{56,64},{64,7... | collective-permute-start | bytes 25165832 | tf_op jit(solution)/shard_map/ppermute | solution.py:12
  215.5 86.3 %copy-start.1 = (u32[256]{0:T(256)S(1)}, u32[256]{0:T(256)}, u32[]{:S(2)}) copy-start(u32[256]{0:T(256)} %constant.2) | copy-start | bytes 3076
Sparse Core Ops, SparseCore 0:
  301.9 90.7 all-reduce.2
where the time goes:
time: 404 us; the launch traced here: 401 us
  waiting for transfers between devices  361 us (89%)
  matrix products  21.9 us (5%)
  between operations  14.1 us (3%)
    ppermute x3, waiting for transfers between devices, from_behind(): return lax.ppermute(value, axis, pairs)  272 us
    unnamed x2, waiting for transfers between devices  89.7 us
    dot_general x4, matrix products, contract(): lax.dot_general(own, other, (((0, 2), (0, 2)), ((), ())), preferred_eleme...  21.9 us
  transfers between devices with their start and end apart: 4, of which 4 were waited for; matrix products, arithmetic and copies ran while one was open for 4% of the time, Pallas kernels for 0%

commit v1 on v0

v1 whole, which is shorter than its diff:
```python
import jax
import jax.numpy as jnp
from jax import lax
from jax.sharding import PartitionSpec as P

COUNT = 32
HALF = 8
SLICES = 8

TO_MATE = [(b, b ^ 1) for b in range(COUNT)]
TO_NEAR = [(b, (b - 1 if b % 2 == 0 else b + 1) % COUNT) for b in range(COUNT)]
FROM_FAR_NEAR = [(b, (b + 2 if b % 2 == 0 else b - 2) % COUNT) for b in range(COUNT)]
FROM_FAR_MATE = [(b, (b - 2 if b % 2 == 0 else b + 2) % COUNT) for b in range(COUNT)]
UP_ONE = [(b, (b + 1) % COUNT) for b in range(COUNT)]
UP_TWO = [(b, (b + 2) % COUNT) for b in range(COUNT)]
LAST_EVEN = [(b, (b + 2) % COUNT) for b in range(0, COUNT, 2)]
LAST_ODD = [(b, (b + 1) % COUNT) for b in range(1, COUNT, 2)]


def send(value, pairs):
    return lax.ppermute(value, "blk", pairs)


def contract(one, other):
    return lax.dot_general(
        one, other, (((0, 2), (0, 2)), ((), ())), preferred_element_type=jnp.float32
    )


def reduced(tiles):
    count = len(tiles)
    parts = jnp.stack(tiles).reshape(count, SLICES, 32, 256).transpose(1, 0, 2, 3)
    parts = lax.all_to_all(parts, "aux", 0, 0)
    return parts.sum(0)


def local(factors):
    odd = lax.axis_index("blk") % 2
    is_odd = odd == 1
    own = lax.dynamic_slice_in_dim(factors, odd * HALF, HALF, 0)
    rest = lax.dynamic_slice_in_dim(factors, (1 - odd) * HALF, HALF, 0)
    near = send(rest, TO_NEAR)
    mate = send(rest, TO_MATE)
    far_near = send(own, FROM_FAR_NEAR)
    far_mate = send(own, FROM_FAR_MATE)

    def oriented(one, other):
        tile = contract(one, other)
        return jnp.where(is_odd, tile.T, tile)

    first = reduced([contract(own, own), contract(mate, mate), oriented(own, mate)])
    own_own, mate_mate, own_mate = first[0], first[1], first[2]
    second = reduced(
        [oriented(near, own), oriented(near, mate), oriented(far_near, own), oriented(far_near, mate)]
    )
    near_own, near_mate, far_own, far_mate_ = second[0], second[1], second[2], second[3]

    zero = jnp.zeros_like(own_own)
    pick = lambda even, odd_: jnp.where(is_odd, odd_, even)
    from_mate = send(mate_mate, TO_MATE)
    from_below = send(
        jnp.stack([pick(own_mate, near_own), near_mate, pick(far_mate_, zero)]), UP_ONE
    )
    from_two = send(
        jnp.stack([pick(zero, far_own), pick(zero, far_mate_)]), UP_TWO
    )
    s0 = own_own + from_mate
    s1 = pick(near_own, own_mate) + from_below[0]
    s2 = pick(far_own, zero) + from_below[1] + from_two[0]
    s3 = from_below[2] + from_two[1]

    near, s3 = lax.optimization_barrier((near, s3))
    last = reduced([oriented(near, far_mate)])[0]
    s3 = s3 + send(last, LAST_EVEN) + send(last, LAST_ODD)
    return jnp.stack([s0, s1, s2, s3]).transpose(2, 0, 1)


def solution(mesh):
    placed = (P("aux", "blk", None),)
    return jax.shard_map(
        local, mesh=mesh, in_specs=placed, out_specs=P("blk", None, "aux"), check_vma=False
    )
```

time: 404 us -> 220 us (0.54)
  waiting for transfers between devices: 361 us -> 134 us
  starting transfers between devices: 0.01 us -> 33.8 us
  matrix products: 21.9 us -> 38 us
  between operations: 14.1 us -> 0.27 us
  local copies, waits for them, and re-layouts: 3.55 us -> 8.76 us
    ppermute x3 -> x9, waiting for transfers between devices: 272 us -> 77.3 us  [send(): return lax.ppermute(value, 'blk', pairs)]
    unnamed x2 -> x0, waiting for transfers between devices: 89.7 us -> none
    all_to_all x0 -> x3, waiting for transfers between devices: none -> 56.5 us  [reduced(): parts = lax.all_to_all(parts, 'aux', 0, 0)]
    all_to_all x0 -> x3, starting transfers between devices: none -> 19.4 us  [reduced(): parts = lax.all_to_all(parts, 'aux', 0, 0)]
    dot_general x4 -> x8, matrix products: 21.9 us -> 38 us  [contract(): lax.dot_general(one, other, (((0, 2), (0, 2)), ((), ())), preferred_eleme...]
    ppermute x3 -> x9, starting transfers between devices: 0.01 us -> 14.4 us  [send(): return lax.ppermute(value, 'blk', pairs)]
    dynamic_slice x0 -> x1, local copies, waits for them, and re-layouts: none -> 7.99 us  [local(): own = lax.dynamic_slice_in_dim(factors, odd * HALF, HALF, 0)]
  transfers between devices with their start and end apart: 4 -> 12, of which waited for: 4 -> 7; matrix products, arithmetic and copies ran while one was open for 4% -> 17% of each run, Pallas kernels for 0% -> 0%
where the time goes in v1:
time: 220 us; the launch traced here: 218 us
  waiting for transfers between devices  134 us (61%)
  matrix products  38 us (17%)
  starting transfers between devices  33.8 us (15%)
  local copies, waits for them, and re-layouts  8.76 us (4%)
  other arithmetic  3.92 us (2%)
    ppermute x9, waiting for transfers between devices, send(): return lax.ppermute(value, 'blk', pairs)  77.3 us
    all_to_all x3, waiting for transfers between devices, reduced(): parts = lax.all_to_all(parts, 'aux', 0, 0)  56.5 us
    dot_general x8, matrix products, contract(): lax.dot_general(one, other, (((0, 2), (0, 2)), ((), ())), preferred_eleme...  38 us
    all_to_all x3, starting transfers between devices, reduced(): parts = lax.all_to_all(parts, 'aux', 0, 0)  19.4 us
    ppermute x9, starting transfers between devices, send(): return lax.ppermute(value, 'blk', pairs)  14.4 us
    dynamic_slice x1, local copies, waits for them, and re-layouts, local(): own = lax.dynamic_slice_in_dim(factors, odd * HALF, HALF, 0)  7.99 us
  transfers between devices with their start and end apart: 12, of which 7 were waited for; matrix products, arithmetic and copies ran while one was open for 17% of the time, Pallas kernels for 0%

profile of v1, /device:TPU:16, one launch (start us, length us, event | category | flops | bytes accessed | tf_op | source)
XLA Modules:
  0.0 218.5 jit_solution(8243505107295008702)
XLA Ops:
  0.0 8.0 %constant_dynamic-slice_fusion.1 = (bf16[8,256,1024]{2,1,0:T(8,128)(2,1)}, bf16[8,256,1024]{2,1,0:T(8,128)(2,1)}) fusion(bf16[16,256,1024]{2,1,0:T(8,128)(2,1)} %param.1, s32[]{:T(128)S(6)} %select_n.76, s32[]{:T(128)S(6)} %select_n.77), kind=kLoop, calls=%fused_computation.32 | loop fusion | bytes 16777224 | tf_op jit(solution)/shard_map/dynamic_slice | solution.py:40
  8.0 6.9 %collective-permute-start.2 = (bf16[8,256,1024]{2,1,0:T(8,128)(2,1)}, bf16[8,256,1024]{2,1,0:T(8,128)(2,1)}, u32[]{:S(2)}, u32[]{:S(2)}) collective-permute-start(bf16[8,256,1024]{2,1,0:T(8,128)(2,1)} %get-tuple-element.10), channel_id=1, source_target_pairs={{0,248},{8,16},{16,8},{24,32},{32,24},{40,48},{48,40},{56,64},{64,... | collective-permute-start | bytes 12582920 | tf_op jit(solution)/shard_map/ppermute | solution.py:21
  14.9 4.1 %collective-permute-start.6 = (bf16[8,256,1024]{2,1,0:T(8,128)(2,1)}, bf16[8,256,1024]{2,1,0:T(8,128)(2,1)}, u32[]{:S(2)}, u32[]{:S(2)}) collective-permute-start(bf16[8,256,1024]{2,1,0:T(8,128)(2,1)} %get-tuple-element.9), channel_id=1, source_target_pairs={{0,240},{8,24},{16,0},{24,40},{32,16},{40,56},{48,32},{56,72},{64,... | collective-permute-start | bytes 12582920 | tf_op jit(solution)/shard_map/ppermute | solution.py:21
  19.0 4.7 %fusion.3 = f32[256,256,1]{1,0,2:T(8,128)S(1)} fusion(bf16[8,256,1024]{2,1,0:T(8,128)(2,1)} %get-tuple-element.9), kind=kOutput, calls=%fused_computation.33 | convolution fusion | flops 1073741824 | bytes 4456448 | tf_op jit(solution)/shard_map/dot_general | solution.py:25
  23.8 4.7 %convolution_bitcast_fusion.5 = f32[256,256]{1,0:T(8,128)S(1)} fusion(bf16[8,256,1024]{2,1,0:T(8,128)(2,1)} %get-tuple-element.9, bf16[8,256,1024]{2,1,0:T(8,128)(2,1)} %collective-permute-done), kind=kOutput, calls=%fused_computation.5 | convolution fusion | flops 1073741824 | bytes 8650752 | tf_op jit(solution)/shard_map/dot_general | solution.py:25
  28.5 0.1 copy.8
  28.7 4.7 %fusion.4 = f32[256,256,1]{1,0,2:T(8,128)S(1)} fusion(bf16[8,256,1024]{2,1,0:T(8,128)(2,1)} %collective-permute-done), kind=kOutput, calls=%fused_computation.34 | convolution fusion | flops 1073741824 | bytes 4456448 | tf_op jit(solution)/shard_map/dot_general | solution.py:25
  33.5 1.0 maximum_bitcast_fusion.1
  34.5 7.0 %all-to-all-start = ((f32[8,3,32,256]{3,2,1,0:T(8,128)}), f32[8,3,32,256]{3,2,1,0:T(8,128)S(1)}, u32[]{:S(2)}, u32[]{:S(2)}) async-start(f32[8,3,32,256]{3,2,1,0:T(8,128)} %maximum_bitcast_fusion.1), calls=%async_computation | async-start | bytes 1572864 | tf_op jit(solution)/shard_map/all_to_all | solution.py:33
  41.5 64.2 %collective-permute-done.2 = bf16[8,256,1024]{2,1,0:T(8,128)(2,1)} collective-permute-done((bf16[8,256,1024]{2,1,0:T(8,128)(2,1)}, bf16[8,256,1024]{2,1,0:T(8,128)(2,1)}, u32[]{:S(2)}, u32[]{:S(2)}) %collective-permute-start.2) | collective-permute-done | bytes 4194336 | tf_op jit(solution)/shard_map/ppermute | solution.py:21
  105.7 4.7 %convolution_bitcast_fusion.4 = f32[256,256]{1,0:T(8,128)S(1)} fusion(bf16[8,256,1024]{2,1,0:T(8,128)(2,1)} %collective-permute-done.2, bf16[8,256,1024]{2,1,0:T(8,128)(2,1)} %get-tuple-element.9), kind=kOutput, calls=%fused_computation.4 | convolution fusion | flops 1073741824 | bytes 8650752 | tf_op jit(solution)/shard_map/dot_general | solution.py:25
  110.4 0.1 copy.12
  110.6 4.7 %convolution_bitcast_fusion.3 = f32[256,256]{1,0:T(8,128)S(1)} fusion(bf16[8,256,1024]{2,1,0:T(8,128)(2,1)} %collective-permute-done.2, bf16[8,256,1024]{2,1,0:T(8,128)(2,1)} %collective-permute-done), kind=kOutput, calls=%fused_computation.3 | convolution fusion | flops 1073741824 | bytes 8650752 | tf_op jit(solution)/shard_map/dot_general | solution.py:25
  115.3 0.1 copy.13
  115.5 4.7 %convolution_bitcast_fusion.2 = f32[256,256]{1,0:T(8,128)S(1)} fusion(bf16[8,256,1024]{2,1,0:T(8,128)(2,1)} %collective-permute-done.3, bf16[8,256,1024]{2,1,0:T(8,128)(2,1)} %get-tuple-element.9), kind=kOutput, calls=%fused_computation.2 | convolution fusion | flops 1073741824 | bytes 8650752 | tf_op jit(solution)/shard_map/dot_general | solution.py:25
  120.3 4.7 %convolution_bitcast_fusion.1 = f32[256,256]{1,0:T(8,128)S(1)} fusion(bf16[8,256,1024]{2,1,0:T(8,128)(2,1)} %collective-permute-done.3, bf16[8,256,1024]{2,1,0:T(8,128)(2,1)} %collective-permute-done), kind=kOutput, calls=%fused_computation.1 | convolution fusion | flops 1073741824 | bytes 8650752 | tf_op jit(solution)/shard_map/dot_general | solution.py:25
  125.0 0.1 copy.14
  125.2 0.1 copy.15
  125.4 1.1 maximum_bitcast_fusion
  126.5 34.5 %all-to-all-done = f32[8,3,32,256]{3,2,1,0:T(8,128)S(1)} async-done(((f32[8,3,32,256]{3,2,1,0:T(8,128)}), f32[8,3,32,256]{3,2,1,0:T(8,128)S(1)}, u32[]{:S(2)}, u32[]{:S(2)}) %all-to-all-start) | async-done | bytes 786464 | tf_op jit(solution)/shard_map/all_to_all | solution.py:33
  161.0 6.4 %all-to-all-start.1 = ((f32[8,4,32,256]{3,2,1,0:T(8,128)}), f32[8,4,32,256]{3,2,1,0:T(8,128)S(1)}, u32[]{:S(2)}, u32[]{:S(2)}) async-start(f32[8,4,32,256]{3,2,1,0:T(8,128)} %maximum_bitcast_fusion), calls=%async_computation.1 | async-start | bytes 2097152 | tf_op jit(solution)/shard_map/all_to_all | solution.py:33
  167.5 15.0 %all-to-all-done.1 = f32[8,4,32,256]{3,2,1,0:T(8,128)S(1)} async-done(((f32[8,4,32,256]{3,2,1,0:T(8,128)}), f32[8,4,32,256]{3,2,1,0:T(8,128)S(1)}, u32[]{:S(2)}, u32[]{:S(2)}) %all-to-all-start.1) | async-done | bytes 1048608 | tf_op jit(solution)/shard_map/all_to_all | solution.py:33
  182.7 7.0 %collective-permute-done.5 = f32[2,32,256]{2,1,0:T(8,128)S(1)} collective-permute-done((f32[2,32,256]{2,1,0:T(8,128)S(1)}, f32[2,32,256]{2,1,0:T(8,128)S(1)}, u32[]{:S(2)}, u32[]{:S(2)}) %collective-permute-start.5) | collective-permute-done | bytes 65568 | tf_op jit(solution)/shard_map/ppermute | solution.py:21
  189.8 4.7 %convolution_bitcast_fusion = f32[256,256]{1,0:T(8,128)S(1)} fusion(bf16[8,256,1024]{2,1,0:T(8,128)(2,1)} %collective-permute-done.2, bf16[8,256,1024]{2,1,0:T(8,128)(2,1)} %collective-permute-done.6), kind=kOutput, calls=%fused_computation | convolution fusion | flops 1073741824 | bytes 8650752 | tf_op jit(solution)/shard_map/dot_general | solution.py:25
  194.7 0.7 bitcast_select_fusion
  195.4 6.0 %all-to-all-start.2 = ((f32[8,1,32,256]{3,2,1,0:T(8,128)}), f32[8,1,32,256]{3,2,1,0:T(8,128)S(1)}, u32[]{:S(2)}, u32[]{:S(2)}) async-start(f32[8,1,32,256]{3,2,1,0:T(8,128)} %bitcast.35), calls=%async_computation.2 | async-start | bytes 524288 | tf_op jit(solution)/shard_map/all_to_all | solution.py:33
  201.5 7.1 %all-to-all-done.2 = f32[8,1,32,256]{3,2,1,0:T(8,128)S(1)} async-done(((f32[8,1,32,256]{3,2,1,0:T(8,128)}), f32[8,1,32,256]{3,2,1,0:T(8,128)S(1)}, u32[]{:S(2)}, u32[]{:S(2)}) %all-to-all-start.2) | async-done | bytes 262176 | tf_op jit(solution)/shard_map/all_to_all | solution.py:33
  208.5 1.9 collective-permute-start.7
  210.5 1.3 collective-permute-start.8
  211.8 4.7 %collective-permute-done.7 = f32[32,256]{1,0:T(8,128)S(1)} collective-permute-done((f32[32,256]{1,0:T(8,128)S(1)}, f32[32,256]{1,0:T(8,128)S(1)}, u32[]{:S(2)}, u32[]{:S(2)}) %collective-permute-start.7) | collective-permute-done | bytes 32800 | tf_op jit(solution)/shard_map/ppermute | solution.py:21
  216.5 1.4 collective-permute-done.8
  217.8 0.7 maximum_bitcast_fusion.2
  (25 shorter events, 0.7 us)
Async XLA Ops:
  8.0 15.8 %collective-permute-start = (bf16[8,256,1024]{2,1,0:T(8,128)(2,1)}, bf16[8,256,1024]{2,1,0:T(8,128)(2,1)}, u32[]{:S(2)}, u32[]{:S(2)}) collective-permute-start(bf16[8,256,1024]{2,1,0:T(8,128)(2,1)} %get-tuple-element.10), channel_id=1, source_target_pairs={{0,8},{8,0},{16,24},{24,16},{32,40},{40,32},{48,56},{56,48},{64,72... | collective-permute-start | bytes 12582920 | tf_op jit(solution)/shard_map/ppermute | solution.py:21
  8.0 97.7 %collective-permute-start.2 = (bf16[8,256,1024]{2,1,0:T(8,128)(2,1)}, bf16[8,256,1024]{2,1,0:T(8,128)(2,1)}, u32[]{:S(2)}, u32[]{:S(2)}) collective-permute-start(bf16[8,256,1024]{2,1,0:T(8,128)(2,1)} %get-tuple-element.10), channel_id=1, source_target_pairs={{0,248},{8,16},{16,8},{24,32},{32,24},{40,48},{48,40},{56,64},{64,... | collective-permute-start | bytes 12582920 | tf_op jit(solution)/shard_map/ppermute | solution.py:21
  14.9 100.6 %collective-permute-start.3 = (bf16[8,256,1024]{2,1,0:T(8,128)(2,1)}, bf16[8,256,1024]{2,1,0:T(8,128)(2,1)}, u32[]{:S(2)}, u32[]{:S(2)}) collective-permute-start(bf16[8,256,1024]{2,1,0:T(8,128)(2,1)} %get-tuple-element.9), channel_id=1, source_target_pairs={{0,16},{8,248},{16,32},{24,8},{32,48},{40,24},{48,64},{56,40},{64,... | collective-permute-start | bytes 12582920 | tf_op jit(solution)/shard_map/ppermute | solution.py:21
  14.9 174.9 %collective-permute-start.6 = (bf16[8,256,1024]{2,1,0:T(8,128)(2,1)}, bf16[8,256,1024]{2,1,0:T(8,128)(2,1)}, u32[]{:S(2)}, u32[]{:S(2)}) collective-permute-start(bf16[8,256,1024]{2,1,0:T(8,128)(2,1)} %get-tuple-element.9), channel_id=1, source_target_pairs={{0,240},{8,24},{16,0},{24,40},{32,16},{40,56},{48,32},{56,72},{64,... | collective-permute-start | bytes 12582920 | tf_op jit(solution)/shard_map/ppermute | solution.py:21
  34.5 126.5 %all-to-all-start = ((f32[8,3,32,256]{3,2,1,0:T(8,128)}), f32[8,3,32,256]{3,2,1,0:T(8,128)S(1)}, u32[]{:S(2)}, u32[]{:S(2)}) async-start(f32[8,3,32,256]{3,2,1,0:T(8,128)} %maximum_bitcast_fusion.1), calls=%async_computation | async-start | bytes 1572864 | tf_op jit(solution)/shard_map/all_to_all | solution.py:33
  161.0 21.4 %all-to-all-start.1 = ((f32[8,4,32,256]{3,2,1,0:T(8,128)}), f32[8,4,32,256]{3,2,1,0:T(8,128)S(1)}, u32[]{:S(2)}, u32[]{:S(2)}) async-start(f32[8,4,32,256]{3,2,1,0:T(8,128)} %maximum_bitcast_fusion), calls=%async_computation.1 | async-start | bytes 2097152 | tf_op jit(solution)/shard_map/all_to_all | solution.py:33
  182.5 7.2 %collective-permute-start.4 = (f32[3,32,256]{2,1,0:T(8,128)S(1)}, f32[3,32,256]{2,1,0:T(8,128)S(1)}, u32[]{:S(2)}, u32[]{:S(2)}) collective-permute-start(f32[3,32,256]{2,1,0:T(8,128)S(1)} %pad_maximum_fusion), channel_id=1, source_target_pairs={{0,8},{8,16},{16,24},{24,32},{32,40},{40,48},{48,56},{56,64},{64,7... | collective-permute-start | bytes 294920 | tf_op jit(solution)/shard_map/ppermute | solution.py:21
  182.6 7.1 %collective-permute-start.5 = (f32[2,32,256]{2,1,0:T(8,128)S(1)}, f32[2,32,256]{2,1,0:T(8,128)S(1)}, u32[]{:S(2)}, u32[]{:S(2)}) collective-permute-start(f32[2,32,256]{2,1,0:T(8,128)S(1)} %pad_maximum_fusion.1), channel_id=1, source_target_pairs={{0,16},{8,24},{16,32},{24,40},{32,48},{40,56},{48,64},{56,72},{64,... | collective-permute-start | bytes 196616 | tf_op jit(solution)/shard_map/ppermute | solution.py:21
  195.4 13.1 %all-to-all-start.2 = ((f32[8,1,32,256]{3,2,1,0:T(8,128)}), f32[8,1,32,256]{3,2,1,0:T(8,128)S(1)}, u32[]{:S(2)}, u32[]{:S(2)}) async-start(f32[8,1,32,256]{3,2,1,0:T(8,128)} %bitcast.35), calls=%async_computation.2 | async-start | bytes 524288 | tf_op jit(solution)/shard_map/all_to_all | solution.py:33
  201.4 10.3 %collective-permute-start.1 = (f32[32,256]{1,0:T(8,128)S(1)}, f32[32,256]{1,0:T(8,128)S(1)}, u32[]{:S(2)}, u32[]{:S(2)}) collective-permute-start(f32[32,256]{1,0:T(8,128)S(1)} %get-tuple-element.19), channel_id=1, source_target_pairs={{0,8},{8,0},{16,24},{24,16},{32,40},{40,32},{48,56},{56,48},{64,72... | collective-permute-start | bytes 98312 | tf_op jit(solution)/shard_map/ppermute | solution.py:21
  208.5 7.9 %collective-permute-start.7 = (f32[32,256]{1,0:T(8,128)S(1)}, f32[32,256]{1,0:T(8,128)S(1)}, u32[]{:S(2)}, u32[]{:S(2)}) collective-permute-start(f32[32,256]{1,0:T(8,128)S(1)} %reduce_sum.29), channel_id=1, source_target_pairs={{0,16},{16,32},{32,48},{48,64},{64,80},{80,96},{96,112},{112,128},... | collective-permute-start | bytes 98312 | tf_op jit(solution)/shard_map/ppermute | solution.py:21
  210.5 7.3 %collective-permute-start.8 = (f32[32,256]{1,0:T(8,128)S(1)}, f32[32,256]{1,0:T(8,128)S(1)}, u32[]{:S(2)}, u32[]{:S(2)}) collective-permute-start(f32[32,256]{1,0:T(8,128)S(1)} %reduce_sum.29), channel_id=1, source_target_pairs={{8,16},{24,32},{40,48},{56,64},{72,80},{88,96},{104,112},{120,128}... | collective-permute-start | bytes 98312 | tf_op jit(solution)/shard_map/ppermute | solution.py:21

commit v2 on v0

v2 whole, which is shorter than its diff:
```python
import functools

import jax
import jax.numpy as jnp
from jax import lax
from jax.experimental import pallas as pl
from jax.experimental.pallas import tpu as pltpu
from jax.sharding import PartitionSpec as P

COUNT = 32
HALF = 8
CUT = 6
ROWS = 256
DEPTH = 1024
F32 = jnp.float32
BF16 = jnp.bfloat16
ANY = pl.BlockSpec(memory_space=pl.ANY)
HBM = pl.BlockSpec(memory_space=pltpu.HBM)
VMEM = pl.BlockSpec(memory_space=pltpu.VMEM)

TO_MATE = [(b, b ^ 1) for b in range(COUNT)]
TO_NEAR = [(b, (b - 1 if b % 2 == 0 else b + 1) % COUNT) for b in range(COUNT)]
TO_FAR_NEAR = [(b, (b + 2 if b % 2 == 0 else b - 2) % COUNT) for b in range(COUNT)]
TO_FAR_MATE = [(b, (b - 2 if b % 2 == 0 else b + 2) % COUNT) for b in range(COUNT)]
EVEN_UP = [(b, (b + 2) % COUNT) for b in range(0, COUNT, 2)]


def along_y(shift):
    return [(a, ((a // 2 + shift) % 4) * 2 + a % 2) for a in range(8)]


ACROSS_X = [(a, a ^ 1) for a in range(8)]


def to_upper_even(flip):
    pairs = []
    for b in range(COUNT):
        core = b % 2
        for y in range(4):
            source, target = 2 * y + (core ^ flip), 2 * y + core
            pairs.append((b * 8 + source, (b - core + 2) % COUNT * 8 + target))
    return pairs


def f32(*shape):
    return jax.ShapeDtypeStruct(shape, F32)


def parity():
    return lax.rem(lax.axis_index("blk"), 2)


def call(kernel, out_shape, *args, flops=0, scratch=(), specs=None, hidden=(), limit=16):
    single = not isinstance(out_shape, list)
    moved = sum(a.size * a.dtype.itemsize for a in args)
    return pl.pallas_call(
        kernel,
        out_shape=out_shape,
        in_specs=(specs or [VMEM] * len(args)) + [ANY] * len(hidden),
        out_specs=VMEM if single else [VMEM] * len(out_shape),
        scratch_shapes=list(scratch),
        compiler_params=pltpu.CompilerParams(vmem_limit_bytes=limit << 20),
        cost_estimate=pl.CostEstimate(flops=flops, bytes_accessed=moved, transcendentals=0),
    )(*args, *hidden)


def take_kernel(other, first, count, factors, *refs):
    out, sems = refs[-2:]
    odd = parity()
    base = (1 - odd if other else odd) * HALF + first
    copies = [
        pltpu.make_async_copy(factors.at[base + i], out.at[i], sems.at[i]) for i in range(count)
    ]
    for copy in copies:
        copy.start()
    for copy in copies:
        copy.wait()


def take(factors, other, first, count, after=(), limit=16):
    return call(
        functools.partial(take_kernel, other, first, count),
        jax.ShapeDtypeStruct((count, ROWS, DEPTH), BF16),
        factors,
        scratch=[pltpu.SemaphoreType.DMA((count,))],
        specs=[HBM],
        hidden=after,
        limit=limit,
    )


def dot(lo, hi):
    return lax.dot_general(lo, hi, (((1,), (1,)), ((), ())), preferred_element_type=F32)


def accumulate(totals, pairs, first=0, last=HALF):
    totals[...] = jnp.zeros(totals.shape, F32)
    cuts = {first, last}
    for pair in pairs:
        for operand in pair:
            cuts |= {at for _, at in operand if first < at < last}
    cuts = sorted(cuts)

    def holder(operand, at):
        return [piece for piece in operand if piece[1] <= at][-1]

    for low, high in zip(cuts, cuts[1:]):
        held = [[holder(operand, low) for operand in pair] for pair in pairs]

        def step(q, carry):
            for t, ((lo, lo_at), (hi, hi_at)) in enumerate(held):
                totals[t] += dot(lo[q - lo_at], hi[q - hi_at])
            return carry

        lax.fori_loop(low, high, step, 0)


def by_parity(even, odd):
    for which, action in ((0, even), (1, odd)):
        pl.when(parity() == which)(action)


def row_of(shift, height):
    y = lax.div(lax.axis_index("aux"), 2)
    return pl.multiple_of(lax.rem(y + shift, 4) * height, height)


def spread(totals, outs):
    for shift, out in enumerate(outs):
        out[...] = totals[:, pl.ds(row_of(shift, 64), 64)]


def chip_kernel(own0, own1, mate0, *refs):
    outs, totals = refs[:4], refs[4]
    own, mate = [(own0, 0), (own1, CUT)], [(mate0, 0)]
    by_parity(
        lambda: accumulate(totals, [(own, own), (mate, mate), (own, mate)]),
        lambda: accumulate(totals, [(mate, mate), (own, own), (mate, own)]),
    )
    spread(totals, outs)


def window_kernel(own0, own1, mate0, near0, far0, far1, hidden, *refs):
    outs, totals = refs[:4], refs[4]
    own, far = [(own0, 0), (own1, CUT)], [(far0, 0), (far1, CUT)]
    mate, near = [(mate0, 0)], [(near0, 0)]
    by_parity(
        lambda: accumulate(totals, [(near, own), (near, mate), (far, own), (far, mate)]),
        lambda: accumulate(totals, [(own, near), (own, far), (mate, near), (mate, far)]),
    )
    spread(totals, outs)


def sum_kernel(a, b, c, d, total):
    total[...] = a[...] + b[...] + c[...] + d[...]


def choose_kernel(chip, swapped, lower, keep, give):
    def even():
        keep[0] = chip[0]
        keep[1] = lower[0]
        keep[2] = lower[2]
        keep[3] = jnp.zeros((64, ROWS), F32)
        give[0:2] = chip[1:3]
        give[2] = lower[1]
        give[3] = lower[3]

    def odd():
        keep[0:2] = chip[1:3]
        keep[2] = swapped[1]
        keep[3] = swapped[3]
        give[0] = chip[0]
        give[1] = swapped[0]
        give[2] = swapped[2]
        give[3] = jnp.zeros((64, ROWS), F32)

    by_parity(even, odd)


def split_kernel(keep, given, stay, leave):
    pair = lax.rem(lax.axis_index("aux"), 2)
    for half, out in ((pair, stay), (1 - pair, leave)):
        rows = pl.ds(pl.multiple_of(32 * half, 32), 32)
        out[...] = keep[:, rows] + given[:, rows]


def early_kernel(near0, far0, hidden, total):
    near, far = [(near0, 0)], [(far0, 0)]
    by_parity(
        lambda: accumulate(total, [(near, far)], 0, CUT),
        lambda: accumulate(total, [(far, near)], 0, CUT),
    )


def last_kernel(near0, far1, early, keep, give, total):
    near, far = [(near0, 0)], [(far1, CUT)]
    by_parity(
        lambda: accumulate(total, [(near, far)], CUT, HALF),
        lambda: accumulate(total, [(far, near)], CUT, HALF),
    )
    core = parity()
    for y in range(4):
        for half, out in ((core, keep), (1 - core, give)):
            rows = pl.ds(pl.multiple_of(64 * y + 32 * half, 32), 32)
            out[32 * y : 32 * y + 32] = early[0, rows] + total[0, rows]


def combine_last_kernel(keep, given, *outs):
    for shift, out in enumerate(outs):
        rows = pl.ds(row_of(shift, 32), 32)
        out[...] = keep[rows] + given[rows]


def finish_kernel(stay, come, a, b, out):
    out[0:3] = stay[0:3] + come[0:3]
    out[3] = (stay[3] + come[3]) + (a[...] + b[...])


def sum_along_y(parts):
    return [parts[0]] + [lax.ppermute(parts[d], "aux", along_y(d)) for d in (1, 2, 3)]


def local(factors):
    def send(value, pairs):
        return lax.ppermute(value, "blk", pairs)

    tile = 2 * ROWS * ROWS * DEPTH
    rest = take(factors, True, 0, HALF)
    near = send(rest, TO_NEAR)
    own = [
        take(factors, False, 0, CUT, (rest,)),
        take(factors, False, CUT, HALF - CUT, (rest,)),
    ]
    far_near = [send(part, TO_FAR_NEAR) for part in own]
    far_mate = [send(part, TO_FAR_MATE) for part in own]
    mate = send(take(factors, True, 0, HALF, own), TO_MATE)

    parts = call(
        chip_kernel,
        [f32(3, 64, ROWS)] * 4,
        *own,
        mate,
        flops=3 * tile * HALF,
        scratch=[pltpu.VMEM((3, ROWS, ROWS), F32)],
    )
    chip = call(sum_kernel, f32(3, 64, ROWS), *sum_along_y(parts))
    parts = call(
        window_kernel,
        [f32(4, 64, ROWS)] * 4,
        *own,
        mate,
        near,
        *far_near,
        hidden=(chip,),
        flops=4 * tile * HALF,
        scratch=[pltpu.VMEM((4, ROWS, ROWS), F32)],
    )
    window = call(sum_kernel, f32(4, 64, ROWS), *sum_along_y(parts))
    swapped = send(window, TO_MATE)
    lower = send(swapped, EVEN_UP)
    keep, give = call(choose_kernel, [f32(4, 64, ROWS)] * 2, chip, swapped, lower)
    given = send(give, TO_MATE)

    stay, leave = call(split_kernel, [f32(4, 32, ROWS)] * 2, keep, given)
    come = lax.ppermute(leave, "aux", ACROSS_X)

    early = call(
        early_kernel, f32(1, ROWS, ROWS), near, far_mate[0], flops=CUT * tile, hidden=(leave,)
    )
    keep_last, give_last = call(
        last_kernel,
        [f32(128, ROWS)] * 2,
        near,
        far_mate[1],
        early,
        flops=(HALF - CUT) * tile,
        scratch=[pltpu.VMEM((1, ROWS, ROWS), F32)],
    )
    parts = call(combine_last_kernel, [f32(32, ROWS)] * 4, keep_last, send(give_last, TO_MATE))
    last = call(sum_kernel, f32(32, ROWS), *sum_along_y(parts))
    arrived = [lax.ppermute(last, ("blk", "aux"), to_upper_even(flip)) for flip in (1, 0)]
    out = call(finish_kernel, f32(4, 32, ROWS), stay, come, *arrived)
    return out.transpose(2, 0, 1)


def solution(mesh):
    placed = (P("aux", "blk", None),)
    return jax.shard_map(
        local, mesh=mesh, in_specs=placed, out_specs=P("blk", None, "aux"), check_vma=False
    )
```

time: 404 us -> 172 us (0.43)
  waiting for transfers between devices: 361 us -> 119 us
  starting transfers between devices: 0.01 us -> 32.1 us
  matrix products: 21.9 us -> 0 us
  Pallas kernels: 0 us -> 15.8 us
  between operations: 14.1 us -> 0.17 us
    ppermute x3 -> x22, waiting for transfers between devices: 272 us -> 119 us  [the longest x10 85.1 us: send(): return lax.ppermute(value, 'blk', pairs)]
    unnamed x2 -> x0, waiting for transfers between devices: 89.7 us -> none
    ppermute x3 -> x22, starting transfers between devices: 0.01 us -> 32.1 us  [the longest x10 16.6 us: send(): return lax.ppermute(value, 'blk', pairs)]
    dot_general x4 -> x0, matrix products: 21.9 us -> none  [contract(): lax.dot_general(own, other, (((0, 2), (0, 2)), ((), ())), preferred_eleme...]
    pallas_call x0 -> x15, Pallas kernels: none -> 15.8 us  [call(): pl.pallas_call(kernel, out_shape=out_shape, in_specs=(specs or [VMEM] * l...]
  transfers between devices with their start and end apart: 4 -> 22, of which waited for: 4 -> 15; matrix products, arithmetic and copies ran while one was open for 4% -> 0% of each run, Pallas kernels for 0% -> 8%
where the time goes in v2:
time: 172 us; the launch traced here: 171 us
  waiting for transfers between devices  119 us (69%)
  starting transfers between devices  32.1 us (19%)
  Pallas kernels  15.8 us (9%)
  local copies, waits for them, and re-layouts  3.38 us (2%)
    ppermute x10, waiting for transfers between devices, send(): return lax.ppermute(value, 'blk', pairs)  85.1 us
    ppermute x9, waiting for transfers between devices, sum_along_y(): lax.ppermute(parts[d], 'aux', along_y(d))  27.9 us
    ppermute x10, starting transfers between devices, send(): return lax.ppermute(value, 'blk', pairs)  16.6 us
    pallas_call x15, Pallas kernels, call(): pl.pallas_call(kernel, out_shape=out_shape, in_specs=(specs or [VMEM] * l...  15.8 us
    ppermute x9, starting transfers between devices, sum_along_y(): lax.ppermute(parts[d], 'aux', along_y(d))  9.52 us
    ppermute x2, waiting for transfers between devices, local(): lax.ppermute(last, ('blk', 'aux'), to_upper_even(flip))  5.98 us
  transfers between devices with their start and end apart: 22, of which 15 were waited for; matrix products, arithmetic and copies ran while one was open for 0% of the time, Pallas kernels for 8%

profile of v2, /device:TPU:16, one launch (start us, length us, event | category | flops | bytes accessed | tf_op | source)
XLA Modules:
  0.0 170.5 jit_solution(18157794707137268463)
XLA Ops:
  0.0 3.4 %copy-done = bf16[16,256,1024]{2,1,0:T(8,128)(2,1)S(1)} copy-done((bf16[16,256,1024]{2,1,0:T(8,128)(2,1)S(1)}, bf16[16,256,1024]{2,1,0:T(8,128)(2,1)}, u32[]{:S(2)}) %copy-start) | copy-done | bytes 8388632
  4.7 6.9 %collective-permute-start.4 = (bf16[8,256,1024]{2,1,0:T(8,128)(2,1)S(1)}, bf16[8,256,1024]{2,1,0:T(8,128)(2,1)S(1)}, u32[]{:S(2)}, u32[]{:S(2)}) collective-permute-start(bf16[8,256,1024]{2,1,0:T(8,128)(2,1)S(1)} %shard_map.17.refs_0_), channel_id=1, source_target_pairs={{0,248},{8,16},{16,8},{24,32},{32,24},{40,48},{48,40},{56,64},{64,... | collective-permute-start | bytes 12582920 | tf_op jit(solution)/shard_map/ppermute | solution.py:225
  11.6 4.1 %collective-permute-start.15 = (bf16[6,256,1024]{2,1,0:T(8,128)(2,1)S(1)}, bf16[6,256,1024]{2,1,0:T(8,128)(2,1)S(1)}, u32[]{:S(2)}, u32[]{:S(2)}) collective-permute-start(bf16[6,256,1024]{2,1,0:T(8,128)(2,1)S(1)} %shard_map.18.refs_0_.own0), channel_id=1, source_target_pairs={{0,240},{8,24},{16,0},{24,40},{32,16},{40,56},{48,32},{56,72},{64,... | collective-permute-start | bytes 9437192 | tf_op jit(solution)/shard_map/ppermute | solution.py:225
  15.7 5.0 %shard_map.21 = (f32[3,64,256]{2,1,0:T(8,128)S(1)}, f32[3,64,256]{2,1,0:T(8,128)S(1)}, f32[3,64,256]{2,1,0:T(8,128)S(1)}, f32[3,64,256]{2,1,0:T(8,128)S(1)}) custom-call(bf16[6,256,1024]{2,1,0:T(8,128)(2,1)S(1)} %shard_map.18.refs_0_.own0, bf16[2,256,1024]{2,1,0:T(8,128)(2,1)S(1)} %shard_map.19.refs_1_.own1, bf16[8,256,1024]{2,1,0:T(8,128)(2,1)S(1)} %collective-permute-done.mate0), custom_call_target="tpu_custom_call" | custom-call | flops 3221225472 | bytes 8388608 | tf_op jit(solution)/shard_map/pallas_call | solution.py:56
  20.7 1.4 collective-permute-start.1
  22.0 5.1 %collective-permute-done.1.b = f32[3,64,256]{2,1,0:T(8,128)S(1)} collective-permute-done((f32[3,64,256]{2,1,0:T(8,128)S(1)}, f32[3,64,256]{2,1,0:T(8,128)S(1)}, u32[]{:S(2)}, u32[]{:S(2)}) %collective-permute-start.1) | collective-permute-done | bytes 196640 | tf_op jit(solution)/shard_map/ppermute | solution.py:220
  27.1 1.6 collective-permute-start.2
  28.7 5.6 %collective-permute-done.2.c = f32[3,64,256]{2,1,0:T(8,128)S(1)} collective-permute-done((f32[3,64,256]{2,1,0:T(8,128)S(1)}, f32[3,64,256]{2,1,0:T(8,128)S(1)}, u32[]{:S(2)}, u32[]{:S(2)}) %collective-permute-start.2) | collective-permute-done | bytes 196640 | tf_op jit(solution)/shard_map/ppermute | solution.py:220
  34.8 5.2 %collective-permute-done.3.d = f32[3,64,256]{2,1,0:T(8,128)S(1)} collective-permute-done((f32[3,64,256]{2,1,0:T(8,128)S(1)}, f32[3,64,256]{2,1,0:T(8,128)S(1)}, u32[]{:S(2)}, u32[]{:S(2)}) %collective-permute-start.3) | collective-permute-done | bytes 196640 | tf_op jit(solution)/shard_map/ppermute | solution.py:220
  40.0 67.1 %collective-permute-done.6.far1 = bf16[2,256,1024]{2,1,0:T(8,128)(2,1)S(1)} collective-permute-done((bf16[2,256,1024]{2,1,0:T(8,128)(2,1)S(1)}, bf16[2,256,1024]{2,1,0:T(8,128)(2,1)S(1)}, u32[]{:S(2)}, u32[]{:S(2)}) %collective-permute-start.6) | collective-permute-done | bytes 1048608 | tf_op jit(solution)/shard_map/ppermute | solution.py:225
  107.2 6.1 %shard_map.23 = (f32[4,64,256]{2,1,0:T(8,128)S(1)}, f32[4,64,256]{2,1,0:T(8,128)S(1)}, f32[4,64,256]{2,1,0:T(8,128)S(1)}, f32[4,64,256]{2,1,0:T(8,128)S(1)}) custom-call(bf16[6,256,1024]{2,1,0:T(8,128)(2,1)S(1)} %shard_map.18.refs_0_.own0, bf16[2,256,1024]{2,1,0:T(8,128)(2,1)S(1)} %shard_map.19.refs_1_.own1, ...), custom_call_target="tpu_custom_call" | custom-call | flops 4294967296 | bytes 16777216 | tf_op jit(solution)/shard_map/pallas_call | solution.py:56
  113.3 1.4 collective-permute-start.7
  115.3 1.1 collective-permute-start.9
  116.3 3.4 %collective-permute-done.7.b = f32[4,64,256]{2,1,0:T(8,128)S(1)} collective-permute-done((f32[4,64,256]{2,1,0:T(8,128)S(1)}, f32[4,64,256]{2,1,0:T(8,128)S(1)}, u32[]{:S(2)}, u32[]{:S(2)}) %collective-permute-start.7) | collective-permute-done | bytes 262176 | tf_op jit(solution)/shard_map/ppermute | solution.py:220
  119.7 2.8 %collective-permute-done.8.c = f32[4,64,256]{2,1,0:T(8,128)S(1)} collective-permute-done((f32[4,64,256]{2,1,0:T(8,128)S(1)}, f32[4,64,256]{2,1,0:T(8,128)S(1)}, u32[]{:S(2)}, u32[]{:S(2)}) %collective-permute-start.8) | collective-permute-done | bytes 262176 | tf_op jit(solution)/shard_map/ppermute | solution.py:220
  122.5 2.1 %collective-permute-done.9.d = f32[4,64,256]{2,1,0:T(8,128)S(1)} collective-permute-done((f32[4,64,256]{2,1,0:T(8,128)S(1)}, f32[4,64,256]{2,1,0:T(8,128)S(1)}, u32[]{:S(2)}, u32[]{:S(2)}) %collective-permute-start.9) | collective-permute-done | bytes 262176 | tf_op jit(solution)/shard_map/ppermute | solution.py:220
  124.8 1.5 collective-permute-done.10.swapped
  126.3 1.9 %collective-permute-start.11 = (f32[4,64,256]{2,1,0:T(8,128)S(1)}, f32[4,64,256]{2,1,0:T(8,128)S(1)}, u32[]{:S(2)}, u32[]{:S(2)}) collective-permute-start(f32[4,64,256]{2,1,0:T(8,128)S(1)} %collective-permute-done.10.swapped), channel_id=1, source_target_pairs={{0,16},{16,32},{32,48},{48,64},{64,80},{80,96},{96,112},{112,128},... | collective-permute-start | bytes 786440 | tf_op jit(solution)/shard_map/ppermute | solution.py:225
  128.2 11.3 %collective-permute-done.11.lower = f32[4,64,256]{2,1,0:T(8,128)S(1)} collective-permute-done((f32[4,64,256]{2,1,0:T(8,128)S(1)}, f32[4,64,256]{2,1,0:T(8,128)S(1)}, u32[]{:S(2)}, u32[]{:S(2)}) %collective-permute-start.11) | collective-permute-done | bytes 262176 | tf_op jit(solution)/shard_map/ppermute | solution.py:225
  139.7 1.5 collective-permute-done.12.given
  141.3 2.1 %shard_map.27.early = f32[1,256,256]{2,1,0:T(8,128)S(1)} custom-call(bf16[8,256,1024]{2,1,0:T(8,128)(2,1)S(1)} %collective-permute-done.4.near0, bf16[6,256,1024]{2,1,0:T(8,128)(2,1)S(1)} %collective-permute-done.15.far0, f32[4,32,256]{2,1,0:T(8,128)S(1)} %get-tuple-element.34.hidden), custom_call_target="tpu_custom_call" | custom-call | flops 805306368 | bytes 7340032 | tf_op jit(solution)/shard_map/pallas_call | solution.py:56
  143.3 3.6 %collective-permute-done.14.far1 = bf16[2,256,1024]{2,1,0:T(8,128)(2,1)S(1)} collective-permute-done((bf16[2,256,1024]{2,1,0:T(8,128)(2,1)S(1)}, bf16[2,256,1024]{2,1,0:T(8,128)(2,1)S(1)}, u32[]{:S(2)}, u32[]{:S(2)}) %collective-permute-start.14) | collective-permute-done | bytes 1048608 | tf_op jit(solution)/shard_map/ppermute | solution.py:225
  146.9 0.7 shard_map.28
  147.6 3.4 %collective-permute-start.16 = (f32[128,256]{1,0:T(8,128)S(1)}, f32[128,256]{1,0:T(8,128)S(1)}, u32[]{:S(2)}, u32[]{:S(2)}) collective-permute-start(f32[128,256]{1,0:T(8,128)S(1)} %get-tuple-element.36), channel_id=1, source_target_pairs={{0,8},{8,0},{16,24},{24,16},{32,40},{40,32},{48,56},{56,48},{64,72... | collective-permute-start | bytes 393224 | tf_op jit(solution)/shard_map/ppermute | solution.py:225
  151.1 2.7 %collective-permute-start.13 = (f32[4,32,256]{2,1,0:T(8,128)S(1)}, f32[4,32,256]{2,1,0:T(8,128)S(1)}, u32[]{:S(2)}, u32[]{:S(2)}) collective-permute-start(f32[4,32,256]{2,1,0:T(8,128)S(1)} %get-tuple-element.34.hidden), channel_id=1, source_target_pairs={{0,1},{1,0},{2,3},{3,2},{4,5},{5,4},{6,7},{7,6},{8,9},{9,8},{10,11... | collective-permute-start | bytes 393224 | tf_op jit(solution)/shard_map/ppermute | solution.py:265
  153.8 1.4 collective-permute-start.17
  155.8 1.1 collective-permute-start.19
  156.9 0.9 collective-permute-done.17.b
  157.8 2.8 %collective-permute-done.18.c = f32[32,256]{1,0:T(8,128)S(1)} collective-permute-done((f32[32,256]{1,0:T(8,128)S(1)}, f32[32,256]{1,0:T(8,128)S(1)}, u32[]{:S(2)}, u32[]{:S(2)}) %collective-permute-start.18) | collective-permute-done | bytes 32800 | tf_op jit(solution)/shard_map/ppermute | solution.py:220
  160.6 1.3 collective-permute-start.20
  161.9 1.9 %collective-permute-start.21 = (f32[32,256]{1,0:T(8,128)S(1)}, f32[32,256]{1,0:T(8,128)S(1)}, u32[]{:S(2)}, u32[]{:S(2)}) collective-permute-start(f32[32,256]{1,0:T(8,128)S(1)} %shard_map.30), channel_id=1, source_target_pairs={{0,16},{2,18},{4,20},{6,22},{9,17},{11,19},{13,21},{15,23},{16,32}... | collective-permute-start | bytes 98312 | tf_op jit(solution)/shard_map/ppermute | solution.py:281
  163.9 5.9 %collective-permute-done.20.a = f32[32,256]{1,0:T(8,128)S(1)} collective-permute-done((f32[32,256]{1,0:T(8,128)S(1)}, f32[32,256]{1,0:T(8,128)S(1)}, u32[]{:S(2)}, u32[]{:S(2)}) %collective-permute-start.20) | collective-permute-done | bytes 32800 | tf_op jit(solution)/shard_map/ppermute | solution.py:281
  (29 shorter events, 4.1 us)
Async XLA Ops:
  0.0 3.4 %copy-start = (bf16[16,256,1024]{2,1,0:T(8,128)(2,1)S(1)}, bf16[16,256,1024]{2,1,0:T(8,128)(2,1)}, u32[]{:S(2)}) copy-start(bf16[16,256,1024]{2,1,0:T(8,128)(2,1)} %factors.7) | copy-start | bytes 25165828
  4.6 11.1 %collective-permute-start = (bf16[8,256,1024]{2,1,0:T(8,128)(2,1)S(1)}, bf16[8,256,1024]{2,1,0:T(8,128)(2,1)S(1)}, u32[]{:S(2)}, u32[]{:S(2)}) collective-permute-start(bf16[8,256,1024]{2,1,0:T(8,128)(2,1)S(1)} %shard_map.20), channel_id=1, source_target_pairs={{0,8},{8,0},{16,24},{24,16},{32,40},{40,32},{48,56},{56,48},{64,72... | collective-permute-start | bytes 12582920 | tf_op jit(solution)/shard_map/ppermute | solution.py:225
  4.7 102.5 %collective-permute-start.4 = (bf16[8,256,1024]{2,1,0:T(8,128)(2,1)S(1)}, bf16[8,256,1024]{2,1,0:T(8,128)(2,1)S(1)}, u32[]{:S(2)}, u32[]{:S(2)}) collective-permute-start(bf16[8,256,1024]{2,1,0:T(8,128)(2,1)S(1)} %shard_map.17.refs_0_), channel_id=1, source_target_pairs={{0,248},{8,16},{16,8},{24,32},{32,24},{40,48},{48,40},{56,64},{64,... | collective-permute-start | bytes 12582920 | tf_op jit(solution)/shard_map/ppermute | solution.py:225
  11.6 95.6 %collective-permute-start.5 = (bf16[6,256,1024]{2,1,0:T(8,128)(2,1)S(1)}, bf16[6,256,1024]{2,1,0:T(8,128)(2,1)S(1)}, u32[]{:S(2)}, u32[]{:S(2)}) collective-permute-start(bf16[6,256,1024]{2,1,0:T(8,128)(2,1)S(1)} %shard_map.18.refs_0_.own0), channel_id=1, source_target_pairs={{0,16},{8,248},{16,32},{24,8},{32,48},{40,24},{48,64},{56,40},{64,... | collective-permute-start | bytes 9437192 | tf_op jit(solution)/shard_map/ppermute | solution.py:225
  11.6 129.7 %collective-permute-start.15 = (bf16[6,256,1024]{2,1,0:T(8,128)(2,1)S(1)}, bf16[6,256,1024]{2,1,0:T(8,128)(2,1)S(1)}, u32[]{:S(2)}, u32[]{:S(2)}) collective-permute-start(bf16[6,256,1024]{2,1,0:T(8,128)(2,1)S(1)} %shard_map.18.refs_0_.own0), channel_id=1, source_target_pairs={{0,240},{8,24},{16,0},{24,40},{32,16},{40,56},{48,32},{56,72},{64,... | collective-permute-start | bytes 9437192 | tf_op jit(solution)/shard_map/ppermute | solution.py:225
  15.7 91.5 %collective-permute-start.6 = (bf16[2,256,1024]{2,1,0:T(8,128)(2,1)S(1)}, bf16[2,256,1024]{2,1,0:T(8,128)(2,1)S(1)}, u32[]{:S(2)}, u32[]{:S(2)}) collective-permute-start(bf16[2,256,1024]{2,1,0:T(8,128)(2,1)S(1)} %shard_map.19.refs_1_.own1), channel_id=1, source_target_pairs={{0,16},{8,248},{16,32},{24,8},{32,48},{40,24},{48,64},{56,40},{64,... | collective-permute-start | bytes 3145736 | tf_op jit(solution)/shard_map/ppermute | solution.py:225
  20.7 6.5 %collective-permute-start.1 = (f32[3,64,256]{2,1,0:T(8,128)S(1)}, f32[3,64,256]{2,1,0:T(8,128)S(1)}, u32[]{:S(2)}, u32[]{:S(2)}) collective-permute-start(f32[3,64,256]{2,1,0:T(8,128)S(1)} %get-tuple-element.24), channel_id=1, source_target_pairs={{0,2},{1,3},{2,4},{3,5},{4,6},{5,7},{6,0},{7,1},{8,10},{9,11},{10,... | collective-permute-start | bytes 589832 | tf_op jit(solution)/shard_map/ppermute | solution.py:220
  27.1 7.2 %collective-permute-start.2 = (f32[3,64,256]{2,1,0:T(8,128)S(1)}, f32[3,64,256]{2,1,0:T(8,128)S(1)}, u32[]{:S(2)}, u32[]{:S(2)}) collective-permute-start(f32[3,64,256]{2,1,0:T(8,128)S(1)} %get-tuple-element.25), channel_id=1, source_target_pairs={{0,4},{1,5},{2,6},{3,7},{4,0},{5,1},{6,2},{7,3},{8,12},{9,13},{10,... | collective-permute-start | bytes 589832 | tf_op jit(solution)/shard_map/ppermute | solution.py:220
  34.3 5.7 %collective-permute-start.3 = (f32[3,64,256]{2,1,0:T(8,128)S(1)}, f32[3,64,256]{2,1,0:T(8,128)S(1)}, u32[]{:S(2)}, u32[]{:S(2)}) collective-permute-start(f32[3,64,256]{2,1,0:T(8,128)S(1)} %get-tuple-element.26), channel_id=1, source_target_pairs={{0,6},{1,7},{2,0},{3,1},{4,2},{5,3},{6,4},{7,5},{8,14},{9,15},{10,... | collective-permute-start | bytes 589832 | tf_op jit(solution)/shard_map/ppermute | solution.py:220
  113.3 6.5 %collective-permute-start.7 = (f32[4,64,256]{2,1,0:T(8,128)S(1)}, f32[4,64,256]{2,1,0:T(8,128)S(1)}, u32[]{:S(2)}, u32[]{:S(2)}) collective-permute-start(f32[4,64,256]{2,1,0:T(8,128)S(1)} %get-tuple-element.28), channel_id=1, source_target_pairs={{0,2},{1,3},{2,4},{3,5},{4,6},{5,7},{6,0},{7,1},{8,10},{9,11},{10,... | collective-permute-start | bytes 786440 | tf_op jit(solution)/shard_map/ppermute | solution.py:220
  114.6 7.9 %collective-permute-start.8 = (f32[4,64,256]{2,1,0:T(8,128)S(1)}, f32[4,64,256]{2,1,0:T(8,128)S(1)}, u32[]{:S(2)}, u32[]{:S(2)}) collective-permute-start(f32[4,64,256]{2,1,0:T(8,128)S(1)} %get-tuple-element.29), channel_id=1, source_target_pairs={{0,4},{1,5},{2,6},{3,7},{4,0},{5,1},{6,2},{7,3},{8,12},{9,13},{10,... | collective-permute-start | bytes 786440 | tf_op jit(solution)/shard_map/ppermute | solution.py:220
  115.3 9.4 %collective-permute-start.9 = (f32[4,64,256]{2,1,0:T(8,128)S(1)}, f32[4,64,256]{2,1,0:T(8,128)S(1)}, u32[]{:S(2)}, u32[]{:S(2)}) collective-permute-start(f32[4,64,256]{2,1,0:T(8,128)S(1)} %get-tuple-element.30), channel_id=1, source_target_pairs={{0,6},{1,7},{2,0},{3,1},{4,2},{5,3},{6,4},{7,5},{8,14},{9,15},{10,... | collective-permute-start | bytes 786440 | tf_op jit(solution)/shard_map/ppermute | solution.py:220
  116.3 30.6 %collective-permute-start.14 = (bf16[2,256,1024]{2,1,0:T(8,128)(2,1)S(1)}, bf16[2,256,1024]{2,1,0:T(8,128)(2,1)S(1)}, u32[]{:S(2)}, u32[]{:S(2)}) collective-permute-start(bf16[2,256,1024]{2,1,0:T(8,128)(2,1)S(1)} %shard_map.19.refs_1_.own1), channel_id=1, source_target_pairs={{0,240},{8,24},{16,0},{24,40},{32,16},{40,56},{48,32},{56,72},{64,... | collective-permute-start | bytes 3145736 | tf_op jit(solution)/shard_map/ppermute | solution.py:225
  124.7 1.6 collective-permute-start.10
  126.3 13.2 %collective-permute-start.11 = (f32[4,64,256]{2,1,0:T(8,128)S(1)}, f32[4,64,256]{2,1,0:T(8,128)S(1)}, u32[]{:S(2)}, u32[]{:S(2)}) collective-permute-start(f32[4,64,256]{2,1,0:T(8,128)S(1)} %collective-permute-done.10.swapped), channel_id=1, source_target_pairs={{0,16},{16,32},{32,48},{48,64},{64,80},{80,96},{96,112},{112,128},... | collective-permute-start | bytes 786440 | tf_op jit(solution)/shard_map/ppermute | solution.py:225
  139.6 1.6 collective-permute-start.12
  147.6 6.1 %collective-permute-start.16 = (f32[128,256]{1,0:T(8,128)S(1)}, f32[128,256]{1,0:T(8,128)S(1)}, u32[]{:S(2)}, u32[]{:S(2)}) collective-permute-start(f32[128,256]{1,0:T(8,128)S(1)} %get-tuple-element.36), channel_id=1, source_target_pairs={{0,8},{8,0},{16,24},{24,16},{32,40},{40,32},{48,56},{56,48},{64,72... | collective-permute-start | bytes 393224 | tf_op jit(solution)/shard_map/ppermute | solution.py:225
  151.1 12.8 %collective-permute-start.13 = (f32[4,32,256]{2,1,0:T(8,128)S(1)}, f32[4,32,256]{2,1,0:T(8,128)S(1)}, u32[]{:S(2)}, u32[]{:S(2)}) collective-permute-start(f32[4,32,256]{2,1,0:T(8,128)S(1)} %get-tuple-element.34.hidden), channel_id=1, source_target_pairs={{0,1},{1,0},{2,3},{3,2},{4,5},{5,4},{6,7},{7,6},{8,9},{9,8},{10,11... | collective-permute-start | bytes 393224 | tf_op jit(solution)/shard_map/ppermute | solution.py:265
  153.8 4.0 %collective-permute-start.17 = (f32[32,256]{1,0:T(8,128)S(1)}, f32[32,256]{1,0:T(8,128)S(1)}, u32[]{:S(2)}, u32[]{:S(2)}) collective-permute-start(f32[32,256]{1,0:T(8,128)S(1)} %get-tuple-element.38), channel_id=1, source_target_pairs={{0,2},{1,3},{2,4},{3,5},{4,6},{5,7},{6,0},{7,1},{8,10},{9,11},{10,... | collective-permute-start | bytes 98312 | tf_op jit(solution)/shard_map/ppermute | solution.py:220
  155.2 5.4 %collective-permute-start.18 = (f32[32,256]{1,0:T(8,128)S(1)}, f32[32,256]{1,0:T(8,128)S(1)}, u32[]{:S(2)}, u32[]{:S(2)}) collective-permute-start(f32[32,256]{1,0:T(8,128)S(1)} %get-tuple-element.39), channel_id=1, source_target_pairs={{0,4},{1,5},{2,6},{3,7},{4,0},{5,1},{6,2},{7,3},{8,12},{9,13},{10,... | collective-permute-start | bytes 98312 | tf_op jit(solution)/shard_map/ppermute | solution.py:220
  155.8 4.8 %collective-permute-start.19 = (f32[32,256]{1,0:T(8,128)S(1)}, f32[32,256]{1,0:T(8,128)S(1)}, u32[]{:S(2)}, u32[]{:S(2)}) collective-permute-start(f32[32,256]{1,0:T(8,128)S(1)} %get-tuple-element.40), channel_id=1, source_target_pairs={{0,6},{1,7},{2,0},{3,1},{4,2},{5,3},{6,4},{7,5},{8,14},{9,15},{10,... | collective-permute-start | bytes 98312 | tf_op jit(solution)/shard_map/ppermute | solution.py:220
  160.6 9.2 %collective-permute-start.20 = (f32[32,256]{1,0:T(8,128)S(1)}, f32[32,256]{1,0:T(8,128)S(1)}, u32[]{:S(2)}, u32[]{:S(2)}) collective-permute-start(f32[32,256]{1,0:T(8,128)S(1)} %shard_map.30), channel_id=1, source_target_pairs={{1,16},{3,18},{5,20},{7,22},{8,17},{10,19},{12,21},{14,23},{17,32}... | collective-permute-start | bytes 98312 | tf_op jit(solution)/shard_map/ppermute | solution.py:281
  161.9 7.9 %collective-permute-start.21 = (f32[32,256]{1,0:T(8,128)S(1)}, f32[32,256]{1,0:T(8,128)S(1)}, u32[]{:S(2)}, u32[]{:S(2)}) collective-permute-start(f32[32,256]{1,0:T(8,128)S(1)} %shard_map.30), channel_id=1, source_target_pairs={{0,16},{2,18},{4,20},{6,22},{9,17},{11,19},{13,21},{15,23},{16,32}... | collective-permute-start | bytes 98312 | tf_op jit(solution)/shard_map/ppermute | solution.py:281

commit v3 on v2

--- a/solution.py
+++ b/solution.py
@@ -9,7 +9,7 @@
 
 COUNT = 32
 HALF = 8
-CUT = 6
+CUT = 7
 ROWS = 256
 DEPTH = 1024
 F32 = jnp.float32
@@ -22,7 +22,7 @@
 TO_NEAR = [(b, (b - 1 if b % 2 == 0 else b + 1) % COUNT) for b in range(COUNT)]
 TO_FAR_NEAR = [(b, (b + 2 if b % 2 == 0 else b - 2) % COUNT) for b in range(COUNT)]
 TO_FAR_MATE = [(b, (b - 2 if b % 2 == 0 else b + 2) % COUNT) for b in range(COUNT)]
-EVEN_UP = [(b, (b + 2) % COUNT) for b in range(0, COUNT, 2)]
+EVEN_UP = [(b, (b + 2) % COUNT if b % 2 == 0 else b) for b in range(COUNT)]
 
 
 def along_y(shift):
@@ -36,9 +36,11 @@
     pairs = []
     for b in range(COUNT):
         core = b % 2
-        for y in range(4):
-            source, target = 2 * y + (core ^ flip), 2 * y + core
-            pairs.append((b * 8 + source, (b - core + 2) % COUNT * 8 + target))
+        for a in range(8):
+            if a % 2 == core ^ flip:
+                pairs.append((b * 8 + a, (b - core + 2) % COUNT * 8 + a // 2 * 2 + core))
+            else:
+                pairs.append((b * 8 + a, (b | 1) * 8 + a))
     return pairs
 
 
@@ -69,7 +71,7 @@
     odd = parity()
     base = (1 - odd if other else odd) * HALF + first
     copies = [
-        pltpu.make_async_copy(factors.at[base + i], out.at[i], sems.at[i]) for i in range(count)
+        pltpu.make_async_copy(factors.at[base + q], out.at[q], sems.at[q]) for q in range(count)
     ]
     for copy in copies:
         copy.start()
@@ -77,7 +79,7 @@
         copy.wait()
 
 
-def take(factors, other, first, count, after=(), limit=16):
+def take(factors, other, first, count, after=()):
     return call(
         functools.partial(take_kernel, other, first, count),
         jax.ShapeDtypeStruct((count, ROWS, DEPTH), BF16),
@@ -85,7 +87,7 @@
         scratch=[pltpu.SemaphoreType.DMA((count,))],
         specs=[HBM],
         hidden=after,
-        limit=limit,
+        limit=44,
     )
 
 
@@ -184,7 +186,7 @@
         out[...] = keep[:, rows] + given[:, rows]
 
 
-def early_kernel(near0, far0, hidden, total):
+def early_kernel(near0, far0, total):
     near, far = [(near0, 0)], [(far0, 0)]
     by_parity(
         lambda: accumulate(total, [(near, far)], 0, CUT),
@@ -192,7 +194,7 @@
     )
 
 
-def last_kernel(near0, far1, early, keep, give, total):
+def last_kernel(near0, far1, early, hidden, keep, give, total):
     near, far = [(near0, 0)], [(far1, CUT)]
     by_parity(
         lambda: accumulate(total, [(near, far)], CUT, HALF),
@@ -213,7 +215,11 @@
 
 def finish_kernel(stay, come, a, b, out):
     out[0:3] = stay[0:3] + come[0:3]
-    out[3] = (stay[3] + come[3]) + (a[...] + b[...])
+    out[3] = stay[3] + come[3]
+
+    @pl.when(parity() == 0)
+    def _():
+        out[3] += a[...] + b[...]
 
 
 def sum_along_y(parts):
@@ -227,13 +233,11 @@
     tile = 2 * ROWS * ROWS * DEPTH
     rest = take(factors, True, 0, HALF)
     near = send(rest, TO_NEAR)
-    own = [
-        take(factors, False, 0, CUT, (rest,)),
-        take(factors, False, CUT, HALF - CUT, (rest,)),
-    ]
+    own = [take(factors, False, CUT, HALF - CUT, (rest,))]
+    own.insert(0, take(factors, False, 0, CUT, (own[0],)))
     far_near = [send(part, TO_FAR_NEAR) for part in own]
     far_mate = [send(part, TO_FAR_MATE) for part in own]
-    mate = send(take(factors, True, 0, HALF, own), TO_MATE)
+    mate = send(rest, TO_MATE)
 
     parts = call(
         chip_kernel,
@@ -265,7 +269,7 @@
     come = lax.ppermute(leave, "aux", ACROSS_X)
 
     early = call(
-        early_kernel, f32(1, ROWS, ROWS), near, far_mate[0], flops=CUT * tile, hidden=(leave,)
+        early_kernel, f32(1, ROWS, ROWS), near, far_mate[0], flops=CUT * tile
     )
     keep_last, give_last = call(
         last_kernel,
@@ -273,6 +277,7 @@
         near,
         far_mate[1],
         early,
+        hidden=(leave,),
         flops=(HALF - CUT) * tile,
         scratch=[pltpu.VMEM((1, ROWS, ROWS), F32)],
     )

time: 172 us -> 170 us (0.988)
  waiting for transfers between devices: 119 us -> 112 us
  Pallas kernels: 15.8 us -> 20 us
  starting transfers between devices: 32.1 us -> 35.9 us
  local copies, waits for them, and re-layouts: 3.38 us -> 0 us
    ppermute x10, waiting for transfers between devices: 85.1 us -> 75.2 us  [send(): return lax.ppermute(value, 'blk', pairs)]
    pallas_call x15 -> x14, Pallas kernels: 15.8 us -> 20 us  [call(): pl.pallas_call(kernel, out_shape=out_shape, in_specs=(specs or [VMEM] * l...]
    ppermute x10, starting transfers between devices: 16.6 us -> 20.5 us  [send(): return lax.ppermute(value, 'blk', pairs)]
    unnamed x2 -> x0, local copies, waits for them, and re-layouts: 3.38 us -> none
    ppermute x9, waiting for transfers between devices: 27.9 us -> 31.2 us  [sum_along_y(): lax.ppermute(parts[d], 'aux', along_y(d))]
  transfers between devices with their start and end apart: 22 -> 22, of which waited for: 15 -> 14; matrix products, arithmetic and copies ran while one was open for 0% -> 0% of each run, Pallas kernels for 8% -> 10%
where the time goes in v3:
time: 170 us; the launch traced here: 168 us
  waiting for transfers between devices  112 us (66%)
  starting transfers between devices  35.9 us (21%)
  Pallas kernels  20 us (12%)
    ppermute x10, waiting for transfers between devices, send(): return lax.ppermute(value, 'blk', pairs)  75.2 us
    ppermute x9, waiting for transfers between devices, sum_along_y(): lax.ppermute(parts[d], 'aux', along_y(d))  31.2 us
    ppermute x10, starting transfers between devices, send(): return lax.ppermute(value, 'blk', pairs)  20.5 us
    pallas_call x14, Pallas kernels, call(): pl.pallas_call(kernel, out_shape=out_shape, in_specs=(specs or [VMEM] * l...  20 us
    ppermute x9, starting transfers between devices, sum_along_y(): lax.ppermute(parts[d], 'aux', along_y(d))  8.75 us
    ppermute x2, waiting for transfers between devices, local(): lax.ppermute(last, ('blk', 'aux'), to_upper_even(flip))  5.98 us
    ppermute x2, starting transfers between devices, local(): lax.ppermute(last, ('blk', 'aux'), to_upper_even(flip))  3.84 us
  transfers between devices with their start and end apart: 22, of which 14 were waited for; matrix products, arithmetic and copies ran while one was open for 0% of the time, Pallas kernels for 10%

profile of v3, /device:TPU:16, one launch (start us, length us, event | category | flops | bytes accessed | tf_op | source)
XLA Modules:
  0.0 168.4 jit_solution(10866508248339916464)
XLA Ops:
  0.0 2.2 %shard_map.17.refs_0_ = bf16[8,256,1024]{2,1,0:T(8,128)(2,1)S(1)} custom-call(bf16[16,256,1024]{2,1,0:T(8,128)(2,1)} %factors.5), custom_call_target="tpu_custom_call" | custom-call | bytes 8388608 | tf_op jit(solution)/shard_map/pallas_call | solution.py:58
  2.3 6.9 %collective-permute-start.4 = (bf16[8,256,1024]{2,1,0:T(8,128)(2,1)S(1)}, bf16[8,256,1024]{2,1,0:T(8,128)(2,1)S(1)}, u32[]{:S(2)}, u32[]{:S(2)}) collective-permute-start(bf16[8,256,1024]{2,1,0:T(8,128)(2,1)S(1)} %shard_map.17.refs_0_), channel_id=1, source_target_pairs={{0,248},{8,16},{16,8},{24,32},{32,24},{40,48},{48,40},{56,64},{64,... | collective-permute-start | bytes 12582920 | tf_op jit(solution)/shard_map/ppermute | solution.py:231
  9.2 1.0 shard_map.18.refs_0_.own1
  10.3 2.1 %shard_map.19.own0 = bf16[7,256,1024]{2,1,0:T(8,128)(2,1)S(1)} custom-call(bf16[16,256,1024]{2,1,0:T(8,128)(2,1)} %factors.5, bf16[1,256,1024]{2,1,0:T(8,128)(2,1)S(1)} %shard_map.18.refs_0_.own1), custom_call_target="tpu_custom_call" | custom-call | bytes 8388608 | tf_op jit(solution)/shard_map/pallas_call | solution.py:58
  12.4 4.1 %collective-permute-start.15 = (bf16[7,256,1024]{2,1,0:T(8,128)(2,1)S(1)}, bf16[7,256,1024]{2,1,0:T(8,128)(2,1)S(1)}, u32[]{:S(2)}, u32[]{:S(2)}) collective-permute-start(bf16[7,256,1024]{2,1,0:T(8,128)(2,1)S(1)} %shard_map.19.own0), channel_id=1, source_target_pairs={{0,240},{8,24},{16,0},{24,40},{32,16},{40,56},{48,32},{56,72},{64,... | collective-permute-start | bytes 11010056 | tf_op jit(solution)/shard_map/ppermute | solution.py:231
  16.6 5.0 %shard_map.20 = (f32[3,64,256]{2,1,0:T(8,128)S(1)}, f32[3,64,256]{2,1,0:T(8,128)S(1)}, f32[3,64,256]{2,1,0:T(8,128)S(1)}, f32[3,64,256]{2,1,0:T(8,128)S(1)}) custom-call(bf16[7,256,1024]{2,1,0:T(8,128)(2,1)S(1)} %shard_map.19.own0, bf16[1,256,1024]{2,1,0:T(8,128)(2,1)S(1)} %shard_map.18.refs_0_.own1, bf16[8,256,1024]{2,1,0:T(8,128)(2,1)S(1)} %collective-permute-done.mate0), custom_call_target="tpu_custom_call" | custom-call | flops 3221225472 | bytes 8388608 | tf_op jit(solution)/shard_map/pallas_call | solution.py:58
  21.5 1.4 collective-permute-start.1
  22.9 6.5 %collective-permute-done.1.b = f32[3,64,256]{2,1,0:T(8,128)S(1)} collective-permute-done((f32[3,64,256]{2,1,0:T(8,128)S(1)}, f32[3,64,256]{2,1,0:T(8,128)S(1)}, u32[]{:S(2)}, u32[]{:S(2)}) %collective-permute-start.1) | collective-permute-done | bytes 196640 | tf_op jit(solution)/shard_map/ppermute | solution.py:226
  29.5 7.0 %collective-permute-done.2.c = f32[3,64,256]{2,1,0:T(8,128)S(1)} collective-permute-done((f32[3,64,256]{2,1,0:T(8,128)S(1)}, f32[3,64,256]{2,1,0:T(8,128)S(1)}, u32[]{:S(2)}, u32[]{:S(2)}) %collective-permute-start.2) | collective-permute-done | bytes 196640 | tf_op jit(solution)/shard_map/ppermute | solution.py:226
  36.5 1.1 collective-permute-start.3
  37.7 5.6 %collective-permute-done.3.d = f32[3,64,256]{2,1,0:T(8,128)S(1)} collective-permute-done((f32[3,64,256]{2,1,0:T(8,128)S(1)}, f32[3,64,256]{2,1,0:T(8,128)S(1)}, u32[]{:S(2)}, u32[]{:S(2)}) %collective-permute-start.3) | collective-permute-done | bytes 196640 | tf_op jit(solution)/shard_map/ppermute | solution.py:226
  43.4 64.7 %collective-permute-done.6.far1 = bf16[1,256,1024]{2,1,0:T(8,128)(2,1)S(1)} collective-permute-done((bf16[1,256,1024]{2,1,0:T(8,128)(2,1)S(1)}, bf16[1,256,1024]{2,1,0:T(8,128)(2,1)S(1)}, u32[]{:S(2)}, u32[]{:S(2)}) %collective-permute-start.6) | collective-permute-done | bytes 524320 | tf_op jit(solution)/shard_map/ppermute | solution.py:231
  108.0 6.1 %shard_map.22 = (f32[4,64,256]{2,1,0:T(8,128)S(1)}, f32[4,64,256]{2,1,0:T(8,128)S(1)}, f32[4,64,256]{2,1,0:T(8,128)S(1)}, f32[4,64,256]{2,1,0:T(8,128)S(1)}) custom-call(bf16[7,256,1024]{2,1,0:T(8,128)(2,1)S(1)} %shard_map.19.own0, bf16[1,256,1024]{2,1,0:T(8,128)(2,1)S(1)} %shard_map.18.refs_0_.own1, bf16[8,256,1024]{2,1,0:T(8,128)(2,1)S(1)} %collective-permute-done.mate0, ...), custom_call_target="tpu_custom_call" | custom-call | flops 4294967296 | bytes 16777216 | tf_op jit(solution)/shard_map/pallas_call | solution.py:58
  114.1 1.4 collective-permute-start.7
  116.1 1.1 collective-permute-start.9
  117.2 3.4 %collective-permute-done.7.b = f32[4,64,256]{2,1,0:T(8,128)S(1)} collective-permute-done((f32[4,64,256]{2,1,0:T(8,128)S(1)}, f32[4,64,256]{2,1,0:T(8,128)S(1)}, u32[]{:S(2)}, u32[]{:S(2)}) %collective-permute-start.7) | collective-permute-done | bytes 262176 | tf_op jit(solution)/shard_map/ppermute | solution.py:226
  120.6 2.8 %collective-permute-done.8.c = f32[4,64,256]{2,1,0:T(8,128)S(1)} collective-permute-done((f32[4,64,256]{2,1,0:T(8,128)S(1)}, f32[4,64,256]{2,1,0:T(8,128)S(1)}, u32[]{:S(2)}, u32[]{:S(2)}) %collective-permute-start.8) | collective-permute-done | bytes 262176 | tf_op jit(solution)/shard_map/ppermute | solution.py:226
  123.4 2.1 %collective-permute-done.9.d = f32[4,64,256]{2,1,0:T(8,128)S(1)} collective-permute-done((f32[4,64,256]{2,1,0:T(8,128)S(1)}, f32[4,64,256]{2,1,0:T(8,128)S(1)}, u32[]{:S(2)}, u32[]{:S(2)}) %collective-permute-start.9) | collective-permute-done | bytes 262176 | tf_op jit(solution)/shard_map/ppermute | solution.py:226
  125.8 1.5 collective-permute-done.10.swapped
  127.3 1.9 %collective-permute-start.11 = (f32[4,64,256]{2,1,0:T(8,128)S(1)}, f32[4,64,256]{2,1,0:T(8,128)S(1)}, u32[]{:S(2)}, u32[]{:S(2)}) collective-permute-start(f32[4,64,256]{2,1,0:T(8,128)S(1)} %collective-permute-done.10.swapped), channel_id=1, source_target_pairs={{0,16},{8,8},{16,32},{24,24},{32,48},{40,40},{48,64},{56,56},{64,8... | collective-permute-start | bytes 786440 | tf_op jit(solution)/shard_map/ppermute | solution.py:231
  129.3 4.2 %collective-permute-start.14 = (bf16[1,256,1024]{2,1,0:T(8,128)(2,1)S(1)}, bf16[1,256,1024]{2,1,0:T(8,128)(2,1)S(1)}, u32[]{:S(2)}, u32[]{:S(2)}) collective-permute-start(bf16[1,256,1024]{2,1,0:T(8,128)(2,1)S(1)} %shard_map.18.refs_0_.own1), channel_id=1, source_target_pairs={{0,240},{8,24},{16,0},{24,40},{32,16},{40,56},{48,32},{56,72},{64,... | collective-permute-start | bytes 1572872 | tf_op jit(solution)/shard_map/ppermute | solution.py:231
  133.5 7.1 %collective-permute-done.11.lower = f32[4,64,256]{2,1,0:T(8,128)S(1)} collective-permute-done((f32[4,64,256]{2,1,0:T(8,128)S(1)}, f32[4,64,256]{2,1,0:T(8,128)S(1)}, u32[]{:S(2)}, u32[]{:S(2)}) %collective-permute-start.11) | collective-permute-done | bytes 262176 | tf_op jit(solution)/shard_map/ppermute | solution.py:231
  140.7 2.4 %shard_map.26.early = f32[1,256,256]{2,1,0:T(8,128)S(1)} custom-call(bf16[8,256,1024]{2,1,0:T(8,128)(2,1)S(1)} %collective-permute-done.4.near0, bf16[7,256,1024]{2,1,0:T(8,128)(2,1)S(1)} %collective-permute-done.15.far0), custom_call_target="tpu_custom_call" | custom-call | flops 939524096 | bytes 7864320 | tf_op jit(solution)/shard_map/pallas_call | solution.py:58
  143.2 1.9 %collective-permute-done.14.far1 = bf16[1,256,1024]{2,1,0:T(8,128)(2,1)S(1)} collective-permute-done((bf16[1,256,1024]{2,1,0:T(8,128)(2,1)S(1)}, bf16[1,256,1024]{2,1,0:T(8,128)(2,1)S(1)}, u32[]{:S(2)}, u32[]{:S(2)}) %collective-permute-start.14) | collective-permute-done | bytes 524320 | tf_op jit(solution)/shard_map/ppermute | solution.py:231
  145.5 2.9 %collective-permute-start.16 = (f32[128,256]{1,0:T(8,128)S(1)}, f32[128,256]{1,0:T(8,128)S(1)}, u32[]{:S(2)}, u32[]{:S(2)}) collective-permute-start(f32[128,256]{1,0:T(8,128)S(1)} %get-tuple-element.36), channel_id=1, source_target_pairs={{0,8},{8,0},{16,24},{24,16},{32,40},{40,32},{48,56},{56,48},{64,72... | collective-permute-start | bytes 393224 | tf_op jit(solution)/shard_map/ppermute | solution.py:231
  148.4 2.7 %collective-permute-start.13 = (f32[4,32,256]{2,1,0:T(8,128)S(1)}, f32[4,32,256]{2,1,0:T(8,128)S(1)}, u32[]{:S(2)}, u32[]{:S(2)}) collective-permute-start(f32[4,32,256]{2,1,0:T(8,128)S(1)} %get-tuple-element.34.hidden), channel_id=1, source_target_pairs={{0,1},{1,0},{2,3},{3,2},{4,5},{5,4},{6,7},{7,6},{8,9},{9,8},{10,11... | collective-permute-start | bytes 393224 | tf_op jit(solution)/shard_map/ppermute | solution.py:269
  151.1 1.4 collective-permute-start.17
  153.1 1.1 collective-permute-start.19
  155.1 2.8 %collective-permute-done.18.c = f32[32,256]{1,0:T(8,128)S(1)} collective-permute-done((f32[32,256]{1,0:T(8,128)S(1)}, f32[32,256]{1,0:T(8,128)S(1)}, u32[]{:S(2)}, u32[]{:S(2)}) %collective-permute-start.18) | collective-permute-done | bytes 32800 | tf_op jit(solution)/shard_map/ppermute | solution.py:226
  157.9 1.9 %collective-permute-start.20 = (f32[32,256]{1,0:T(8,128)S(1)}, f32[32,256]{1,0:T(8,128)S(1)}, u32[]{:S(2)}, u32[]{:S(2)}) collective-permute-start(f32[32,256]{1,0:T(8,128)S(1)} %shard_map.29), channel_id=1, source_target_pairs={{0,8},{1,16},{2,10},{3,18},{4,12},{5,20},{6,14},{7,22},{8,17},{9,9... | collective-permute-start | bytes 98312 | tf_op jit(solution)/shard_map/ppermute | solution.py:286
  159.8 1.9 %collective-permute-start.21 = (f32[32,256]{1,0:T(8,128)S(1)}, f32[32,256]{1,0:T(8,128)S(1)}, u32[]{:S(2)}, u32[]{:S(2)}) collective-permute-start(f32[32,256]{1,0:T(8,128)S(1)} %shard_map.29), channel_id=1, source_target_pairs={{0,16},{1,9},{2,18},{3,11},{4,20},{5,13},{6,22},{7,15},{8,8},{9,17... | collective-permute-start | bytes 98312 | tf_op jit(solution)/shard_map/ppermute | solution.py:286
  161.8 5.3 %collective-permute-done.20.a = f32[32,256]{1,0:T(8,128)S(1)} collective-permute-done((f32[32,256]{1,0:T(8,128)S(1)}, f32[32,256]{1,0:T(8,128)S(1)}, u32[]{:S(2)}, u32[]{:S(2)}) %collective-permute-start.20) | collective-permute-done | bytes 32800 | tf_op jit(solution)/shard_map/ppermute | solution.py:286
  (26 shorter events, 4.9 us)
Async XLA Ops:
  2.2 14.3 %collective-permute-start = (bf16[8,256,1024]{2,1,0:T(8,128)(2,1)S(1)}, bf16[8,256,1024]{2,1,0:T(8,128)(2,1)S(1)}, u32[]{:S(2)}, u32[]{:S(2)}) collective-permute-start(bf16[8,256,1024]{2,1,0:T(8,128)(2,1)S(1)} %shard_map.17.refs_0_), channel_id=1, source_target_pairs={{0,8},{8,0},{16,24},{24,16},{32,40},{40,32},{48,56},{56,48},{64,72... | collective-permute-start | bytes 12582920 | tf_op jit(solution)/shard_map/ppermute | solution.py:231
  2.3 105.7 %collective-permute-start.4 = (bf16[8,256,1024]{2,1,0:T(8,128)(2,1)S(1)}, bf16[8,256,1024]{2,1,0:T(8,128)(2,1)S(1)}, u32[]{:S(2)}, u32[]{:S(2)}) collective-permute-start(bf16[8,256,1024]{2,1,0:T(8,128)(2,1)S(1)} %shard_map.17.refs_0_), channel_id=1, source_target_pairs={{0,248},{8,16},{16,8},{24,32},{32,24},{40,48},{48,40},{56,64},{64,... | collective-permute-start | bytes 12582920 | tf_op jit(solution)/shard_map/ppermute | solution.py:231
  12.3 95.7 %collective-permute-start.5 = (bf16[7,256,1024]{2,1,0:T(8,128)(2,1)S(1)}, bf16[7,256,1024]{2,1,0:T(8,128)(2,1)S(1)}, u32[]{:S(2)}, u32[]{:S(2)}) collective-permute-start(bf16[7,256,1024]{2,1,0:T(8,128)(2,1)S(1)} %shard_map.19.own0), channel_id=1, source_target_pairs={{0,16},{8,248},{16,32},{24,8},{32,48},{40,24},{48,64},{56,40},{64,... | collective-permute-start | bytes 11010056 | tf_op jit(solution)/shard_map/ppermute | solution.py:231
  12.4 128.3 %collective-permute-start.15 = (bf16[7,256,1024]{2,1,0:T(8,128)(2,1)S(1)}, bf16[7,256,1024]{2,1,0:T(8,128)(2,1)S(1)}, u32[]{:S(2)}, u32[]{:S(2)}) collective-permute-start(bf16[7,256,1024]{2,1,0:T(8,128)(2,1)S(1)} %shard_map.19.own0), channel_id=1, source_target_pairs={{0,240},{8,24},{16,0},{24,40},{32,16},{40,56},{48,32},{56,72},{64,... | collective-permute-start | bytes 11010056 | tf_op jit(solution)/shard_map/ppermute | solution.py:231
  21.5 7.9 %collective-permute-start.1 = (f32[3,64,256]{2,1,0:T(8,128)S(1)}, f32[3,64,256]{2,1,0:T(8,128)S(1)}, u32[]{:S(2)}, u32[]{:S(2)}) collective-permute-start(f32[3,64,256]{2,1,0:T(8,128)S(1)} %get-tuple-element.24), channel_id=1, source_target_pairs={{0,2},{1,3},{2,4},{3,5},{4,6},{5,7},{6,0},{7,1},{8,10},{9,11},{10,... | collective-permute-start | bytes 589832 | tf_op jit(solution)/shard_map/ppermute | solution.py:226
  22.9 85.2 %collective-permute-start.6 = (bf16[1,256,1024]{2,1,0:T(8,128)(2,1)S(1)}, bf16[1,256,1024]{2,1,0:T(8,128)(2,1)S(1)}, u32[]{:S(2)}, u32[]{:S(2)}) collective-permute-start(bf16[1,256,1024]{2,1,0:T(8,128)(2,1)S(1)} %shard_map.18.refs_0_.own1), channel_id=1, source_target_pairs={{0,16},{8,248},{16,32},{24,8},{32,48},{40,24},{48,64},{56,40},{64,... | collective-permute-start | bytes 1572872 | tf_op jit(solution)/shard_map/ppermute | solution.py:231
  29.4 7.2 %collective-permute-start.2 = (f32[3,64,256]{2,1,0:T(8,128)S(1)}, f32[3,64,256]{2,1,0:T(8,128)S(1)}, u32[]{:S(2)}, u32[]{:S(2)}) collective-permute-start(f32[3,64,256]{2,1,0:T(8,128)S(1)} %get-tuple-element.25), channel_id=1, source_target_pairs={{0,4},{1,5},{2,6},{3,7},{4,0},{5,1},{6,2},{7,3},{8,12},{9,13},{10,... | collective-permute-start | bytes 589832 | tf_op jit(solution)/shard_map/ppermute | solution.py:226
  36.5 6.8 %collective-permute-start.3 = (f32[3,64,256]{2,1,0:T(8,128)S(1)}, f32[3,64,256]{2,1,0:T(8,128)S(1)}, u32[]{:S(2)}, u32[]{:S(2)}) collective-permute-start(f32[3,64,256]{2,1,0:T(8,128)S(1)} %get-tuple-element.26), channel_id=1, source_target_pairs={{0,6},{1,7},{2,0},{3,1},{4,2},{5,3},{6,4},{7,5},{8,14},{9,15},{10,... | collective-permute-start | bytes 589832 | tf_op jit(solution)/shard_map/ppermute | solution.py:226
  114.1 6.5 %collective-permute-start.7 = (f32[4,64,256]{2,1,0:T(8,128)S(1)}, f32[4,64,256]{2,1,0:T(8,128)S(1)}, u32[]{:S(2)}, u32[]{:S(2)}) collective-permute-start(f32[4,64,256]{2,1,0:T(8,128)S(1)} %get-tuple-element.28), channel_id=1, source_target_pairs={{0,2},{1,3},{2,4},{3,5},{4,6},{5,7},{6,0},{7,1},{8,10},{9,11},{10,... | collective-permute-start | bytes 786440 | tf_op jit(solution)/shard_map/ppermute | solution.py:226
  115.5 7.9 %collective-permute-start.8 = (f32[4,64,256]{2,1,0:T(8,128)S(1)}, f32[4,64,256]{2,1,0:T(8,128)S(1)}, u32[]{:S(2)}, u32[]{:S(2)}) collective-permute-start(f32[4,64,256]{2,1,0:T(8,128)S(1)} %get-tuple-element.29), channel_id=1, source_target_pairs={{0,4},{1,5},{2,6},{3,7},{4,0},{5,1},{6,2},{7,3},{8,12},{9,13},{10,... | collective-permute-start | bytes 786440 | tf_op jit(solution)/shard_map/ppermute | solution.py:226
  116.1 9.4 %collective-permute-start.9 = (f32[4,64,256]{2,1,0:T(8,128)S(1)}, f32[4,64,256]{2,1,0:T(8,128)S(1)}, u32[]{:S(2)}, u32[]{:S(2)}) collective-permute-start(f32[4,64,256]{2,1,0:T(8,128)S(1)} %get-tuple-element.30), channel_id=1, source_target_pairs={{0,6},{1,7},{2,0},{3,1},{4,2},{5,3},{6,4},{7,5},{8,14},{9,15},{10,... | collective-permute-start | bytes 786440 | tf_op jit(solution)/shard_map/ppermute | solution.py:226
  125.5 1.8 %collective-permute-start.10 = (f32[4,64,256]{2,1,0:T(8,128)S(1)}, f32[4,64,256]{2,1,0:T(8,128)S(1)}, u32[]{:S(2)}, u32[]{:S(2)}) collective-permute-start(f32[4,64,256]{2,1,0:T(8,128)S(1)} %shard_map.23), channel_id=1, source_target_pairs={{0,8},{8,0},{16,24},{24,16},{32,40},{40,32},{48,56},{56,48},{64,72... | collective-permute-start | bytes 786440 | tf_op jit(solution)/shard_map/ppermute | solution.py:231
  127.3 13.2 %collective-permute-start.11 = (f32[4,64,256]{2,1,0:T(8,128)S(1)}, f32[4,64,256]{2,1,0:T(8,128)S(1)}, u32[]{:S(2)}, u32[]{:S(2)}) collective-permute-start(f32[4,64,256]{2,1,0:T(8,128)S(1)} %collective-permute-done.10.swapped), channel_id=1, source_target_pairs={{0,16},{8,8},{16,32},{24,24},{32,48},{40,40},{48,64},{56,56},{64,8... | collective-permute-start | bytes 786440 | tf_op jit(solution)/shard_map/ppermute | solution.py:231
  129.3 15.9 %collective-permute-start.14 = (bf16[1,256,1024]{2,1,0:T(8,128)(2,1)S(1)}, bf16[1,256,1024]{2,1,0:T(8,128)(2,1)S(1)}, u32[]{:S(2)}, u32[]{:S(2)}) collective-permute-start(bf16[1,256,1024]{2,1,0:T(8,128)(2,1)S(1)} %shard_map.18.refs_0_.own1), channel_id=1, source_target_pairs={{0,240},{8,24},{16,0},{24,40},{32,16},{40,56},{48,32},{56,72},{64,... | collective-permute-start | bytes 1572872 | tf_op jit(solution)/shard_map/ppermute | solution.py:231
  140.6 2.5 %collective-permute-start.12 = (f32[4,64,256]{2,1,0:T(8,128)S(1)}, f32[4,64,256]{2,1,0:T(8,128)S(1)}, u32[]{:S(2)}, u32[]{:S(2)}) collective-permute-start(f32[4,64,256]{2,1,0:T(8,128)S(1)} %get-tuple-element.32), channel_id=1, source_target_pairs={{0,8},{8,0},{16,24},{24,16},{32,40},{40,32},{48,56},{56,48},{64,72... | collective-permute-start | bytes 786440 | tf_op jit(solution)/shard_map/ppermute | solution.py:231
  145.5 5.6 %collective-permute-start.16 = (f32[128,256]{1,0:T(8,128)S(1)}, f32[128,256]{1,0:T(8,128)S(1)}, u32[]{:S(2)}, u32[]{:S(2)}) collective-permute-start(f32[128,256]{1,0:T(8,128)S(1)} %get-tuple-element.36), channel_id=1, source_target_pairs={{0,8},{8,0},{16,24},{24,16},{32,40},{40,32},{48,56},{56,48},{64,72... | collective-permute-start | bytes 393224 | tf_op jit(solution)/shard_map/ppermute | solution.py:231
  148.4 13.4 %collective-permute-start.13 = (f32[4,32,256]{2,1,0:T(8,128)S(1)}, f32[4,32,256]{2,1,0:T(8,128)S(1)}, u32[]{:S(2)}, u32[]{:S(2)}) collective-permute-start(f32[4,32,256]{2,1,0:T(8,128)S(1)} %get-tuple-element.34.hidden), channel_id=1, source_target_pairs={{0,1},{1,0},{2,3},{3,2},{4,5},{5,4},{6,7},{7,6},{8,9},{9,8},{10,11... | collective-permute-start | bytes 393224 | tf_op jit(solution)/shard_map/ppermute | solution.py:269
  151.1 4.0 %collective-permute-start.17 = (f32[32,256]{1,0:T(8,128)S(1)}, f32[32,256]{1,0:T(8,128)S(1)}, u32[]{:S(2)}, u32[]{:S(2)}) collective-permute-start(f32[32,256]{1,0:T(8,128)S(1)} %get-tuple-element.38), channel_id=1, source_target_pairs={{0,2},{1,3},{2,4},{3,5},{4,6},{5,7},{6,0},{7,1},{8,10},{9,11},{10,... | collective-permute-start | bytes 98312 | tf_op jit(solution)/shard_map/ppermute | solution.py:226
  152.5 5.4 %collective-permute-start.18 = (f32[32,256]{1,0:T(8,128)S(1)}, f32[32,256]{1,0:T(8,128)S(1)}, u32[]{:S(2)}, u32[]{:S(2)}) collective-permute-start(f32[32,256]{1,0:T(8,128)S(1)} %get-tuple-element.39), channel_id=1, source_target_pairs={{0,4},{1,5},{2,6},{3,7},{4,0},{5,1},{6,2},{7,3},{8,12},{9,13},{10,... | collective-permute-start | bytes 98312 | tf_op jit(solution)/shard_map/ppermute | solution.py:226
  153.1 4.8 %collective-permute-start.19 = (f32[32,256]{1,0:T(8,128)S(1)}, f32[32,256]{1,0:T(8,128)S(1)}, u32[]{:S(2)}, u32[]{:S(2)}) collective-permute-start(f32[32,256]{1,0:T(8,128)S(1)} %get-tuple-element.40), channel_id=1, source_target_pairs={{0,6},{1,7},{2,0},{3,1},{4,2},{5,3},{6,4},{7,5},{8,14},{9,15},{10,... | collective-permute-start | bytes 98312 | tf_op jit(solution)/shard_map/ppermute | solution.py:226
  157.9 9.2 %collective-permute-start.20 = (f32[32,256]{1,0:T(8,128)S(1)}, f32[32,256]{1,0:T(8,128)S(1)}, u32[]{:S(2)}, u32[]{:S(2)}) collective-permute-start(f32[32,256]{1,0:T(8,128)S(1)} %shard_map.29), channel_id=1, source_target_pairs={{0,8},{1,16},{2,10},{3,18},{4,12},{5,20},{6,14},{7,22},{8,17},{9,9... | collective-permute-start | bytes 98312 | tf_op jit(solution)/shard_map/ppermute | solution.py:286
  159.8 7.9 %collective-permute-start.21 = (f32[32,256]{1,0:T(8,128)S(1)}, f32[32,256]{1,0:T(8,128)S(1)}, u32[]{:S(2)}, u32[]{:S(2)}) collective-permute-start(f32[32,256]{1,0:T(8,128)S(1)} %shard_map.29), channel_id=1, source_target_pairs={{0,16},{1,9},{2,18},{3,11},{4,20},{5,13},{6,22},{7,15},{8,8},{9,17... | collective-permute-start | bytes 98312 | tf_op jit(solution)/shard_map/ppermute | solution.py:286

commit v4 on v3

--- a/solution.py
+++ b/solution.py
@@ -22,25 +22,30 @@
 TO_NEAR = [(b, (b - 1 if b % 2 == 0 else b + 1) % COUNT) for b in range(COUNT)]
 TO_FAR_NEAR = [(b, (b + 2 if b % 2 == 0 else b - 2) % COUNT) for b in range(COUNT)]
 TO_FAR_MATE = [(b, (b - 2 if b % 2 == 0 else b + 2) % COUNT) for b in range(COUNT)]
-EVEN_UP = [(b, (b + 2) % COUNT if b % 2 == 0 else b) for b in range(COUNT)]
 
 
 def along_y(shift):
     return [(a, ((a // 2 + shift) % 4) * 2 + a % 2) for a in range(8)]
 
 
+def by_core(even_shift, odd_shift):
+    pairs = []
+    for b in range(COUNT):
+        moves = along_y(odd_shift if b % 2 else even_shift)
+        pairs += [(b * 8 + source, b * 8 + target) for source, target in moves]
+    return pairs
+
+
 ACROSS_X = [(a, a ^ 1) for a in range(8)]
 
 
-def to_upper_even(flip):
+def to_upper_chip():
     pairs = []
     for b in range(COUNT):
         core = b % 2
         for a in range(8):
-            if a % 2 == core ^ flip:
-                pairs.append((b * 8 + a, (b - core + 2) % COUNT * 8 + a // 2 * 2 + core))
-            else:
-                pairs.append((b * 8 + a, (b | 1) * 8 + a))
+            block = (b - core + 2 + (core ^ a % 2)) % COUNT
+            pairs.append((b * 8 + a, block * 8 + a // 2 * 2 + core))
     return pairs
 
 
@@ -157,33 +162,52 @@
     total[...] = a[...] + b[...] + c[...] + d[...]
 
 
-def choose_kernel(chip, swapped, lower, keep, give):
+def choose_kernel(chip, window, keep, give):
+    zero = jnp.zeros((64, ROWS), F32)
+
     def even():
-        keep[0] = chip[0]
-        keep[1] = lower[0]
-        keep[2] = lower[2]
-        keep[3] = jnp.zeros((64, ROWS), F32)
-        give[0:2] = chip[1:3]
-        give[2] = lower[1]
-        give[3] = lower[3]
+        for slot, tile in enumerate((chip[0], window[0], window[2], zero)):
+            keep[slot] = tile
+        for slot, tile in enumerate((chip[1], chip[2], window[1], window[3])):
+            give[slot] = tile
 
     def odd():
-        keep[0:2] = chip[1:3]
-        keep[2] = swapped[1]
-        keep[3] = swapped[3]
+        for slot, tile in enumerate((chip[1], chip[2], zero, zero)):
+            keep[slot] = tile
         give[0] = chip[0]
-        give[1] = swapped[0]
-        give[2] = swapped[2]
-        give[3] = jnp.zeros((64, ROWS), F32)
+        for pair in range(2):
+            give[1 + pair, 0:32] = window[2 * pair, 0:32]
+            give[1 + pair, 32:64] = window[2 * pair + 1, 0:32]
+        give[3] = zero
 
     by_parity(even, odd)
 
 
-def split_kernel(keep, given, stay, leave):
+def split_kernel(keep, given, window, stay, leave, up):
     pair = lax.rem(lax.axis_index("aux"), 2)
-    for half, out in ((pair, stay), (1 - pair, leave)):
-        rows = pl.ds(pl.multiple_of(32 * half, 32), 32)
-        out[...] = keep[:, rows] + given[:, rows]
+    mine = pl.ds(pl.multiple_of(32 * pair, 32), 32)
+    theirs = pl.ds(pl.multiple_of(32 - 32 * pair, 32), 32)
+    for rows, out in ((mine, stay), (theirs, leave)):
+
+        def even():
+            out[0] = keep[0, rows] + given[0, rows]
+            out[1:4] = keep[1:4, rows]
+
+        def odd():
+            out[0:2] = keep[0:2, rows] + given[0:2, rows]
+            out[2:4] = given[2:4, rows]
+
+        by_parity(even, odd)
+
+    def up_even():
+        for i in range(4):
+            first = 32 * (i % 2)
+            up[i] = given[1 + i // 2, first : first + 32]
+
+    def up_odd():
+        up[...] = window[:, 32:64]
+
+    by_parity(up_even, up_odd)
 
 
 def early_kernel(near0, far0, total):
@@ -194,32 +218,63 @@
     )
 
 
-def last_kernel(near0, far1, early, hidden, keep, give, total):
+def last_kernel(near0, far1, early, hidden, total):
     near, far = [(near0, 0)], [(far1, CUT)]
     by_parity(
         lambda: accumulate(total, [(near, far)], CUT, HALF),
         lambda: accumulate(total, [(far, near)], CUT, HALF),
     )
-    core = parity()
-    for y in range(4):
-        for half, out in ((core, keep), (1 - core, give)):
-            rows = pl.ds(pl.multiple_of(64 * y + 32 * half, 32), 32)
-            out[32 * y : 32 * y + 32] = early[0, rows] + total[0, rows]
-
-
-def combine_last_kernel(keep, given, *outs):
-    for shift, out in enumerate(outs):
-        rows = pl.ds(row_of(shift, 32), 32)
-        out[...] = keep[rows] + given[rows]
-
-
-def finish_kernel(stay, come, a, b, out):
-    out[0:3] = stay[0:3] + come[0:3]
-    out[3] = stay[3] + come[3]
-
-    @pl.when(parity() == 0)
-    def _():
-        out[3] += a[...] + b[...]
+    total[...] += early[...]
+
+
+def combine_last_kernel(mine, given, own, first, second):
+    even = parity() == 0
+    for shift, out in ((0, own), (jnp.where(even, 1, 2), first), (3, second)):
+        rows = pl.ds(row_of(shift, 64), 64)
+        out[...] = mine[0, rows] + given[0, rows]
+
+
+def collect_kernel(own, first, second, keep, give):
+    def even():
+        total = own[...] + first[...] + second[...]
+        keep[...] = total[0:32]
+        give[...] = total[32:64]
+
+    def odd():
+        keep[...] = first[32:64]
+        give[...] = first[0:32]
+
+    by_parity(even, odd)
+
+
+def join_kernel(a, b, up, hidden, out):
+    out[0] = a[...] + b[...]
+    for slot, tile in ((1, 0), (2, 2), (3, 1), (4, 3)):
+        out[slot] = up[tile]
+
+
+def hand_kernel(arrived, give):
+    def even():
+        give[0:2] = arrived[3:5]
+        give[2] = jnp.zeros((32, ROWS), F32)
+
+    def odd():
+        give[...] = arrived[0:3]
+
+    by_parity(even, odd)
+
+
+def finish_kernel(stay, come, arrived, given, out):
+    def even():
+        out[0] = stay[0] + come[0]
+        out[1:3] = (stay[1:3] + come[1:3]) + (arrived[1:3] + given[1:3])
+        out[3] = arrived[0] + given[0]
+
+    def odd():
+        out[0:2] = stay[0:2] + come[0:2]
+        out[2:4] = (stay[2:4] + come[2:4]) + (arrived[3:5] + given[0:2])
+
+    by_parity(even, odd)
 
 
 def sum_along_y(parts):
@@ -260,31 +315,33 @@
         scratch=[pltpu.VMEM((4, ROWS, ROWS), F32)],
     )
     window = call(sum_kernel, f32(4, 64, ROWS), *sum_along_y(parts))
-    swapped = send(window, TO_MATE)
-    lower = send(swapped, EVEN_UP)
-    keep, give = call(choose_kernel, [f32(4, 64, ROWS)] * 2, chip, swapped, lower)
+    keep, give = call(choose_kernel, [f32(4, 64, ROWS)] * 2, chip, window)
     given = send(give, TO_MATE)
-
-    stay, leave = call(split_kernel, [f32(4, 32, ROWS)] * 2, keep, given)
+    stay, leave, up = call(split_kernel, [f32(4, 32, ROWS)] * 3, keep, given, window)
     come = lax.ppermute(leave, "aux", ACROSS_X)
 
     early = call(
         early_kernel, f32(1, ROWS, ROWS), near, far_mate[0], flops=CUT * tile
     )
-    keep_last, give_last = call(
+    mine = call(
         last_kernel,
-        [f32(128, ROWS)] * 2,
+        f32(1, ROWS, ROWS),
         near,
         far_mate[1],
         early,
         hidden=(leave,),
         flops=(HALF - CUT) * tile,
-        scratch=[pltpu.VMEM((1, ROWS, ROWS), F32)],
-    )
-    parts = call(combine_last_kernel, [f32(32, ROWS)] * 4, keep_last, send(give_last, TO_MATE))
-    last = call(sum_kernel, f32(32, ROWS), *sum_along_y(parts))
-    arrived = [lax.ppermute(last, ("blk", "aux"), to_upper_even(flip)) for flip in (1, 0)]
-    out = call(finish_kernel, f32(4, 32, ROWS), stay, come, *arrived)
+    )
+    parts = call(combine_last_kernel, [f32(64, ROWS)] * 3, mine, send(mine, TO_MATE))
+    moved = [
+        lax.ppermute(part, ("blk", "aux"), by_core(even, odd))
+        for part, even, odd in ((parts[1], 1, 2), (parts[2], 3, 3))
+    ]
+    keep, give = call(collect_kernel, [f32(32, ROWS)] * 2, parts[0], *moved)
+    joined = call(join_kernel, f32(5, 32, ROWS), keep, send(give, TO_MATE), up, hidden=(come,))
+    arrived = lax.ppermute(joined, ("blk", "aux"), to_upper_chip())
+    given = send(call(hand_kernel, f32(3, 32, ROWS), arrived), TO_MATE)
+    out = call(finish_kernel, f32(4, 32, ROWS), stay, come, arrived, given)
     return out.transpose(2, 0, 1)
 
 

time: 170 us -> 168 us (0.988)
  starting transfers between devices: 35.9 us -> 22.7 us
  waiting for transfers between devices: 112 us -> 123 us
    ppermute x10, starting transfers between devices: 20.5 us -> 11.9 us  [send(): return lax.ppermute(value, 'blk', pairs)]
    ppermute x10, waiting for transfers between devices: 75.2 us -> 83.7 us  [send(): return lax.ppermute(value, 'blk', pairs)]
    ppermute x2 -> x3, waiting for transfers between devices: 5.98 us -> 12 us  [the longest x1 8.5 us: local(): arrived = lax.ppermute(joined, ('blk', 'aux'), to_upper_chip())]
    ppermute x9 -> x6, waiting for transfers between devices: 31.2 us -> 27.5 us  [sum_along_y(): lax.ppermute(parts[d], 'aux', along_y(d))]
    ppermute x9 -> x6, starting transfers between devices: 8.75 us -> 5.71 us  [sum_along_y(): lax.ppermute(parts[d], 'aux', along_y(d))]
    ppermute x2 -> x3, starting transfers between devices: 3.84 us -> 2.19 us  [the longest x2 2.1 us: local(): lax.ppermute(part, ('blk', 'aux'), by_core(even, odd))]
    pallas_call x14 -> x16, Pallas kernels: 20 us -> 20 us  [call(): pl.pallas_call(kernel, out_shape=out_shape, in_specs=(specs or [VMEM] * l...]
  transfers between devices with their start and end apart: 22 -> 20, of which waited for: 14 -> 14; matrix products, arithmetic and copies ran while one was open for 0% -> 0% of each run, Pallas kernels for 10% -> 10%
where the time goes in v4:
time: 168 us; the launch traced here: 166 us
  waiting for transfers between devices  123 us (73%)
  starting transfers between devices  22.7 us (14%)
  Pallas kernels  20 us (12%)
    ppermute x10, waiting for transfers between devices, send(): return lax.ppermute(value, 'blk', pairs)  83.7 us
    ppermute x6, waiting for transfers between devices, sum_along_y(): lax.ppermute(parts[d], 'aux', along_y(d))  27.5 us
    pallas_call x16, Pallas kernels, call(): pl.pallas_call(kernel, out_shape=out_shape, in_specs=(specs or [VMEM] * l...  20 us
    ppermute x10, starting transfers between devices, send(): return lax.ppermute(value, 'blk', pairs)  11.9 us
    ppermute x1, waiting for transfers between devices, local(): arrived = lax.ppermute(joined, ('blk', 'aux'), to_upper_chip())  8.5 us
    ppermute x6, starting transfers between devices, sum_along_y(): lax.ppermute(parts[d], 'aux', along_y(d))  5.71 us
    ppermute x2, waiting for transfers between devices, local(): lax.ppermute(part, ('blk', 'aux'), by_core(even, odd))  3.52 us
  transfers between devices with their start and end apart: 20, of which 14 were waited for; matrix products, arithmetic and copies ran while one was open for 0% of the time, Pallas kernels for 10%

profile of v4, /device:TPU:16, one launch (start us, length us, event | category | flops | bytes accessed | tf_op | source)
XLA Modules:
  0.0 166.1 jit_solution(10291928269810630879)
XLA Ops:
  0.0 2.2 %shard_map.17.refs_0_ = bf16[8,256,1024]{2,1,0:T(8,128)(2,1)S(1)} custom-call(bf16[16,256,1024]{2,1,0:T(8,128)(2,1)} %factors.5), custom_call_target="tpu_custom_call" | custom-call | bytes 8388608 | tf_op jit(solution)/shard_map/pallas_call | solution.py:63
  2.3 6.9 %collective-permute-start.4 = (bf16[8,256,1024]{2,1,0:T(8,128)(2,1)S(1)}, bf16[8,256,1024]{2,1,0:T(8,128)(2,1)S(1)}, u32[]{:S(2)}, u32[]{:S(2)}) collective-permute-start(bf16[8,256,1024]{2,1,0:T(8,128)(2,1)S(1)} %shard_map.17.refs_0_), channel_id=1, source_target_pairs={{0,248},{8,16},{16,8},{24,32},{32,24},{40,48},{48,40},{56,64},{64,... | collective-permute-start | bytes 12582920 | tf_op jit(solution)/shard_map/ppermute | solution.py:286
  9.2 1.0 shard_map.18.refs_0_.own1
  10.3 2.1 %shard_map.19.own0 = bf16[7,256,1024]{2,1,0:T(8,128)(2,1)S(1)} custom-call(bf16[16,256,1024]{2,1,0:T(8,128)(2,1)} %factors.5, bf16[1,256,1024]{2,1,0:T(8,128)(2,1)S(1)} %shard_map.18.refs_0_.own1), custom_call_target="tpu_custom_call" | custom-call | bytes 8388608 | tf_op jit(solution)/shard_map/pallas_call | solution.py:63
  12.4 4.1 %collective-permute-start.13 = (bf16[7,256,1024]{2,1,0:T(8,128)(2,1)S(1)}, bf16[7,256,1024]{2,1,0:T(8,128)(2,1)S(1)}, u32[]{:S(2)}, u32[]{:S(2)}) collective-permute-start(bf16[7,256,1024]{2,1,0:T(8,128)(2,1)S(1)} %shard_map.19.own0), channel_id=1, source_target_pairs={{0,240},{8,24},{16,0},{24,40},{32,16},{40,56},{48,32},{56,72},{64,... | collective-permute-start | bytes 11010056 | tf_op jit(solution)/shard_map/ppermute | solution.py:286
  16.6 5.0 %shard_map.20 = (f32[3,64,256]{2,1,0:T(8,128)S(1)}, f32[3,64,256]{2,1,0:T(8,128)S(1)}, f32[3,64,256]{2,1,0:T(8,128)S(1)}, f32[3,64,256]{2,1,0:T(8,128)S(1)}) custom-call(bf16[7,256,1024]{2,1,0:T(8,128)(2,1)S(1)} %shard_map.19.own0, bf16[1,256,1024]{2,1,0:T(8,128)(2,1)S(1)} %shard_map.18.refs_0_.own1, bf16[8,256,1024]{2,1,0:T(8,128)(2,1)S(1)} %collective-permute-done.mate0), custom_call_target="tpu_custom_call" | custom-call | flops 3221225472 | bytes 8388608 | tf_op jit(solution)/shard_map/pallas_call | solution.py:63
  21.5 1.4 collective-permute-start.1
  22.9 6.5 %collective-permute-done.1.b = f32[3,64,256]{2,1,0:T(8,128)S(1)} collective-permute-done((f32[3,64,256]{2,1,0:T(8,128)S(1)}, f32[3,64,256]{2,1,0:T(8,128)S(1)}, u32[]{:S(2)}, u32[]{:S(2)}) %collective-permute-start.1) | collective-permute-done | bytes 196640 | tf_op jit(solution)/shard_map/ppermute | solution.py:281
  29.5 7.0 %collective-permute-done.2.c = f32[3,64,256]{2,1,0:T(8,128)S(1)} collective-permute-done((f32[3,64,256]{2,1,0:T(8,128)S(1)}, f32[3,64,256]{2,1,0:T(8,128)S(1)}, u32[]{:S(2)}, u32[]{:S(2)}) %collective-permute-start.2) | collective-permute-done | bytes 196640 | tf_op jit(solution)/shard_map/ppermute | solution.py:281
  36.5 1.1 collective-permute-start.3
  37.7 5.6 %collective-permute-done.3.d = f32[3,64,256]{2,1,0:T(8,128)S(1)} collective-permute-done((f32[3,64,256]{2,1,0:T(8,128)S(1)}, f32[3,64,256]{2,1,0:T(8,128)S(1)}, u32[]{:S(2)}, u32[]{:S(2)}) %collective-permute-start.3) | collective-permute-done | bytes 196640 | tf_op jit(solution)/shard_map/ppermute | solution.py:281
  43.4 64.7 %collective-permute-done.6.far1 = bf16[1,256,1024]{2,1,0:T(8,128)(2,1)S(1)} collective-permute-done((bf16[1,256,1024]{2,1,0:T(8,128)(2,1)S(1)}, bf16[1,256,1024]{2,1,0:T(8,128)(2,1)S(1)}, u32[]{:S(2)}, u32[]{:S(2)}) %collective-permute-start.6) | collective-permute-done | bytes 524320 | tf_op jit(solution)/shard_map/ppermute | solution.py:286
  108.0 6.1 %shard_map.22 = (f32[4,64,256]{2,1,0:T(8,128)S(1)}, f32[4,64,256]{2,1,0:T(8,128)S(1)}, f32[4,64,256]{2,1,0:T(8,128)S(1)}, f32[4,64,256]{2,1,0:T(8,128)S(1)}) custom-call(bf16[7,256,1024]{2,1,0:T(8,128)(2,1)S(1)} %shard_map.19.own0, bf16[1,256,1024]{2,1,0:T(8,128)(2,1)S(1)} %shard_map.18.refs_0_.own1, bf16[8,256,1024]{2,1,0:T(8,128)(2,1)S(1)} %collective-permute-done.mate0, ...), custom_call_target="tpu_custom_call" | custom-call | flops 4294967296 | bytes 16777216 | tf_op jit(solution)/shard_map/pallas_call | solution.py:63
  114.1 1.4 collective-permute-start.7
  115.5 0.6 collective-permute-start.8
  116.1 1.1 collective-permute-start.9
  117.2 3.4 %collective-permute-done.7.b = f32[4,64,256]{2,1,0:T(8,128)S(1)} collective-permute-done((f32[4,64,256]{2,1,0:T(8,128)S(1)}, f32[4,64,256]{2,1,0:T(8,128)S(1)}, u32[]{:S(2)}, u32[]{:S(2)}) %collective-permute-start.7) | collective-permute-done | bytes 262176 | tf_op jit(solution)/shard_map/ppermute | solution.py:281
  120.6 2.8 %collective-permute-done.8.c = f32[4,64,256]{2,1,0:T(8,128)S(1)} collective-permute-done((f32[4,64,256]{2,1,0:T(8,128)S(1)}, f32[4,64,256]{2,1,0:T(8,128)S(1)}, u32[]{:S(2)}, u32[]{:S(2)}) %collective-permute-start.8) | collective-permute-done | bytes 262176 | tf_op jit(solution)/shard_map/ppermute | solution.py:281
  123.4 2.1 %collective-permute-done.9.d = f32[4,64,256]{2,1,0:T(8,128)S(1)} collective-permute-done((f32[4,64,256]{2,1,0:T(8,128)S(1)}, f32[4,64,256]{2,1,0:T(8,128)S(1)}, u32[]{:S(2)}, u32[]{:S(2)}) %collective-permute-start.9) | collective-permute-done | bytes 262176 | tf_op jit(solution)/shard_map/ppermute | solution.py:281
  125.7 13.8 %collective-permute-done.13.far0 = bf16[7,256,1024]{2,1,0:T(8,128)(2,1)S(1)} collective-permute-done((bf16[7,256,1024]{2,1,0:T(8,128)(2,1)S(1)}, bf16[7,256,1024]{2,1,0:T(8,128)(2,1)S(1)}, u32[]{:S(2)}, u32[]{:S(2)}) %collective-permute-start.13) | collective-permute-done | bytes 3670048 | tf_op jit(solution)/shard_map/ppermute | solution.py:286
  139.5 2.4 %shard_map.26.early = f32[1,256,256]{2,1,0:T(8,128)S(1)} custom-call(bf16[8,256,1024]{2,1,0:T(8,128)(2,1)S(1)} %collective-permute-done.4.near0, bf16[7,256,1024]{2,1,0:T(8,128)(2,1)S(1)} %collective-permute-done.13.far0), custom_call_target="tpu_custom_call" | custom-call | flops 939524096 | bytes 7864320 | tf_op jit(solution)/shard_map/pallas_call | solution.py:63
  142.0 3.1 %collective-permute-done.12.far1 = bf16[1,256,1024]{2,1,0:T(8,128)(2,1)S(1)} collective-permute-done((bf16[1,256,1024]{2,1,0:T(8,128)(2,1)S(1)}, bf16[1,256,1024]{2,1,0:T(8,128)(2,1)S(1)}, u32[]{:S(2)}, u32[]{:S(2)}) %collective-permute-start.12) | collective-permute-done | bytes 524320 | tf_op jit(solution)/shard_map/ppermute | solution.py:286
  145.6 2.8 %collective-permute-start.11 = (f32[4,32,256]{2,1,0:T(8,128)S(1)}, f32[4,32,256]{2,1,0:T(8,128)S(1)}, u32[]{:S(2)}, u32[]{:S(2)}) collective-permute-start(f32[4,32,256]{2,1,0:T(8,128)S(1)} %get-tuple-element.34.hidden), channel_id=1, source_target_pairs={{0,1},{1,0},{2,3},{3,2},{4,5},{5,4},{6,7},{7,6},{8,9},{9,8},{10,11... | collective-permute-start | bytes 393224 | tf_op jit(solution)/shard_map/ppermute | solution.py:321
  148.4 1.4 collective-permute-start.15
  149.8 0.7 collective-permute-start.16
  150.5 2.2 %collective-permute-done.15.first = f32[64,256]{1,0:T(8,128)S(1)} collective-permute-done((f32[64,256]{1,0:T(8,128)S(1)}, f32[64,256]{1,0:T(8,128)S(1)}, u32[]{:S(2)}, u32[]{:S(2)}) %collective-permute-start.15) | collective-permute-done | bytes 65568 | tf_op jit(solution)/shard_map/ppermute | solution.py:337
  152.8 1.3 collective-permute-done.16.second
  154.2 1.2 collective-permute-done.17.b
  155.5 8.5 %collective-permute-done.18.arrived = f32[5,32,256]{2,1,0:T(8,128)S(1)} collective-permute-done((f32[5,32,256]{2,1,0:T(8,128)S(1)}, f32[5,32,256]{2,1,0:T(8,128)S(1)}, u32[]{:S(2)}, u32[]{:S(2)}) %collective-permute-start.18) | collective-permute-done | bytes 163872 | tf_op jit(solution)/shard_map/ppermute | solution.py:342
  164.0 0.5 collective-permute-start.19
  164.5 0.9 collective-permute-done.19.given
  165.4 0.7 shard_map.32
  (24 shorter events, 1.3 us)
Async XLA Ops:
  2.2 14.3 %collective-permute-start = (bf16[8,256,1024]{2,1,0:T(8,128)(2,1)S(1)}, bf16[8,256,1024]{2,1,0:T(8,128)(2,1)S(1)}, u32[]{:S(2)}, u32[]{:S(2)}) collective-permute-start(bf16[8,256,1024]{2,1,0:T(8,128)(2,1)S(1)} %shard_map.17.refs_0_), channel_id=1, source_target_pairs={{0,8},{8,0},{16,24},{24,16},{32,40},{40,32},{48,56},{56,48},{64,72... | collective-permute-start | bytes 12582920 | tf_op jit(solution)/shard_map/ppermute | solution.py:286
  2.3 105.7 %collective-permute-start.4 = (bf16[8,256,1024]{2,1,0:T(8,128)(2,1)S(1)}, bf16[8,256,1024]{2,1,0:T(8,128)(2,1)S(1)}, u32[]{:S(2)}, u32[]{:S(2)}) collective-permute-start(bf16[8,256,1024]{2,1,0:T(8,128)(2,1)S(1)} %shard_map.17.refs_0_), channel_id=1, source_target_pairs={{0,248},{8,16},{16,8},{24,32},{32,24},{40,48},{48,40},{56,64},{64,... | collective-permute-start | bytes 12582920 | tf_op jit(solution)/shard_map/ppermute | solution.py:286
  12.3 95.7 %collective-permute-start.5 = (bf16[7,256,1024]{2,1,0:T(8,128)(2,1)S(1)}, bf16[7,256,1024]{2,1,0:T(8,128)(2,1)S(1)}, u32[]{:S(2)}, u32[]{:S(2)}) collective-permute-start(bf16[7,256,1024]{2,1,0:T(8,128)(2,1)S(1)} %shard_map.19.own0), channel_id=1, source_target_pairs={{0,16},{8,248},{16,32},{24,8},{32,48},{40,24},{48,64},{56,40},{64,... | collective-permute-start | bytes 11010056 | tf_op jit(solution)/shard_map/ppermute | solution.py:286
  12.4 127.1 %collective-permute-start.13 = (bf16[7,256,1024]{2,1,0:T(8,128)(2,1)S(1)}, bf16[7,256,1024]{2,1,0:T(8,128)(2,1)S(1)}, u32[]{:S(2)}, u32[]{:S(2)}) collective-permute-start(bf16[7,256,1024]{2,1,0:T(8,128)(2,1)S(1)} %shard_map.19.own0), channel_id=1, source_target_pairs={{0,240},{8,24},{16,0},{24,40},{32,16},{40,56},{48,32},{56,72},{64,... | collective-permute-start | bytes 11010056 | tf_op jit(solution)/shard_map/ppermute | solution.py:286
  21.5 7.9 %collective-permute-start.1 = (f32[3,64,256]{2,1,0:T(8,128)S(1)}, f32[3,64,256]{2,1,0:T(8,128)S(1)}, u32[]{:S(2)}, u32[]{:S(2)}) collective-permute-start(f32[3,64,256]{2,1,0:T(8,128)S(1)} %get-tuple-element.24), channel_id=1, source_target_pairs={{0,2},{1,3},{2,4},{3,5},{4,6},{5,7},{6,0},{7,1},{8,10},{9,11},{10,... | collective-permute-start | bytes 589832 | tf_op jit(solution)/shard_map/ppermute | solution.py:281
  22.9 85.2 %collective-permute-start.6 = (bf16[1,256,1024]{2,1,0:T(8,128)(2,1)S(1)}, bf16[1,256,1024]{2,1,0:T(8,128)(2,1)S(1)}, u32[]{:S(2)}, u32[]{:S(2)}) collective-permute-start(bf16[1,256,1024]{2,1,0:T(8,128)(2,1)S(1)} %shard_map.18.refs_0_.own1), channel_id=1, source_target_pairs={{0,16},{8,248},{16,32},{24,8},{32,48},{40,24},{48,64},{56,40},{64,... | collective-permute-start | bytes 1572872 | tf_op jit(solution)/shard_map/ppermute | solution.py:286
  29.4 7.2 %collective-permute-start.2 = (f32[3,64,256]{2,1,0:T(8,128)S(1)}, f32[3,64,256]{2,1,0:T(8,128)S(1)}, u32[]{:S(2)}, u32[]{:S(2)}) collective-permute-start(f32[3,64,256]{2,1,0:T(8,128)S(1)} %get-tuple-element.25), channel_id=1, source_target_pairs={{0,4},{1,5},{2,6},{3,7},{4,0},{5,1},{6,2},{7,3},{8,12},{9,13},{10,... | collective-permute-start | bytes 589832 | tf_op jit(solution)/shard_map/ppermute | solution.py:281
  36.5 6.8 %collective-permute-start.3 = (f32[3,64,256]{2,1,0:T(8,128)S(1)}, f32[3,64,256]{2,1,0:T(8,128)S(1)}, u32[]{:S(2)}, u32[]{:S(2)}) collective-permute-start(f32[3,64,256]{2,1,0:T(8,128)S(1)} %get-tuple-element.26), channel_id=1, source_target_pairs={{0,6},{1,7},{2,0},{3,1},{4,2},{5,3},{6,4},{7,5},{8,14},{9,15},{10,... | collective-permute-start | bytes 589832 | tf_op jit(solution)/shard_map/ppermute | solution.py:281
  114.1 6.5 %collective-permute-start.7 = (f32[4,64,256]{2,1,0:T(8,128)S(1)}, f32[4,64,256]{2,1,0:T(8,128)S(1)}, u32[]{:S(2)}, u32[]{:S(2)}) collective-permute-start(f32[4,64,256]{2,1,0:T(8,128)S(1)} %get-tuple-element.28), channel_id=1, source_target_pairs={{0,2},{1,3},{2,4},{3,5},{4,6},{5,7},{6,0},{7,1},{8,10},{9,11},{10,... | collective-permute-start | bytes 786440 | tf_op jit(solution)/shard_map/ppermute | solution.py:281
  115.5 7.9 %collective-permute-start.8 = (f32[4,64,256]{2,1,0:T(8,128)S(1)}, f32[4,64,256]{2,1,0:T(8,128)S(1)}, u32[]{:S(2)}, u32[]{:S(2)}) collective-permute-start(f32[4,64,256]{2,1,0:T(8,128)S(1)} %get-tuple-element.29), channel_id=1, source_target_pairs={{0,4},{1,5},{2,6},{3,7},{4,0},{5,1},{6,2},{7,3},{8,12},{9,13},{10,... | collective-permute-start | bytes 786440 | tf_op jit(solution)/shard_map/ppermute | solution.py:281
  116.1 9.4 %collective-permute-start.9 = (f32[4,64,256]{2,1,0:T(8,128)S(1)}, f32[4,64,256]{2,1,0:T(8,128)S(1)}, u32[]{:S(2)}, u32[]{:S(2)}) collective-permute-start(f32[4,64,256]{2,1,0:T(8,128)S(1)} %get-tuple-element.30), channel_id=1, source_target_pairs={{0,6},{1,7},{2,0},{3,1},{4,2},{5,3},{6,4},{7,5},{8,14},{9,15},{10,... | collective-permute-start | bytes 786440 | tf_op jit(solution)/shard_map/ppermute | solution.py:281
  117.2 27.9 %collective-permute-start.12 = (bf16[1,256,1024]{2,1,0:T(8,128)(2,1)S(1)}, bf16[1,256,1024]{2,1,0:T(8,128)(2,1)S(1)}, u32[]{:S(2)}, u32[]{:S(2)}) collective-permute-start(bf16[1,256,1024]{2,1,0:T(8,128)(2,1)S(1)} %shard_map.18.refs_0_.own1), channel_id=1, source_target_pairs={{0,240},{8,24},{16,0},{24,40},{32,16},{40,56},{48,32},{56,72},{64,... | collective-permute-start | bytes 1572872 | tf_op jit(solution)/shard_map/ppermute | solution.py:286
  125.6 16.3 %collective-permute-start.10 = (f32[4,64,256]{2,1,0:T(8,128)S(1)}, f32[4,64,256]{2,1,0:T(8,128)S(1)}, u32[]{:S(2)}, u32[]{:S(2)}) collective-permute-start(f32[4,64,256]{2,1,0:T(8,128)S(1)} %get-tuple-element.32), channel_id=1, source_target_pairs={{0,8},{8,0},{16,24},{24,16},{32,40},{40,32},{48,56},{56,48},{64,72... | collective-permute-start | bytes 786440 | tf_op jit(solution)/shard_map/ppermute | solution.py:286
  145.5 2.9 %collective-permute-start.14 = (f32[1,256,256]{2,1,0:T(8,128)S(1)}, f32[1,256,256]{2,1,0:T(8,128)S(1)}, u32[]{:S(2)}, u32[]{:S(2)}) collective-permute-start(f32[1,256,256]{2,1,0:T(8,128)S(1)} %shard_map.27.mine), channel_id=1, source_target_pairs={{0,8},{8,0},{16,24},{24,16},{32,40},{40,32},{48,56},{56,48},{64,72... | collective-permute-start | bytes 786440 | tf_op jit(solution)/shard_map/ppermute | solution.py:286
  145.6 8.6 %collective-permute-start.11 = (f32[4,32,256]{2,1,0:T(8,128)S(1)}, f32[4,32,256]{2,1,0:T(8,128)S(1)}, u32[]{:S(2)}, u32[]{:S(2)}) collective-permute-start(f32[4,32,256]{2,1,0:T(8,128)S(1)} %get-tuple-element.34.hidden), channel_id=1, source_target_pairs={{0,1},{1,0},{2,3},{3,2},{4,5},{5,4},{6,7},{7,6},{8,9},{9,8},{10,11... | collective-permute-start | bytes 393224 | tf_op jit(solution)/shard_map/ppermute | solution.py:321
  148.4 4.4 %collective-permute-start.15 = (f32[64,256]{1,0:T(8,128)S(1)}, f32[64,256]{1,0:T(8,128)S(1)}, u32[]{:S(2)}, u32[]{:S(2)}) collective-permute-start(f32[64,256]{1,0:T(8,128)S(1)} %get-tuple-element.36), channel_id=1, source_target_pairs={{0,2},{1,3},{2,4},{3,5},{4,6},{5,7},{6,0},{7,1},{8,12},{9,13},{10,... | collective-permute-start | bytes 196616 | tf_op jit(solution)/shard_map/ppermute | solution.py:337
  149.8 4.3 %collective-permute-start.16 = (f32[64,256]{1,0:T(8,128)S(1)}, f32[64,256]{1,0:T(8,128)S(1)}, u32[]{:S(2)}, u32[]{:S(2)}) collective-permute-start(f32[64,256]{1,0:T(8,128)S(1)} %get-tuple-element.37), channel_id=1, source_target_pairs={{0,6},{1,7},{2,0},{3,1},{4,2},{5,3},{6,4},{7,5},{8,14},{9,15},{10,... | collective-permute-start | bytes 196616 | tf_op jit(solution)/shard_map/ppermute | solution.py:337
  154.1 1.3 collective-permute-start.17
  155.4 8.6 %collective-permute-start.18 = (f32[5,32,256]{2,1,0:T(8,128)S(1)}, f32[5,32,256]{2,1,0:T(8,128)S(1)}, u32[]{:S(2)}, u32[]{:S(2)}) collective-permute-start(f32[5,32,256]{2,1,0:T(8,128)S(1)} %shard_map.30), channel_id=1, source_target_pairs={{0,16},{1,24},{2,18},{3,26},{4,20},{5,28},{6,22},{7,30},{8,25},{9,... | collective-permute-start | bytes 491528 | tf_op jit(solution)/shard_map/ppermute | solution.py:342
  164.0 1.4 collective-permute-start.19

commit v5 on v4

--- a/solution.py
+++ b/solution.py
@@ -247,32 +247,35 @@
     by_parity(even, odd)
 
 
-def join_kernel(a, b, up, hidden, out):
-    out[0] = a[...] + b[...]
-    for slot, tile in ((1, 0), (2, 2), (3, 1), (4, 3)):
-        out[slot] = up[tile]
-
-
-def hand_kernel(arrived, give):
+def join_kernel(a, b, hidden, out):
+    out[...] = a[...] + b[...]
+
+
+def hand_kernel(last, up, give):
     def even():
-        give[0:2] = arrived[3:5]
+        give[0] = up[1]
+        give[1] = up[3]
         give[2] = jnp.zeros((32, ROWS), F32)
 
     def odd():
-        give[...] = arrived[0:3]
+        give[0] = up[0]
+        give[1] = up[2]
+        give[2] = last[...]
 
     by_parity(even, odd)
 
 
-def finish_kernel(stay, come, arrived, given, out):
+def finish_kernel(stay, come, last, up, given, out):
     def even():
         out[0] = stay[0] + come[0]
-        out[1:3] = (stay[1:3] + come[1:3]) + (arrived[1:3] + given[1:3])
-        out[3] = arrived[0] + given[0]
+        out[1] = (stay[1] + come[1]) + (up[0] + given[0])
+        out[2] = (stay[2] + come[2]) + (up[2] + given[1])
+        out[3] = last[...] + given[2]
 
     def odd():
         out[0:2] = stay[0:2] + come[0:2]
-        out[2:4] = (stay[2:4] + come[2:4]) + (arrived[3:5] + given[0:2])
+        out[2] = (stay[2] + come[2]) + (up[1] + given[0])
+        out[3] = (stay[3] + come[3]) + (up[3] + given[1])
 
     by_parity(even, odd)
 
@@ -338,10 +341,11 @@
         for part, even, odd in ((parts[1], 1, 2), (parts[2], 3, 3))
     ]
     keep, give = call(collect_kernel, [f32(32, ROWS)] * 2, parts[0], *moved)
-    joined = call(join_kernel, f32(5, 32, ROWS), keep, send(give, TO_MATE), up, hidden=(come,))
-    arrived = lax.ppermute(joined, ("blk", "aux"), to_upper_chip())
-    given = send(call(hand_kernel, f32(3, 32, ROWS), arrived), TO_MATE)
-    out = call(finish_kernel, f32(4, 32, ROWS), stay, come, arrived, given)
+    up = lax.ppermute(up, ("blk", "aux"), to_upper_chip())
+    last = call(join_kernel, f32(32, ROWS), keep, send(give, TO_MATE), hidden=(up,))
+    last = lax.ppermute(last, ("blk", "aux"), to_upper_chip())
+    given = send(call(hand_kernel, f32(3, 32, ROWS), last, up), TO_MATE)
+    out = call(finish_kernel, f32(4, 32, ROWS), stay, come, last, up, given)
     return out.transpose(2, 0, 1)
 
 

time: 168 us -> 166 us (0.988)
  waiting for transfers between devices: 123 us -> 120 us
    ppermute x1 -> x2, waiting for transfers between devices: 8.5 us -> 5.14 us  [the longest x1 3.69 us: local(): last = lax.ppermute(last, ('blk', 'aux'), to_upper_chip())]
  transfers between devices with their start and end apart: 20 -> 21, of which waited for: 14 -> 16; matrix products, arithmetic and copies ran while one was open for 0% -> 0% of each run, Pallas kernels for 10% -> 10%
where the time goes in v5:
time: 166 us; the launch traced here: 164 us
  waiting for transfers between devices  120 us (72%)
  starting transfers between devices  24 us (14%)
  Pallas kernels  20 us (12%)
    ppermute x10, waiting for transfers between devices, send(): return lax.ppermute(value, 'blk', pairs)  83.6 us
    ppermute x6, waiting for transfers between devices, sum_along_y(): lax.ppermute(parts[d], 'aux', along_y(d))  27.5 us
    pallas_call x16, Pallas kernels, call(): pl.pallas_call(kernel, out_shape=out_shape, in_specs=(specs or [VMEM] * l...  20 us
    ppermute x10, starting transfers between devices, send(): return lax.ppermute(value, 'blk', pairs)  13.4 us
    ppermute x6, starting transfers between devices, sum_along_y(): lax.ppermute(parts[d], 'aux', along_y(d))  5.71 us
    ppermute x1, waiting for transfers between devices, local(): last = lax.ppermute(last, ('blk', 'aux'), to_upper_chip())  3.69 us
    ppermute x2, waiting for transfers between devices, local(): lax.ppermute(part, ('blk', 'aux'), by_core(even, odd))  3.52 us
  transfers between devices with their start and end apart: 21, of which 16 were waited for; matrix products, arithmetic and copies ran while one was open for 0% of the time, Pallas kernels for 10%

profile of v5, /device:TPU:16, one launch (start us, length us, event | category | flops | bytes accessed | tf_op | source)
XLA Modules:
  0.0 164.3 jit_solution(7729558928307070752)
XLA Ops:
  0.0 2.2 %shard_map.17.refs_0_ = bf16[8,256,1024]{2,1,0:T(8,128)(2,1)S(1)} custom-call(bf16[16,256,1024]{2,1,0:T(8,128)(2,1)} %factors.5), custom_call_target="tpu_custom_call" | custom-call | bytes 8388608 | tf_op jit(solution)/shard_map/pallas_call | solution.py:63
  2.3 6.9 %collective-permute-start.4 = (bf16[8,256,1024]{2,1,0:T(8,128)(2,1)S(1)}, bf16[8,256,1024]{2,1,0:T(8,128)(2,1)S(1)}, u32[]{:S(2)}, u32[]{:S(2)}) collective-permute-start(bf16[8,256,1024]{2,1,0:T(8,128)(2,1)S(1)} %shard_map.17.refs_0_), channel_id=1, source_target_pairs={{0,248},{8,16},{16,8},{24,32},{32,24},{40,48},{48,40},{56,64},{64,... | collective-permute-start | bytes 12582920 | tf_op jit(solution)/shard_map/ppermute | solution.py:289
  9.2 1.0 shard_map.18.refs_0_.own1
  10.3 2.1 %shard_map.19.own0 = bf16[7,256,1024]{2,1,0:T(8,128)(2,1)S(1)} custom-call(bf16[16,256,1024]{2,1,0:T(8,128)(2,1)} %factors.5, bf16[1,256,1024]{2,1,0:T(8,128)(2,1)S(1)} %shard_map.18.refs_0_.own1), custom_call_target="tpu_custom_call" | custom-call | bytes 8388608 | tf_op jit(solution)/shard_map/pallas_call | solution.py:63
  12.4 4.1 %collective-permute-start.13 = (bf16[7,256,1024]{2,1,0:T(8,128)(2,1)S(1)}, bf16[7,256,1024]{2,1,0:T(8,128)(2,1)S(1)}, u32[]{:S(2)}, u32[]{:S(2)}) collective-permute-start(bf16[7,256,1024]{2,1,0:T(8,128)(2,1)S(1)} %shard_map.19.own0), channel_id=1, source_target_pairs={{0,240},{8,24},{16,0},{24,40},{32,16},{40,56},{48,32},{56,72},{64,... | collective-permute-start | bytes 11010056 | tf_op jit(solution)/shard_map/ppermute | solution.py:289
  16.6 5.0 %shard_map.20 = (f32[3,64,256]{2,1,0:T(8,128)S(1)}, f32[3,64,256]{2,1,0:T(8,128)S(1)}, f32[3,64,256]{2,1,0:T(8,128)S(1)}, f32[3,64,256]{2,1,0:T(8,128)S(1)}) custom-call(bf16[7,256,1024]{2,1,0:T(8,128)(2,1)S(1)} %shard_map.19.own0, bf16[1,256,1024]{2,1,0:T(8,128)(2,1)S(1)} %shard_map.18.refs_0_.own1, bf16[8,256,1024]{2,1,0:T(8,128)(2,1)S(1)} %collective-permute-done.mate0), custom_call_target="tpu_custom_call" | custom-call | flops 3221225472 | bytes 8388608 | tf_op jit(solution)/shard_map/pallas_call | solution.py:63
  21.5 1.4 collective-permute-start.1
  22.9 6.5 %collective-permute-done.1.b = f32[3,64,256]{2,1,0:T(8,128)S(1)} collective-permute-done((f32[3,64,256]{2,1,0:T(8,128)S(1)}, f32[3,64,256]{2,1,0:T(8,128)S(1)}, u32[]{:S(2)}, u32[]{:S(2)}) %collective-permute-start.1) | collective-permute-done | bytes 196640 | tf_op jit(solution)/shard_map/ppermute | solution.py:284
  29.5 7.0 %collective-permute-done.2.c = f32[3,64,256]{2,1,0:T(8,128)S(1)} collective-permute-done((f32[3,64,256]{2,1,0:T(8,128)S(1)}, f32[3,64,256]{2,1,0:T(8,128)S(1)}, u32[]{:S(2)}, u32[]{:S(2)}) %collective-permute-start.2) | collective-permute-done | bytes 196640 | tf_op jit(solution)/shard_map/ppermute | solution.py:284
  36.5 1.1 collective-permute-start.3
  37.7 5.6 %collective-permute-done.3.d = f32[3,64,256]{2,1,0:T(8,128)S(1)} collective-permute-done((f32[3,64,256]{2,1,0:T(8,128)S(1)}, f32[3,64,256]{2,1,0:T(8,128)S(1)}, u32[]{:S(2)}, u32[]{:S(2)}) %collective-permute-start.3) | collective-permute-done | bytes 196640 | tf_op jit(solution)/shard_map/ppermute | solution.py:284
  43.4 64.7 %collective-permute-done.6.far1 = bf16[1,256,1024]{2,1,0:T(8,128)(2,1)S(1)} collective-permute-done((bf16[1,256,1024]{2,1,0:T(8,128)(2,1)S(1)}, bf16[1,256,1024]{2,1,0:T(8,128)(2,1)S(1)}, u32[]{:S(2)}, u32[]{:S(2)}) %collective-permute-start.6) | collective-permute-done | bytes 524320 | tf_op jit(solution)/shard_map/ppermute | solution.py:289
  108.0 6.1 %shard_map.22 = (f32[4,64,256]{2,1,0:T(8,128)S(1)}, f32[4,64,256]{2,1,0:T(8,128)S(1)}, f32[4,64,256]{2,1,0:T(8,128)S(1)}, f32[4,64,256]{2,1,0:T(8,128)S(1)}) custom-call(bf16[7,256,1024]{2,1,0:T(8,128)(2,1)S(1)} %shard_map.19.own0, bf16[1,256,1024]{2,1,0:T(8,128)(2,1)S(1)} %shard_map.18.refs_0_.own1, bf16[8,256,1024]{2,1,0:T(8,128)(2,1)S(1)} %collective-permute-done.mate0, ...), custom_call_target="tpu_custom_call" | custom-call | flops 4294967296 | bytes 16777216 | tf_op jit(solution)/shard_map/pallas_call | solution.py:63
  114.1 1.4 collective-permute-start.7
  115.5 0.6 collective-permute-start.8
  116.1 1.1 collective-permute-start.9
  117.2 3.4 %collective-permute-done.7.b = f32[4,64,256]{2,1,0:T(8,128)S(1)} collective-permute-done((f32[4,64,256]{2,1,0:T(8,128)S(1)}, f32[4,64,256]{2,1,0:T(8,128)S(1)}, u32[]{:S(2)}, u32[]{:S(2)}) %collective-permute-start.7) | collective-permute-done | bytes 262176 | tf_op jit(solution)/shard_map/ppermute | solution.py:284
  120.6 2.8 %collective-permute-done.8.c = f32[4,64,256]{2,1,0:T(8,128)S(1)} collective-permute-done((f32[4,64,256]{2,1,0:T(8,128)S(1)}, f32[4,64,256]{2,1,0:T(8,128)S(1)}, u32[]{:S(2)}, u32[]{:S(2)}) %collective-permute-start.8) | collective-permute-done | bytes 262176 | tf_op jit(solution)/shard_map/ppermute | solution.py:284
  123.4 2.1 %collective-permute-done.9.d = f32[4,64,256]{2,1,0:T(8,128)S(1)} collective-permute-done((f32[4,64,256]{2,1,0:T(8,128)S(1)}, f32[4,64,256]{2,1,0:T(8,128)S(1)}, u32[]{:S(2)}, u32[]{:S(2)}) %collective-permute-start.9) | collective-permute-done | bytes 262176 | tf_op jit(solution)/shard_map/ppermute | solution.py:284
  125.7 13.8 %collective-permute-done.13.far0 = bf16[7,256,1024]{2,1,0:T(8,128)(2,1)S(1)} collective-permute-done((bf16[7,256,1024]{2,1,0:T(8,128)(2,1)S(1)}, bf16[7,256,1024]{2,1,0:T(8,128)(2,1)S(1)}, u32[]{:S(2)}, u32[]{:S(2)}) %collective-permute-start.13) | collective-permute-done | bytes 3670048 | tf_op jit(solution)/shard_map/ppermute | solution.py:289
  139.5 2.4 %shard_map.26.early = f32[1,256,256]{2,1,0:T(8,128)S(1)} custom-call(bf16[8,256,1024]{2,1,0:T(8,128)(2,1)S(1)} %collective-permute-done.4.near0, bf16[7,256,1024]{2,1,0:T(8,128)(2,1)S(1)} %collective-permute-done.13.far0), custom_call_target="tpu_custom_call" | custom-call | flops 939524096 | bytes 7864320 | tf_op jit(solution)/shard_map/pallas_call | solution.py:63
  142.0 3.1 %collective-permute-done.12.far1 = bf16[1,256,1024]{2,1,0:T(8,128)(2,1)S(1)} collective-permute-done((bf16[1,256,1024]{2,1,0:T(8,128)(2,1)S(1)}, bf16[1,256,1024]{2,1,0:T(8,128)(2,1)S(1)}, u32[]{:S(2)}, u32[]{:S(2)}) %collective-permute-start.12) | collective-permute-done | bytes 524320 | tf_op jit(solution)/shard_map/ppermute | solution.py:289
  145.7 1.4 collective-permute-done.14.given
  147.1 1.4 collective-permute-start.15
  148.5 0.7 collective-permute-start.16
  149.2 2.2 %collective-permute-done.15.first = f32[64,256]{1,0:T(8,128)S(1)} collective-permute-done((f32[64,256]{1,0:T(8,128)S(1)}, f32[64,256]{1,0:T(8,128)S(1)}, u32[]{:S(2)}, u32[]{:S(2)}) %collective-permute-start.15) | collective-permute-done | bytes 65568 | tf_op jit(solution)/shard_map/ppermute | solution.py:340
  151.5 1.3 collective-permute-done.16.second
  152.9 1.5 collective-permute-done.18.hidden.up
  154.4 2.5 %collective-permute-start.11 = (f32[4,32,256]{2,1,0:T(8,128)S(1)}, f32[4,32,256]{2,1,0:T(8,128)S(1)}, u32[]{:S(2)}, u32[]{:S(2)}) collective-permute-start(f32[4,32,256]{2,1,0:T(8,128)S(1)} %get-tuple-element.34.hidden), channel_id=1, source_target_pairs={{0,1},{1,0},{2,3},{3,2},{4,5},{5,4},{6,7},{7,6},{8,9},{9,8},{10,11... | collective-permute-start | bytes 393224 | tf_op jit(solution)/shard_map/ppermute | solution.py:324
  157.0 3.7 %collective-permute-done.19.last = f32[32,256]{1,0:T(8,128)S(1)} collective-permute-done((f32[32,256]{1,0:T(8,128)S(1)}, f32[32,256]{1,0:T(8,128)S(1)}, u32[]{:S(2)}, u32[]{:S(2)}) %collective-permute-start.19) | collective-permute-done | bytes 32800 | tf_op jit(solution)/shard_map/ppermute | solution.py:346
  160.7 1.9 %collective-permute-start.20 = (f32[3,32,256]{2,1,0:T(8,128)S(1)}, f32[3,32,256]{2,1,0:T(8,128)S(1)}, u32[]{:S(2)}, u32[]{:S(2)}) collective-permute-start(f32[3,32,256]{2,1,0:T(8,128)S(1)} %shard_map.31), channel_id=1, source_target_pairs={{0,8},{8,0},{16,24},{24,16},{32,40},{40,32},{48,56},{56,48},{64,72... | collective-permute-start | bytes 294920 | tf_op jit(solution)/shard_map/ppermute | solution.py:289
  163.6 0.7 shard_map.32
  (26 shorter events, 2.4 us)
Async XLA Ops:
  2.2 14.3 %collective-permute-start = (bf16[8,256,1024]{2,1,0:T(8,128)(2,1)S(1)}, bf16[8,256,1024]{2,1,0:T(8,128)(2,1)S(1)}, u32[]{:S(2)}, u32[]{:S(2)}) collective-permute-start(bf16[8,256,1024]{2,1,0:T(8,128)(2,1)S(1)} %shard_map.17.refs_0_), channel_id=1, source_target_pairs={{0,8},{8,0},{16,24},{24,16},{32,40},{40,32},{48,56},{56,48},{64,72... | collective-permute-start | bytes 12582920 | tf_op jit(solution)/shard_map/ppermute | solution.py:289
  2.3 105.7 %collective-permute-start.4 = (bf16[8,256,1024]{2,1,0:T(8,128)(2,1)S(1)}, bf16[8,256,1024]{2,1,0:T(8,128)(2,1)S(1)}, u32[]{:S(2)}, u32[]{:S(2)}) collective-permute-start(bf16[8,256,1024]{2,1,0:T(8,128)(2,1)S(1)} %shard_map.17.refs_0_), channel_id=1, source_target_pairs={{0,248},{8,16},{16,8},{24,32},{32,24},{40,48},{48,40},{56,64},{64,... | collective-permute-start | bytes 12582920 | tf_op jit(solution)/shard_map/ppermute | solution.py:289
  12.3 95.7 %collective-permute-start.5 = (bf16[7,256,1024]{2,1,0:T(8,128)(2,1)S(1)}, bf16[7,256,1024]{2,1,0:T(8,128)(2,1)S(1)}, u32[]{:S(2)}, u32[]{:S(2)}) collective-permute-start(bf16[7,256,1024]{2,1,0:T(8,128)(2,1)S(1)} %shard_map.19.own0), channel_id=1, source_target_pairs={{0,16},{8,248},{16,32},{24,8},{32,48},{40,24},{48,64},{56,40},{64,... | collective-permute-start | bytes 11010056 | tf_op jit(solution)/shard_map/ppermute | solution.py:289
  12.4 127.1 %collective-permute-start.13 = (bf16[7,256,1024]{2,1,0:T(8,128)(2,1)S(1)}, bf16[7,256,1024]{2,1,0:T(8,128)(2,1)S(1)}, u32[]{:S(2)}, u32[]{:S(2)}) collective-permute-start(bf16[7,256,1024]{2,1,0:T(8,128)(2,1)S(1)} %shard_map.19.own0), channel_id=1, source_target_pairs={{0,240},{8,24},{16,0},{24,40},{32,16},{40,56},{48,32},{56,72},{64,... | collective-permute-start | bytes 11010056 | tf_op jit(solution)/shard_map/ppermute | solution.py:289
  21.5 7.9 %collective-permute-start.1 = (f32[3,64,256]{2,1,0:T(8,128)S(1)}, f32[3,64,256]{2,1,0:T(8,128)S(1)}, u32[]{:S(2)}, u32[]{:S(2)}) collective-permute-start(f32[3,64,256]{2,1,0:T(8,128)S(1)} %get-tuple-element.24), channel_id=1, source_target_pairs={{0,2},{1,3},{2,4},{3,5},{4,6},{5,7},{6,0},{7,1},{8,10},{9,11},{10,... | collective-permute-start | bytes 589832 | tf_op jit(solution)/shard_map/ppermute | solution.py:284
  22.9 85.2 %collective-permute-start.6 = (bf16[1,256,1024]{2,1,0:T(8,128)(2,1)S(1)}, bf16[1,256,1024]{2,1,0:T(8,128)(2,1)S(1)}, u32[]{:S(2)}, u32[]{:S(2)}) collective-permute-start(bf16[1,256,1024]{2,1,0:T(8,128)(2,1)S(1)} %shard_map.18.refs_0_.own1), channel_id=1, source_target_pairs={{0,16},{8,248},{16,32},{24,8},{32,48},{40,24},{48,64},{56,40},{64,... | collective-permute-start | bytes 1572872 | tf_op jit(solution)/shard_map/ppermute | solution.py:289
  29.4 7.2 %collective-permute-start.2 = (f32[3,64,256]{2,1,0:T(8,128)S(1)}, f32[3,64,256]{2,1,0:T(8,128)S(1)}, u32[]{:S(2)}, u32[]{:S(2)}) collective-permute-start(f32[3,64,256]{2,1,0:T(8,128)S(1)} %get-tuple-element.25), channel_id=1, source_target_pairs={{0,4},{1,5},{2,6},{3,7},{4,0},{5,1},{6,2},{7,3},{8,12},{9,13},{10,... | collective-permute-start | bytes 589832 | tf_op jit(solution)/shard_map/ppermute | solution.py:284
  36.5 6.8 %collective-permute-start.3 = (f32[3,64,256]{2,1,0:T(8,128)S(1)}, f32[3,64,256]{2,1,0:T(8,128)S(1)}, u32[]{:S(2)}, u32[]{:S(2)}) collective-permute-start(f32[3,64,256]{2,1,0:T(8,128)S(1)} %get-tuple-element.26), channel_id=1, source_target_pairs={{0,6},{1,7},{2,0},{3,1},{4,2},{5,3},{6,4},{7,5},{8,14},{9,15},{10,... | collective-permute-start | bytes 589832 | tf_op jit(solution)/shard_map/ppermute | solution.py:284
  114.1 6.5 %collective-permute-start.7 = (f32[4,64,256]{2,1,0:T(8,128)S(1)}, f32[4,64,256]{2,1,0:T(8,128)S(1)}, u32[]{:S(2)}, u32[]{:S(2)}) collective-permute-start(f32[4,64,256]{2,1,0:T(8,128)S(1)} %get-tuple-element.28), channel_id=1, source_target_pairs={{0,2},{1,3},{2,4},{3,5},{4,6},{5,7},{6,0},{7,1},{8,10},{9,11},{10,... | collective-permute-start | bytes 786440 | tf_op jit(solution)/shard_map/ppermute | solution.py:284
  115.5 7.9 %collective-permute-start.8 = (f32[4,64,256]{2,1,0:T(8,128)S(1)}, f32[4,64,256]{2,1,0:T(8,128)S(1)}, u32[]{:S(2)}, u32[]{:S(2)}) collective-permute-start(f32[4,64,256]{2,1,0:T(8,128)S(1)} %get-tuple-element.29), channel_id=1, source_target_pairs={{0,4},{1,5},{2,6},{3,7},{4,0},{5,1},{6,2},{7,3},{8,12},{9,13},{10,... | collective-permute-start | bytes 786440 | tf_op jit(solution)/shard_map/ppermute | solution.py:284
  116.1 9.4 %collective-permute-start.9 = (f32[4,64,256]{2,1,0:T(8,128)S(1)}, f32[4,64,256]{2,1,0:T(8,128)S(1)}, u32[]{:S(2)}, u32[]{:S(2)}) collective-permute-start(f32[4,64,256]{2,1,0:T(8,128)S(1)} %get-tuple-element.30), channel_id=1, source_target_pairs={{0,6},{1,7},{2,0},{3,1},{4,2},{5,3},{6,4},{7,5},{8,14},{9,15},{10,... | collective-permute-start | bytes 786440 | tf_op jit(solution)/shard_map/ppermute | solution.py:284
  117.2 27.9 %collective-permute-start.12 = (bf16[1,256,1024]{2,1,0:T(8,128)(2,1)S(1)}, bf16[1,256,1024]{2,1,0:T(8,128)(2,1)S(1)}, u32[]{:S(2)}, u32[]{:S(2)}) collective-permute-start(bf16[1,256,1024]{2,1,0:T(8,128)(2,1)S(1)} %shard_map.18.refs_0_.own1), channel_id=1, source_target_pairs={{0,240},{8,24},{16,0},{24,40},{32,16},{40,56},{48,32},{56,72},{64,... | collective-permute-start | bytes 1572872 | tf_op jit(solution)/shard_map/ppermute | solution.py:289
  125.6 16.3 %collective-permute-start.10 = (f32[4,64,256]{2,1,0:T(8,128)S(1)}, f32[4,64,256]{2,1,0:T(8,128)S(1)}, u32[]{:S(2)}, u32[]{:S(2)}) collective-permute-start(f32[4,64,256]{2,1,0:T(8,128)S(1)} %get-tuple-element.32), channel_id=1, source_target_pairs={{0,8},{8,0},{16,24},{24,16},{32,40},{40,32},{48,56},{56,48},{64,72... | collective-permute-start | bytes 786440 | tf_op jit(solution)/shard_map/ppermute | solution.py:289
  145.5 1.6 collective-permute-start.14
  145.6 8.7 %collective-permute-start.18 = (f32[4,32,256]{2,1,0:T(8,128)S(1)}, f32[4,32,256]{2,1,0:T(8,128)S(1)}, u32[]{:S(2)}, u32[]{:S(2)}) collective-permute-start(f32[4,32,256]{2,1,0:T(8,128)S(1)} %get-tuple-element.40), channel_id=1, source_target_pairs={{0,16},{1,24},{2,18},{3,26},{4,20},{5,28},{6,22},{7,30},{8,25},{9,... | collective-permute-start | bytes 393224 | tf_op jit(solution)/shard_map/ppermute | solution.py:344
  147.1 4.4 %collective-permute-start.15 = (f32[64,256]{1,0:T(8,128)S(1)}, f32[64,256]{1,0:T(8,128)S(1)}, u32[]{:S(2)}, u32[]{:S(2)}) collective-permute-start(f32[64,256]{1,0:T(8,128)S(1)} %get-tuple-element.36), channel_id=1, source_target_pairs={{0,2},{1,3},{2,4},{3,5},{4,6},{5,7},{6,0},{7,1},{8,12},{9,13},{10,... | collective-permute-start | bytes 196616 | tf_op jit(solution)/shard_map/ppermute | solution.py:340
  148.5 4.3 %collective-permute-start.16 = (f32[64,256]{1,0:T(8,128)S(1)}, f32[64,256]{1,0:T(8,128)S(1)}, u32[]{:S(2)}, u32[]{:S(2)}) collective-permute-start(f32[64,256]{1,0:T(8,128)S(1)} %get-tuple-element.37), channel_id=1, source_target_pairs={{0,6},{1,7},{2,0},{3,1},{4,2},{5,3},{6,4},{7,5},{8,14},{9,15},{10,... | collective-permute-start | bytes 196616 | tf_op jit(solution)/shard_map/ppermute | solution.py:340
  152.8 1.6 collective-permute-start.17
  154.3 6.3 %collective-permute-start.19 = (f32[32,256]{1,0:T(8,128)S(1)}, f32[32,256]{1,0:T(8,128)S(1)}, u32[]{:S(2)}, u32[]{:S(2)}) collective-permute-start(f32[32,256]{1,0:T(8,128)S(1)} %shard_map.30), channel_id=1, source_target_pairs={{0,16},{1,24},{2,18},{3,26},{4,20},{5,28},{6,22},{7,30},{8,25},{9,... | collective-permute-start | bytes 98312 | tf_op jit(solution)/shard_map/ppermute | solution.py:346
  154.4 8.5 %collective-permute-start.11 = (f32[4,32,256]{2,1,0:T(8,128)S(1)}, f32[4,32,256]{2,1,0:T(8,128)S(1)}, u32[]{:S(2)}, u32[]{:S(2)}) collective-permute-start(f32[4,32,256]{2,1,0:T(8,128)S(1)} %get-tuple-element.34.hidden), channel_id=1, source_target_pairs={{0,1},{1,0},{2,3},{3,2},{4,5},{5,4},{6,7},{7,6},{8,9},{9,8},{10,11... | collective-permute-start | bytes 393224 | tf_op jit(solution)/shard_map/ppermute | solution.py:324
  160.7 2.9 %collective-permute-start.20 = (f32[3,32,256]{2,1,0:T(8,128)S(1)}, f32[3,32,256]{2,1,0:T(8,128)S(1)}, u32[]{:S(2)}, u32[]{:S(2)}) collective-permute-start(f32[3,32,256]{2,1,0:T(8,128)S(1)} %shard_map.31), channel_id=1, source_target_pairs={{0,8},{8,0},{16,24},{24,16},{32,40},{40,32},{48,56},{56,48},{64,72... | collective-permute-start | bytes 294920 | tf_op jit(solution)/shard_map/ppermute | solution.py:289

commit v6 on v5

--- a/solution.py
+++ b/solution.py
@@ -46,6 +46,21 @@
         for a in range(8):
             block = (b - core + 2 + (core ^ a % 2)) % COUNT
             pairs.append((b * 8 + a, block * 8 + a // 2 * 2 + core))
+    return pairs
+
+
+def to_upper_even(flip):
+    pairs = []
+    for b in range(COUNT):
+        core = b % 2
+        for a in range(8):
+            if a % 2 == core ^ flip:
+                target = (b - core + 2) % COUNT * 8 + a // 2 * 2 + core
+            elif core == 0:
+                target = (b + 1) * 8 + a
+            else:
+                target = b * 8 + (a + 2) % 8
+            pairs.append((b * 8 + a, target))
     return pairs
 
 
@@ -251,26 +266,24 @@
     out[...] = a[...] + b[...]
 
 
-def hand_kernel(last, up, give):
+def hand_kernel(up, give):
     def even():
         give[0] = up[1]
         give[1] = up[3]
-        give[2] = jnp.zeros((32, ROWS), F32)
 
     def odd():
         give[0] = up[0]
         give[1] = up[2]
-        give[2] = last[...]
 
     by_parity(even, odd)
 
 
-def finish_kernel(stay, come, last, up, given, out):
+def finish_kernel(stay, come, up, given, first, second, out):
     def even():
         out[0] = stay[0] + come[0]
         out[1] = (stay[1] + come[1]) + (up[0] + given[0])
         out[2] = (stay[2] + come[2]) + (up[2] + given[1])
-        out[3] = last[...] + given[2]
+        out[3] = first[...] + second[...]
 
     def odd():
         out[0:2] = stay[0:2] + come[0:2]
@@ -343,9 +356,9 @@
     keep, give = call(collect_kernel, [f32(32, ROWS)] * 2, parts[0], *moved)
     up = lax.ppermute(up, ("blk", "aux"), to_upper_chip())
     last = call(join_kernel, f32(32, ROWS), keep, send(give, TO_MATE), hidden=(up,))
-    last = lax.ppermute(last, ("blk", "aux"), to_upper_chip())
-    given = send(call(hand_kernel, f32(3, 32, ROWS), last, up), TO_MATE)
-    out = call(finish_kernel, f32(4, 32, ROWS), stay, come, last, up, given)
+    last = [lax.ppermute(last, ("blk", "aux"), to_upper_even(flip)) for flip in (1, 0)]
+    given = send(call(hand_kernel, f32(2, 32, ROWS), up), TO_MATE)
+    out = call(finish_kernel, f32(4, 32, ROWS), stay, come, up, given, *last)
     return out.transpose(2, 0, 1)
 
 

time: 166 us -> 164 us (0.988)
    ppermute x2, waiting for transfers between devices: 3.52 us -> 0.79 us  [local(): lax.ppermute(part, ('blk', 'aux'), by_core(even, odd))]
    ppermute x1 -> x2, waiting for transfers between devices: 3.69 us -> 5.42 us  [local(): lax.ppermute(last, ('blk', 'aux'), to_upper_even(flip))]
  transfers between devices with their start and end apart: 21 -> 22, of which waited for: 16 -> 14; matrix products, arithmetic and copies ran while one was open for 0% -> 0% of each run, Pallas kernels for 10% -> 10%
where the time goes in v6:
time: 164 us
  waiting for transfers between devices  120 us (73%)
  starting transfers between devices  23.4 us (14%)
  Pallas kernels  20 us (12%)
    ppermute x10, waiting for transfers between devices, send(): return lax.ppermute(value, 'blk', pairs)  83 us
    ppermute x6, waiting for transfers between devices, sum_along_y(): lax.ppermute(parts[d], 'aux', along_y(d))  27.5 us
    pallas_call x16, Pallas kernels, call(): pl.pallas_call(kernel, out_shape=out_shape, in_specs=(specs or [VMEM] * l...  20 us
    ppermute x10, starting transfers between devices, send(): return lax.ppermute(value, 'blk', pairs)  12.6 us
    ppermute x6, starting transfers between devices, sum_along_y(): lax.ppermute(parts[d], 'aux', along_y(d))  5.71 us
    ppermute x2, waiting for transfers between devices, local(): lax.ppermute(last, ('blk', 'aux'), to_upper_even(flip))  5.42 us
  transfers between devices with their start and end apart: 22, of which 14 were waited for; matrix products, arithmetic and copies ran while one was open for 0% of the time, Pallas kernels for 10%

profile of v6, /device:TPU:16, one launch (start us, length us, event | category | flops | bytes accessed | tf_op | source)
XLA Modules:
  0.0 163.7 jit_solution(15385519874880212406)
XLA Ops:
  0.0 2.2 %shard_map.17.refs_0_ = bf16[8,256,1024]{2,1,0:T(8,128)(2,1)S(1)} custom-call(bf16[16,256,1024]{2,1,0:T(8,128)(2,1)} %factors.5), custom_call_target="tpu_custom_call" | custom-call | bytes 8388608 | tf_op jit(solution)/shard_map/pallas_call | solution.py:78
  2.3 6.9 %collective-permute-start.4 = (bf16[8,256,1024]{2,1,0:T(8,128)(2,1)S(1)}, bf16[8,256,1024]{2,1,0:T(8,128)(2,1)S(1)}, u32[]{:S(2)}, u32[]{:S(2)}) collective-permute-start(bf16[8,256,1024]{2,1,0:T(8,128)(2,1)S(1)} %shard_map.17.refs_0_), channel_id=1, source_target_pairs={{0,248},{8,16},{16,8},{24,32},{32,24},{40,48},{48,40},{56,64},{64,... | collective-permute-start | bytes 12582920 | tf_op jit(solution)/shard_map/ppermute | solution.py:302
  9.2 1.0 shard_map.18.refs_0_.own1
  10.3 2.1 %shard_map.19.own0 = bf16[7,256,1024]{2,1,0:T(8,128)(2,1)S(1)} custom-call(bf16[16,256,1024]{2,1,0:T(8,128)(2,1)} %factors.5, bf16[1,256,1024]{2,1,0:T(8,128)(2,1)S(1)} %shard_map.18.refs_0_.own1), custom_call_target="tpu_custom_call" | custom-call | bytes 8388608 | tf_op jit(solution)/shard_map/pallas_call | solution.py:78
  12.4 4.1 %collective-permute-start.15 = (bf16[7,256,1024]{2,1,0:T(8,128)(2,1)S(1)}, bf16[7,256,1024]{2,1,0:T(8,128)(2,1)S(1)}, u32[]{:S(2)}, u32[]{:S(2)}) collective-permute-start(bf16[7,256,1024]{2,1,0:T(8,128)(2,1)S(1)} %shard_map.19.own0), channel_id=1, source_target_pairs={{0,240},{8,24},{16,0},{24,40},{32,16},{40,56},{48,32},{56,72},{64,... | collective-permute-start | bytes 11010056 | tf_op jit(solution)/shard_map/ppermute | solution.py:302
  16.6 5.0 %shard_map.20 = (f32[3,64,256]{2,1,0:T(8,128)S(1)}, f32[3,64,256]{2,1,0:T(8,128)S(1)}, f32[3,64,256]{2,1,0:T(8,128)S(1)}, f32[3,64,256]{2,1,0:T(8,128)S(1)}) custom-call(bf16[7,256,1024]{2,1,0:T(8,128)(2,1)S(1)} %shard_map.19.own0, bf16[1,256,1024]{2,1,0:T(8,128)(2,1)S(1)} %shard_map.18.refs_0_.own1, bf16[8,256,1024]{2,1,0:T(8,128)(2,1)S(1)} %collective-permute-done.mate0), custom_call_target="tpu_custom_call" | custom-call | flops 3221225472 | bytes 8388608 | tf_op jit(solution)/shard_map/pallas_call | solution.py:78
  21.5 1.4 collective-permute-start.1
  22.9 6.5 %collective-permute-done.1.b = f32[3,64,256]{2,1,0:T(8,128)S(1)} collective-permute-done((f32[3,64,256]{2,1,0:T(8,128)S(1)}, f32[3,64,256]{2,1,0:T(8,128)S(1)}, u32[]{:S(2)}, u32[]{:S(2)}) %collective-permute-start.1) | collective-permute-done | bytes 196640 | tf_op jit(solution)/shard_map/ppermute | solution.py:297
  29.5 7.0 %collective-permute-done.2.c = f32[3,64,256]{2,1,0:T(8,128)S(1)} collective-permute-done((f32[3,64,256]{2,1,0:T(8,128)S(1)}, f32[3,64,256]{2,1,0:T(8,128)S(1)}, u32[]{:S(2)}, u32[]{:S(2)}) %collective-permute-start.2) | collective-permute-done | bytes 196640 | tf_op jit(solution)/shard_map/ppermute | solution.py:297
  36.5 1.1 collective-permute-start.3
  37.7 5.6 %collective-permute-done.3.d = f32[3,64,256]{2,1,0:T(8,128)S(1)} collective-permute-done((f32[3,64,256]{2,1,0:T(8,128)S(1)}, f32[3,64,256]{2,1,0:T(8,128)S(1)}, u32[]{:S(2)}, u32[]{:S(2)}) %collective-permute-start.3) | collective-permute-done | bytes 196640 | tf_op jit(solution)/shard_map/ppermute | solution.py:297
  43.4 64.7 %collective-permute-done.6.far1 = bf16[1,256,1024]{2,1,0:T(8,128)(2,1)S(1)} collective-permute-done((bf16[1,256,1024]{2,1,0:T(8,128)(2,1)S(1)}, bf16[1,256,1024]{2,1,0:T(8,128)(2,1)S(1)}, u32[]{:S(2)}, u32[]{:S(2)}) %collective-permute-start.6) | collective-permute-done | bytes 524320 | tf_op jit(solution)/shard_map/ppermute | solution.py:302
  108.0 6.1 %shard_map.22 = (f32[4,64,256]{2,1,0:T(8,128)S(1)}, f32[4,64,256]{2,1,0:T(8,128)S(1)}, f32[4,64,256]{2,1,0:T(8,128)S(1)}, f32[4,64,256]{2,1,0:T(8,128)S(1)}) custom-call(bf16[7,256,1024]{2,1,0:T(8,128)(2,1)S(1)} %shard_map.19.own0, bf16[1,256,1024]{2,1,0:T(8,128)(2,1)S(1)} %shard_map.18.refs_0_.own1, bf16[8,256,1024]{2,1,0:T(8,128)(2,1)S(1)} %collective-permute-done.mate0, ...), custom_call_target="tpu_custom_call" | custom-call | flops 4294967296 | bytes 16777216 | tf_op jit(solution)/shard_map/pallas_call | solution.py:78
  114.1 1.4 collective-permute-start.7
  115.5 0.6 collective-permute-start.8
  116.1 1.1 collective-permute-start.9
  117.2 3.4 %collective-permute-done.7.b = f32[4,64,256]{2,1,0:T(8,128)S(1)} collective-permute-done((f32[4,64,256]{2,1,0:T(8,128)S(1)}, f32[4,64,256]{2,1,0:T(8,128)S(1)}, u32[]{:S(2)}, u32[]{:S(2)}) %collective-permute-start.7) | collective-permute-done | bytes 262176 | tf_op jit(solution)/shard_map/ppermute | solution.py:297
  120.6 2.8 %collective-permute-done.8.c = f32[4,64,256]{2,1,0:T(8,128)S(1)} collective-permute-done((f32[4,64,256]{2,1,0:T(8,128)S(1)}, f32[4,64,256]{2,1,0:T(8,128)S(1)}, u32[]{:S(2)}, u32[]{:S(2)}) %collective-permute-start.8) | collective-permute-done | bytes 262176 | tf_op jit(solution)/shard_map/ppermute | solution.py:297
  123.4 2.1 %collective-permute-done.9.d = f32[4,64,256]{2,1,0:T(8,128)S(1)} collective-permute-done((f32[4,64,256]{2,1,0:T(8,128)S(1)}, f32[4,64,256]{2,1,0:T(8,128)S(1)}, u32[]{:S(2)}, u32[]{:S(2)}) %collective-permute-start.9) | collective-permute-done | bytes 262176 | tf_op jit(solution)/shard_map/ppermute | solution.py:297
  125.7 13.8 %collective-permute-done.15.far0 = bf16[7,256,1024]{2,1,0:T(8,128)(2,1)S(1)} collective-permute-done((bf16[7,256,1024]{2,1,0:T(8,128)(2,1)S(1)}, bf16[7,256,1024]{2,1,0:T(8,128)(2,1)S(1)}, u32[]{:S(2)}, u32[]{:S(2)}) %collective-permute-start.15) | collective-permute-done | bytes 3670048 | tf_op jit(solution)/shard_map/ppermute | solution.py:302
  139.5 2.4 %shard_map.27.early = f32[1,256,256]{2,1,0:T(8,128)S(1)} custom-call(bf16[8,256,1024]{2,1,0:T(8,128)(2,1)S(1)} %collective-permute-done.4.near0, bf16[7,256,1024]{2,1,0:T(8,128)(2,1)S(1)} %collective-permute-done.15.far0), custom_call_target="tpu_custom_call" | custom-call | flops 939524096 | bytes 7864320 | tf_op jit(solution)/shard_map/pallas_call | solution.py:78
  142.0 3.1 %collective-permute-done.14.far1 = bf16[1,256,1024]{2,1,0:T(8,128)(2,1)S(1)} collective-permute-done((bf16[1,256,1024]{2,1,0:T(8,128)(2,1)S(1)}, bf16[1,256,1024]{2,1,0:T(8,128)(2,1)S(1)}, u32[]{:S(2)}, u32[]{:S(2)}) %collective-permute-start.14) | collective-permute-done | bytes 524320 | tf_op jit(solution)/shard_map/ppermute | solution.py:302
  145.7 1.4 collective-permute-done.16.given
  147.1 1.4 collective-permute-start.17
  148.5 0.7 collective-permute-start.18
  149.2 2.7 %collective-permute-start.11 = (f32[4,32,256]{2,1,0:T(8,128)S(1)}, f32[4,32,256]{2,1,0:T(8,128)S(1)}, u32[]{:S(2)}, u32[]{:S(2)}) collective-permute-start(f32[4,32,256]{2,1,0:T(8,128)S(1)} %get-tuple-element.34.hidden), channel_id=1, source_target_pairs={{0,1},{1,0},{2,3},{3,2},{4,5},{5,4},{6,7},{7,6},{8,9},{9,8},{10,11... | collective-permute-start | bytes 393224 | tf_op jit(solution)/shard_map/ppermute | solution.py:337
  152.0 0.8 collective-permute-done.18.second
  152.9 1.6 collective-permute-done.12.up.hidden
  154.4 1.1 collective-permute-start.13
  155.8 1.8 %collective-permute-done.11.come = f32[4,32,256]{2,1,0:T(8,128)S(1)} collective-permute-done((f32[4,32,256]{2,1,0:T(8,128)S(1)}, f32[4,32,256]{2,1,0:T(8,128)S(1)}, u32[]{:S(2)}, u32[]{:S(2)}) %collective-permute-start.11) | collective-permute-done | bytes 131104 | tf_op jit(solution)/shard_map/ppermute | solution.py:337
  157.6 5.4 %collective-permute-done.20.first = f32[32,256]{1,0:T(8,128)S(1)} collective-permute-done((f32[32,256]{1,0:T(8,128)S(1)}, f32[32,256]{1,0:T(8,128)S(1)}, u32[]{:S(2)}, u32[]{:S(2)}) %collective-permute-start.20) | collective-permute-done | bytes 32800 | tf_op jit(solution)/shard_map/ppermute | solution.py:359
  163.0 0.7 shard_map.32
  (28 shorter events, 1.5 us)
Async XLA Ops:
  2.2 14.3 %collective-permute-start = (bf16[8,256,1024]{2,1,0:T(8,128)(2,1)S(1)}, bf16[8,256,1024]{2,1,0:T(8,128)(2,1)S(1)}, u32[]{:S(2)}, u32[]{:S(2)}) collective-permute-start(bf16[8,256,1024]{2,1,0:T(8,128)(2,1)S(1)} %shard_map.17.refs_0_), channel_id=1, source_target_pairs={{0,8},{8,0},{16,24},{24,16},{32,40},{40,32},{48,56},{56,48},{64,72... | collective-permute-start | bytes 12582920 | tf_op jit(solution)/shard_map/ppermute | solution.py:302
  2.3 105.7 %collective-permute-start.4 = (bf16[8,256,1024]{2,1,0:T(8,128)(2,1)S(1)}, bf16[8,256,1024]{2,1,0:T(8,128)(2,1)S(1)}, u32[]{:S(2)}, u32[]{:S(2)}) collective-permute-start(bf16[8,256,1024]{2,1,0:T(8,128)(2,1)S(1)} %shard_map.17.refs_0_), channel_id=1, source_target_pairs={{0,248},{8,16},{16,8},{24,32},{32,24},{40,48},{48,40},{56,64},{64,... | collective-permute-start | bytes 12582920 | tf_op jit(solution)/shard_map/ppermute | solution.py:302
  12.3 95.7 %collective-permute-start.5 = (bf16[7,256,1024]{2,1,0:T(8,128)(2,1)S(1)}, bf16[7,256,1024]{2,1,0:T(8,128)(2,1)S(1)}, u32[]{:S(2)}, u32[]{:S(2)}) collective-permute-start(bf16[7,256,1024]{2,1,0:T(8,128)(2,1)S(1)} %shard_map.19.own0), channel_id=1, source_target_pairs={{0,16},{8,248},{16,32},{24,8},{32,48},{40,24},{48,64},{56,40},{64,... | collective-permute-start | bytes 11010056 | tf_op jit(solution)/shard_map/ppermute | solution.py:302
  12.4 127.1 %collective-permute-start.15 = (bf16[7,256,1024]{2,1,0:T(8,128)(2,1)S(1)}, bf16[7,256,1024]{2,1,0:T(8,128)(2,1)S(1)}, u32[]{:S(2)}, u32[]{:S(2)}) collective-permute-start(bf16[7,256,1024]{2,1,0:T(8,128)(2,1)S(1)} %shard_map.19.own0), channel_id=1, source_target_pairs={{0,240},{8,24},{16,0},{24,40},{32,16},{40,56},{48,32},{56,72},{64,... | collective-permute-start | bytes 11010056 | tf_op jit(solution)/shard_map/ppermute | solution.py:302
  21.5 7.9 %collective-permute-start.1 = (f32[3,64,256]{2,1,0:T(8,128)S(1)}, f32[3,64,256]{2,1,0:T(8,128)S(1)}, u32[]{:S(2)}, u32[]{:S(2)}) collective-permute-start(f32[3,64,256]{2,1,0:T(8,128)S(1)} %get-tuple-element.24), channel_id=1, source_target_pairs={{0,2},{1,3},{2,4},{3,5},{4,6},{5,7},{6,0},{7,1},{8,10},{9,11},{10,... | collective-permute-start | bytes 589832 | tf_op jit(solution)/shard_map/ppermute | solution.py:297
  22.9 85.2 %collective-permute-start.6 = (bf16[1,256,1024]{2,1,0:T(8,128)(2,1)S(1)}, bf16[1,256,1024]{2,1,0:T(8,128)(2,1)S(1)}, u32[]{:S(2)}, u32[]{:S(2)}) collective-permute-start(bf16[1,256,1024]{2,1,0:T(8,128)(2,1)S(1)} %shard_map.18.refs_0_.own1), channel_id=1, source_target_pairs={{0,16},{8,248},{16,32},{24,8},{32,48},{40,24},{48,64},{56,40},{64,... | collective-permute-start | bytes 1572872 | tf_op jit(solution)/shard_map/ppermute | solution.py:302
  29.4 7.2 %collective-permute-start.2 = (f32[3,64,256]{2,1,0:T(8,128)S(1)}, f32[3,64,256]{2,1,0:T(8,128)S(1)}, u32[]{:S(2)}, u32[]{:S(2)}) collective-permute-start(f32[3,64,256]{2,1,0:T(8,128)S(1)} %get-tuple-element.25), channel_id=1, source_target_pairs={{0,4},{1,5},{2,6},{3,7},{4,0},{5,1},{6,2},{7,3},{8,12},{9,13},{10,... | collective-permute-start | bytes 589832 | tf_op jit(solution)/shard_map/ppermute | solution.py:297
  36.5 6.8 %collective-permute-start.3 = (f32[3,64,256]{2,1,0:T(8,128)S(1)}, f32[3,64,256]{2,1,0:T(8,128)S(1)}, u32[]{:S(2)}, u32[]{:S(2)}) collective-permute-start(f32[3,64,256]{2,1,0:T(8,128)S(1)} %get-tuple-element.26), channel_id=1, source_target_pairs={{0,6},{1,7},{2,0},{3,1},{4,2},{5,3},{6,4},{7,5},{8,14},{9,15},{10,... | collective-permute-start | bytes 589832 | tf_op jit(solution)/shard_map/ppermute | solution.py:297
  114.1 6.5 %collective-permute-start.7 = (f32[4,64,256]{2,1,0:T(8,128)S(1)}, f32[4,64,256]{2,1,0:T(8,128)S(1)}, u32[]{:S(2)}, u32[]{:S(2)}) collective-permute-start(f32[4,64,256]{2,1,0:T(8,128)S(1)} %get-tuple-element.28), channel_id=1, source_target_pairs={{0,2},{1,3},{2,4},{3,5},{4,6},{5,7},{6,0},{7,1},{8,10},{9,11},{10,... | collective-permute-start | bytes 786440 | tf_op jit(solution)/shard_map/ppermute | solution.py:297
  115.5 7.9 %collective-permute-start.8 = (f32[4,64,256]{2,1,0:T(8,128)S(1)}, f32[4,64,256]{2,1,0:T(8,128)S(1)}, u32[]{:S(2)}, u32[]{:S(2)}) collective-permute-start(f32[4,64,256]{2,1,0:T(8,128)S(1)} %get-tuple-element.29), channel_id=1, source_target_pairs={{0,4},{1,5},{2,6},{3,7},{4,0},{5,1},{6,2},{7,3},{8,12},{9,13},{10,... | collective-permute-start | bytes 786440 | tf_op jit(solution)/shard_map/ppermute | solution.py:297
  116.1 9.4 %collective-permute-start.9 = (f32[4,64,256]{2,1,0:T(8,128)S(1)}, f32[4,64,256]{2,1,0:T(8,128)S(1)}, u32[]{:S(2)}, u32[]{:S(2)}) collective-permute-start(f32[4,64,256]{2,1,0:T(8,128)S(1)} %get-tuple-element.30), channel_id=1, source_target_pairs={{0,6},{1,7},{2,0},{3,1},{4,2},{5,3},{6,4},{7,5},{8,14},{9,15},{10,... | collective-permute-start | bytes 786440 | tf_op jit(solution)/shard_map/ppermute | solution.py:297
  117.2 27.9 %collective-permute-start.14 = (bf16[1,256,1024]{2,1,0:T(8,128)(2,1)S(1)}, bf16[1,256,1024]{2,1,0:T(8,128)(2,1)S(1)}, u32[]{:S(2)}, u32[]{:S(2)}) collective-permute-start(bf16[1,256,1024]{2,1,0:T(8,128)(2,1)S(1)} %shard_map.18.refs_0_.own1), channel_id=1, source_target_pairs={{0,240},{8,24},{16,0},{24,40},{32,16},{40,56},{48,32},{56,72},{64,... | collective-permute-start | bytes 1572872 | tf_op jit(solution)/shard_map/ppermute | solution.py:302
  125.6 16.3 %collective-permute-start.10 = (f32[4,64,256]{2,1,0:T(8,128)S(1)}, f32[4,64,256]{2,1,0:T(8,128)S(1)}, u32[]{:S(2)}, u32[]{:S(2)}) collective-permute-start(f32[4,64,256]{2,1,0:T(8,128)S(1)} %get-tuple-element.32), channel_id=1, source_target_pairs={{0,8},{8,0},{16,24},{24,16},{32,40},{40,32},{48,56},{56,48},{64,72... | collective-permute-start | bytes 786440 | tf_op jit(solution)/shard_map/ppermute | solution.py:302
  145.5 1.6 collective-permute-start.16
  145.6 8.9 %collective-permute-start.12 = (f32[4,32,256]{2,1,0:T(8,128)S(1)}, f32[4,32,256]{2,1,0:T(8,128)S(1)}, u32[]{:S(2)}, u32[]{:S(2)}) collective-permute-start(f32[4,32,256]{2,1,0:T(8,128)S(1)} %get-tuple-element.35), channel_id=1, source_target_pairs={{0,16},{1,24},{2,18},{3,26},{4,20},{5,28},{6,22},{7,30},{8,25},{9,... | collective-permute-start | bytes 393224 | tf_op jit(solution)/shard_map/ppermute | solution.py:357
  147.1 4.8 %collective-permute-start.17 = (f32[64,256]{1,0:T(8,128)S(1)}, f32[64,256]{1,0:T(8,128)S(1)}, u32[]{:S(2)}, u32[]{:S(2)}) collective-permute-start(f32[64,256]{1,0:T(8,128)S(1)} %get-tuple-element.37), channel_id=1, source_target_pairs={{0,2},{1,3},{2,4},{3,5},{4,6},{5,7},{6,0},{7,1},{8,12},{9,13},{10,... | collective-permute-start | bytes 196616 | tf_op jit(solution)/shard_map/ppermute | solution.py:353
  148.5 4.3 %collective-permute-start.18 = (f32[64,256]{1,0:T(8,128)S(1)}, f32[64,256]{1,0:T(8,128)S(1)}, u32[]{:S(2)}, u32[]{:S(2)}) collective-permute-start(f32[64,256]{1,0:T(8,128)S(1)} %get-tuple-element.38), channel_id=1, source_target_pairs={{0,6},{1,7},{2,0},{3,1},{4,2},{5,3},{6,4},{7,5},{8,14},{9,15},{10,... | collective-permute-start | bytes 196616 | tf_op jit(solution)/shard_map/ppermute | solution.py:353
  149.2 8.3 %collective-permute-start.11 = (f32[4,32,256]{2,1,0:T(8,128)S(1)}, f32[4,32,256]{2,1,0:T(8,128)S(1)}, u32[]{:S(2)}, u32[]{:S(2)}) collective-permute-start(f32[4,32,256]{2,1,0:T(8,128)S(1)} %get-tuple-element.34.hidden), channel_id=1, source_target_pairs={{0,1},{1,0},{2,3},{3,2},{4,5},{5,4},{6,7},{7,6},{8,9},{9,8},{10,11... | collective-permute-start | bytes 393224 | tf_op jit(solution)/shard_map/ppermute | solution.py:337
  152.8 2.8 %collective-permute-start.19 = (f32[32,256]{1,0:T(8,128)S(1)}, f32[32,256]{1,0:T(8,128)S(1)}, u32[]{:S(2)}, u32[]{:S(2)}) collective-permute-start(f32[32,256]{1,0:T(8,128)S(1)} %get-tuple-element.40), channel_id=1, source_target_pairs={{0,8},{8,0},{16,24},{24,16},{32,40},{40,32},{48,56},{56,48},{64,72... | collective-permute-start | bytes 98312 | tf_op jit(solution)/shard_map/ppermute | solution.py:302
  154.4 3.1 %collective-permute-start.13 = (f32[2,32,256]{2,1,0:T(8,128)S(1)}, f32[2,32,256]{2,1,0:T(8,128)S(1)}, u32[]{:S(2)}, u32[]{:S(2)}) collective-permute-start(f32[2,32,256]{2,1,0:T(8,128)S(1)} %shard_map.26), channel_id=1, source_target_pairs={{0,8},{8,0},{16,24},{24,16},{32,40},{40,32},{48,56},{56,48},{64,72... | collective-permute-start | bytes 196616 | tf_op jit(solution)/shard_map/ppermute | solution.py:302
  155.6 7.4 %collective-permute-start.20 = (f32[32,256]{1,0:T(8,128)S(1)}, f32[32,256]{1,0:T(8,128)S(1)}, u32[]{:S(2)}, u32[]{:S(2)}) collective-permute-start(f32[32,256]{1,0:T(8,128)S(1)} %shard_map.31), channel_id=1, source_target_pairs={{0,8},{1,16},{2,10},{3,18},{4,12},{5,20},{6,14},{7,22},{8,17},{9,1... | collective-permute-start | bytes 98312 | tf_op jit(solution)/shard_map/ppermute | solution.py:359
  155.7 7.3 %collective-permute-start.21 = (f32[32,256]{1,0:T(8,128)S(1)}, f32[32,256]{1,0:T(8,128)S(1)}, u32[]{:S(2)}, u32[]{:S(2)}) collective-permute-start(f32[32,256]{1,0:T(8,128)S(1)} %shard_map.31), channel_id=1, source_target_pairs={{0,16},{1,9},{2,18},{3,11},{4,20},{5,13},{6,22},{7,15},{8,10},{9,1... | collective-permute-start | bytes 98312 | tf_op jit(solution)/shard_map/ppermute | solution.py:359

commit v7 on v6

--- a/solution.py
+++ b/solution.py
@@ -49,17 +49,15 @@
     return pairs
 
 
-def to_upper_even(flip):
+def to_upper_even(from_core):
     pairs = []
     for b in range(COUNT):
         core = b % 2
         for a in range(8):
-            if a % 2 == core ^ flip:
-                target = (b - core + 2) % COUNT * 8 + a // 2 * 2 + core
-            elif core == 0:
-                target = (b + 1) * 8 + a
+            if from_core == 0:
+                target = (b + 2) % COUNT * 8 + a if core == 0 else b * 8 + (a + 2) % 8
             else:
-                target = b * 8 + (a + 2) % 8
+                target = (b + 1) % COUNT * 8 + (a ^ 1 if core == 1 else a)
             pairs.append((b * 8 + a, target))
     return pairs
 
@@ -250,14 +248,17 @@
 
 
 def collect_kernel(own, first, second, keep, give):
+    pair = lax.rem(lax.axis_index("aux"), 2)
+    same = pl.ds(pl.multiple_of(32 * pair, 32), 32)
+    cross = pl.ds(pl.multiple_of(32 - 32 * pair, 32), 32)
+
     def even():
-        total = own[...] + first[...] + second[...]
-        keep[...] = total[0:32]
-        give[...] = total[32:64]
+        keep[...] = own[same] + first[same] + second[same]
+        give[...] = own[cross] + first[cross] + second[cross]
 
     def odd():
-        keep[...] = first[32:64]
-        give[...] = first[0:32]
+        keep[...] = first[cross]
+        give[...] = first[same]
 
     by_parity(even, odd)
 
@@ -356,7 +357,7 @@
     keep, give = call(collect_kernel, [f32(32, ROWS)] * 2, parts[0], *moved)
     up = lax.ppermute(up, ("blk", "aux"), to_upper_chip())
     last = call(join_kernel, f32(32, ROWS), keep, send(give, TO_MATE), hidden=(up,))
-    last = [lax.ppermute(last, ("blk", "aux"), to_upper_even(flip)) for flip in (1, 0)]
+    last = [lax.ppermute(last, ("blk", "aux"), to_upper_even(core)) for core in (1, 0)]
     given = send(call(hand_kernel, f32(2, 32, ROWS), up), TO_MATE)
     out = call(finish_kernel, f32(4, 32, ROWS), stay, come, up, given, *last)
     return out.transpose(2, 0, 1)

time: 164 us -> 163 us (level)
  no operation moved by 1% of the time
where the time goes in v7:
time: 163 us
  waiting for transfers between devices  119 us (73%)
  starting transfers between devices  23.4 us (14%)
  Pallas kernels  20 us (12%)
    ppermute x10, waiting for transfers between devices, send(): return lax.ppermute(value, 'blk', pairs)  83 us
    ppermute x6, waiting for transfers between devices, sum_along_y(): lax.ppermute(parts[d], 'aux', along_y(d))  27.5 us
    pallas_call x16, Pallas kernels, call(): pl.pallas_call(kernel, out_shape=out_shape, in_specs=(specs or [VMEM] * l...  20 us
    ppermute x10, starting transfers between devices, send(): return lax.ppermute(value, 'blk', pairs)  12.6 us
    ppermute x6, starting transfers between devices, sum_along_y(): lax.ppermute(parts[d], 'aux', along_y(d))  5.71 us
    ppermute x2, waiting for transfers between devices, local(): lax.ppermute(last, ('blk', 'aux'), to_upper_even(core))  4.78 us
  transfers between devices with their start and end apart: 22, of which 14 were waited for; matrix products, arithmetic and copies ran while one was open for 0% of the time, Pallas kernels for 10%

profile of v7, /device:TPU:16, one launch (start us, length us, event | category | flops | bytes accessed | tf_op | source)
XLA Modules:
  0.0 163.0 jit_solution(1339471089507778749)
XLA Ops:
  0.0 2.2 %shard_map.17.refs_0_ = bf16[8,256,1024]{2,1,0:T(8,128)(2,1)S(1)} custom-call(bf16[16,256,1024]{2,1,0:T(8,128)(2,1)} %factors.5), custom_call_target="tpu_custom_call" | custom-call | bytes 8388608 | tf_op jit(solution)/shard_map/pallas_call | solution.py:76
  2.3 6.9 %collective-permute-start.4 = (bf16[8,256,1024]{2,1,0:T(8,128)(2,1)S(1)}, bf16[8,256,1024]{2,1,0:T(8,128)(2,1)S(1)}, u32[]{:S(2)}, u32[]{:S(2)}) collective-permute-start(bf16[8,256,1024]{2,1,0:T(8,128)(2,1)S(1)} %shard_map.17.refs_0_), channel_id=1, source_target_pairs={{0,248},{8,16},{16,8},{24,32},{32,24},{40,48},{48,40},{56,64},{64,... | collective-permute-start | bytes 12582920 | tf_op jit(solution)/shard_map/ppermute | solution.py:303
  9.2 1.0 shard_map.18.refs_0_.own1
  10.3 2.1 %shard_map.19.own0 = bf16[7,256,1024]{2,1,0:T(8,128)(2,1)S(1)} custom-call(bf16[16,256,1024]{2,1,0:T(8,128)(2,1)} %factors.5, bf16[1,256,1024]{2,1,0:T(8,128)(2,1)S(1)} %shard_map.18.refs_0_.own1), custom_call_target="tpu_custom_call" | custom-call | bytes 8388608 | tf_op jit(solution)/shard_map/pallas_call | solution.py:76
  12.4 4.1 %collective-permute-start.15 = (bf16[7,256,1024]{2,1,0:T(8,128)(2,1)S(1)}, bf16[7,256,1024]{2,1,0:T(8,128)(2,1)S(1)}, u32[]{:S(2)}, u32[]{:S(2)}) collective-permute-start(bf16[7,256,1024]{2,1,0:T(8,128)(2,1)S(1)} %shard_map.19.own0), channel_id=1, source_target_pairs={{0,240},{8,24},{16,0},{24,40},{32,16},{40,56},{48,32},{56,72},{64,... | collective-permute-start | bytes 11010056 | tf_op jit(solution)/shard_map/ppermute | solution.py:303
  16.6 5.0 %shard_map.20 = (f32[3,64,256]{2,1,0:T(8,128)S(1)}, f32[3,64,256]{2,1,0:T(8,128)S(1)}, f32[3,64,256]{2,1,0:T(8,128)S(1)}, f32[3,64,256]{2,1,0:T(8,128)S(1)}) custom-call(bf16[7,256,1024]{2,1,0:T(8,128)(2,1)S(1)} %shard_map.19.own0, bf16[1,256,1024]{2,1,0:T(8,128)(2,1)S(1)} %shard_map.18.refs_0_.own1, bf16[8,256,1024]{2,1,0:T(8,128)(2,1)S(1)} %collective-permute-done.mate0), custom_call_target="tpu_custom_call" | custom-call | flops 3221225472 | bytes 8388608 | tf_op jit(solution)/shard_map/pallas_call | solution.py:76
  21.5 1.4 collective-permute-start.1
  22.9 6.5 %collective-permute-done.1.b = f32[3,64,256]{2,1,0:T(8,128)S(1)} collective-permute-done((f32[3,64,256]{2,1,0:T(8,128)S(1)}, f32[3,64,256]{2,1,0:T(8,128)S(1)}, u32[]{:S(2)}, u32[]{:S(2)}) %collective-permute-start.1) | collective-permute-done | bytes 196640 | tf_op jit(solution)/shard_map/ppermute | solution.py:298
  29.5 7.0 %collective-permute-done.2.c = f32[3,64,256]{2,1,0:T(8,128)S(1)} collective-permute-done((f32[3,64,256]{2,1,0:T(8,128)S(1)}, f32[3,64,256]{2,1,0:T(8,128)S(1)}, u32[]{:S(2)}, u32[]{:S(2)}) %collective-permute-start.2) | collective-permute-done | bytes 196640 | tf_op jit(solution)/shard_map/ppermute | solution.py:298
  36.5 1.1 collective-permute-start.3
  37.7 5.6 %collective-permute-done.3.d = f32[3,64,256]{2,1,0:T(8,128)S(1)} collective-permute-done((f32[3,64,256]{2,1,0:T(8,128)S(1)}, f32[3,64,256]{2,1,0:T(8,128)S(1)}, u32[]{:S(2)}, u32[]{:S(2)}) %collective-permute-start.3) | collective-permute-done | bytes 196640 | tf_op jit(solution)/shard_map/ppermute | solution.py:298
  43.4 64.7 %collective-permute-done.6.far1 = bf16[1,256,1024]{2,1,0:T(8,128)(2,1)S(1)} collective-permute-done((bf16[1,256,1024]{2,1,0:T(8,128)(2,1)S(1)}, bf16[1,256,1024]{2,1,0:T(8,128)(2,1)S(1)}, u32[]{:S(2)}, u32[]{:S(2)}) %collective-permute-start.6) | collective-permute-done | bytes 524320 | tf_op jit(solution)/shard_map/ppermute | solution.py:303
  108.0 6.1 %shard_map.22 = (f32[4,64,256]{2,1,0:T(8,128)S(1)}, f32[4,64,256]{2,1,0:T(8,128)S(1)}, f32[4,64,256]{2,1,0:T(8,128)S(1)}, f32[4,64,256]{2,1,0:T(8,128)S(1)}) custom-call(bf16[7,256,1024]{2,1,0:T(8,128)(2,1)S(1)} %shard_map.19.own0, bf16[1,256,1024]{2,1,0:T(8,128)(2,1)S(1)} %shard_map.18.refs_0_.own1, bf16[8,256,1024]{2,1,0:T(8,128)(2,1)S(1)} %collective-permute-done.mate0, ...), custom_call_target="tpu_custom_call" | custom-call | flops 4294967296 | bytes 16777216 | tf_op jit(solution)/shard_map/pallas_call | solution.py:76
  114.1 1.4 collective-permute-start.7
  115.5 0.6 collective-permute-start.8
  116.1 1.1 collective-permute-start.9
  117.2 3.4 %collective-permute-done.7.b = f32[4,64,256]{2,1,0:T(8,128)S(1)} collective-permute-done((f32[4,64,256]{2,1,0:T(8,128)S(1)}, f32[4,64,256]{2,1,0:T(8,128)S(1)}, u32[]{:S(2)}, u32[]{:S(2)}) %collective-permute-start.7) | collective-permute-done | bytes 262176 | tf_op jit(solution)/shard_map/ppermute | solution.py:298
  120.6 2.8 %collective-permute-done.8.c = f32[4,64,256]{2,1,0:T(8,128)S(1)} collective-permute-done((f32[4,64,256]{2,1,0:T(8,128)S(1)}, f32[4,64,256]{2,1,0:T(8,128)S(1)}, u32[]{:S(2)}, u32[]{:S(2)}) %collective-permute-start.8) | collective-permute-done | bytes 262176 | tf_op jit(solution)/shard_map/ppermute | solution.py:298
  123.4 2.1 %collective-permute-done.9.d = f32[4,64,256]{2,1,0:T(8,128)S(1)} collective-permute-done((f32[4,64,256]{2,1,0:T(8,128)S(1)}, f32[4,64,256]{2,1,0:T(8,128)S(1)}, u32[]{:S(2)}, u32[]{:S(2)}) %collective-permute-start.9) | collective-permute-done | bytes 262176 | tf_op jit(solution)/shard_map/ppermute | solution.py:298
  125.7 13.8 %collective-permute-done.15.far0 = bf16[7,256,1024]{2,1,0:T(8,128)(2,1)S(1)} collective-permute-done((bf16[7,256,1024]{2,1,0:T(8,128)(2,1)S(1)}, bf16[7,256,1024]{2,1,0:T(8,128)(2,1)S(1)}, u32[]{:S(2)}, u32[]{:S(2)}) %collective-permute-start.15) | collective-permute-done | bytes 3670048 | tf_op jit(solution)/shard_map/ppermute | solution.py:303
  139.5 2.4 %shard_map.27.early = f32[1,256,256]{2,1,0:T(8,128)S(1)} custom-call(bf16[8,256,1024]{2,1,0:T(8,128)(2,1)S(1)} %collective-permute-done.4.near0, bf16[7,256,1024]{2,1,0:T(8,128)(2,1)S(1)} %collective-permute-done.15.far0), custom_call_target="tpu_custom_call" | custom-call | flops 939524096 | bytes 7864320 | tf_op jit(solution)/shard_map/pallas_call | solution.py:76
  142.0 3.1 %collective-permute-done.14.far1 = bf16[1,256,1024]{2,1,0:T(8,128)(2,1)S(1)} collective-permute-done((bf16[1,256,1024]{2,1,0:T(8,128)(2,1)S(1)}, bf16[1,256,1024]{2,1,0:T(8,128)(2,1)S(1)}, u32[]{:S(2)}, u32[]{:S(2)}) %collective-permute-start.14) | collective-permute-done | bytes 524320 | tf_op jit(solution)/shard_map/ppermute | solution.py:303
  145.7 1.4 collective-permute-done.16.given
  147.1 1.4 collective-permute-start.17
  148.5 0.7 collective-permute-start.18
  149.2 2.7 %collective-permute-start.11 = (f32[4,32,256]{2,1,0:T(8,128)S(1)}, f32[4,32,256]{2,1,0:T(8,128)S(1)}, u32[]{:S(2)}, u32[]{:S(2)}) collective-permute-start(f32[4,32,256]{2,1,0:T(8,128)S(1)} %get-tuple-element.34.hidden), channel_id=1, source_target_pairs={{0,1},{1,0},{2,3},{3,2},{4,5},{5,4},{6,7},{7,6},{8,9},{9,8},{10,11... | collective-permute-start | bytes 393224 | tf_op jit(solution)/shard_map/ppermute | solution.py:338
  152.0 0.8 collective-permute-done.18.second
  152.9 1.6 collective-permute-done.12.up.hidden
  154.4 1.1 collective-permute-start.13
  155.8 1.8 %collective-permute-done.11.come = f32[4,32,256]{2,1,0:T(8,128)S(1)} collective-permute-done((f32[4,32,256]{2,1,0:T(8,128)S(1)}, f32[4,32,256]{2,1,0:T(8,128)S(1)}, u32[]{:S(2)}, u32[]{:S(2)}) %collective-permute-start.11) | collective-permute-done | bytes 131104 | tf_op jit(solution)/shard_map/ppermute | solution.py:338
  157.6 4.8 %collective-permute-done.20.first = f32[32,256]{1,0:T(8,128)S(1)} collective-permute-done((f32[32,256]{1,0:T(8,128)S(1)}, f32[32,256]{1,0:T(8,128)S(1)}, u32[]{:S(2)}, u32[]{:S(2)}) %collective-permute-start.20) | collective-permute-done | bytes 32800 | tf_op jit(solution)/shard_map/ppermute | solution.py:360
  162.4 0.7 shard_map.32
  (28 shorter events, 1.5 us)
Async XLA Ops:
  2.2 14.3 %collective-permute-start = (bf16[8,256,1024]{2,1,0:T(8,128)(2,1)S(1)}, bf16[8,256,1024]{2,1,0:T(8,128)(2,1)S(1)}, u32[]{:S(2)}, u32[]{:S(2)}) collective-permute-start(bf16[8,256,1024]{2,1,0:T(8,128)(2,1)S(1)} %shard_map.17.refs_0_), channel_id=1, source_target_pairs={{0,8},{8,0},{16,24},{24,16},{32,40},{40,32},{48,56},{56,48},{64,72... | collective-permute-start | bytes 12582920 | tf_op jit(solution)/shard_map/ppermute | solution.py:303
  2.3 105.7 %collective-permute-start.4 = (bf16[8,256,1024]{2,1,0:T(8,128)(2,1)S(1)}, bf16[8,256,1024]{2,1,0:T(8,128)(2,1)S(1)}, u32[]{:S(2)}, u32[]{:S(2)}) collective-permute-start(bf16[8,256,1024]{2,1,0:T(8,128)(2,1)S(1)} %shard_map.17.refs_0_), channel_id=1, source_target_pairs={{0,248},{8,16},{16,8},{24,32},{32,24},{40,48},{48,40},{56,64},{64,... | collective-permute-start | bytes 12582920 | tf_op jit(solution)/shard_map/ppermute | solution.py:303
  12.3 95.7 %collective-permute-start.5 = (bf16[7,256,1024]{2,1,0:T(8,128)(2,1)S(1)}, bf16[7,256,1024]{2,1,0:T(8,128)(2,1)S(1)}, u32[]{:S(2)}, u32[]{:S(2)}) collective-permute-start(bf16[7,256,1024]{2,1,0:T(8,128)(2,1)S(1)} %shard_map.19.own0), channel_id=1, source_target_pairs={{0,16},{8,248},{16,32},{24,8},{32,48},{40,24},{48,64},{56,40},{64,... | collective-permute-start | bytes 11010056 | tf_op jit(solution)/shard_map/ppermute | solution.py:303
  12.4 127.1 %collective-permute-start.15 = (bf16[7,256,1024]{2,1,0:T(8,128)(2,1)S(1)}, bf16[7,256,1024]{2,1,0:T(8,128)(2,1)S(1)}, u32[]{:S(2)}, u32[]{:S(2)}) collective-permute-start(bf16[7,256,1024]{2,1,0:T(8,128)(2,1)S(1)} %shard_map.19.own0), channel_id=1, source_target_pairs={{0,240},{8,24},{16,0},{24,40},{32,16},{40,56},{48,32},{56,72},{64,... | collective-permute-start | bytes 11010056 | tf_op jit(solution)/shard_map/ppermute | solution.py:303
  21.5 7.9 %collective-permute-start.1 = (f32[3,64,256]{2,1,0:T(8,128)S(1)}, f32[3,64,256]{2,1,0:T(8,128)S(1)}, u32[]{:S(2)}, u32[]{:S(2)}) collective-permute-start(f32[3,64,256]{2,1,0:T(8,128)S(1)} %get-tuple-element.24), channel_id=1, source_target_pairs={{0,2},{1,3},{2,4},{3,5},{4,6},{5,7},{6,0},{7,1},{8,10},{9,11},{10,... | collective-permute-start | bytes 589832 | tf_op jit(solution)/shard_map/ppermute | solution.py:298
  22.9 85.2 %collective-permute-start.6 = (bf16[1,256,1024]{2,1,0:T(8,128)(2,1)S(1)}, bf16[1,256,1024]{2,1,0:T(8,128)(2,1)S(1)}, u32[]{:S(2)}, u32[]{:S(2)}) collective-permute-start(bf16[1,256,1024]{2,1,0:T(8,128)(2,1)S(1)} %shard_map.18.refs_0_.own1), channel_id=1, source_target_pairs={{0,16},{8,248},{16,32},{24,8},{32,48},{40,24},{48,64},{56,40},{64,... | collective-permute-start | bytes 1572872 | tf_op jit(solution)/shard_map/ppermute | solution.py:303
  29.4 7.2 %collective-permute-start.2 = (f32[3,64,256]{2,1,0:T(8,128)S(1)}, f32[3,64,256]{2,1,0:T(8,128)S(1)}, u32[]{:S(2)}, u32[]{:S(2)}) collective-permute-start(f32[3,64,256]{2,1,0:T(8,128)S(1)} %get-tuple-element.25), channel_id=1, source_target_pairs={{0,4},{1,5},{2,6},{3,7},{4,0},{5,1},{6,2},{7,3},{8,12},{9,13},{10,... | collective-permute-start | bytes 589832 | tf_op jit(solution)/shard_map/ppermute | solution.py:298
  36.5 6.8 %collective-permute-start.3 = (f32[3,64,256]{2,1,0:T(8,128)S(1)}, f32[3,64,256]{2,1,0:T(8,128)S(1)}, u32[]{:S(2)}, u32[]{:S(2)}) collective-permute-start(f32[3,64,256]{2,1,0:T(8,128)S(1)} %get-tuple-element.26), channel_id=1, source_target_pairs={{0,6},{1,7},{2,0},{3,1},{4,2},{5,3},{6,4},{7,5},{8,14},{9,15},{10,... | collective-permute-start | bytes 589832 | tf_op jit(solution)/shard_map/ppermute | solution.py:298
  114.1 6.5 %collective-permute-start.7 = (f32[4,64,256]{2,1,0:T(8,128)S(1)}, f32[4,64,256]{2,1,0:T(8,128)S(1)}, u32[]{:S(2)}, u32[]{:S(2)}) collective-permute-start(f32[4,64,256]{2,1,0:T(8,128)S(1)} %get-tuple-element.28), channel_id=1, source_target_pairs={{0,2},{1,3},{2,4},{3,5},{4,6},{5,7},{6,0},{7,1},{8,10},{9,11},{10,... | collective-permute-start | bytes 786440 | tf_op jit(solution)/shard_map/ppermute | solution.py:298
  115.5 7.9 %collective-permute-start.8 = (f32[4,64,256]{2,1,0:T(8,128)S(1)}, f32[4,64,256]{2,1,0:T(8,128)S(1)}, u32[]{:S(2)}, u32[]{:S(2)}) collective-permute-start(f32[4,64,256]{2,1,0:T(8,128)S(1)} %get-tuple-element.29), channel_id=1, source_target_pairs={{0,4},{1,5},{2,6},{3,7},{4,0},{5,1},{6,2},{7,3},{8,12},{9,13},{10,... | collective-permute-start | bytes 786440 | tf_op jit(solution)/shard_map/ppermute | solution.py:298
  116.1 9.4 %collective-permute-start.9 = (f32[4,64,256]{2,1,0:T(8,128)S(1)}, f32[4,64,256]{2,1,0:T(8,128)S(1)}, u32[]{:S(2)}, u32[]{:S(2)}) collective-permute-start(f32[4,64,256]{2,1,0:T(8,128)S(1)} %get-tuple-element.30), channel_id=1, source_target_pairs={{0,6},{1,7},{2,0},{3,1},{4,2},{5,3},{6,4},{7,5},{8,14},{9,15},{10,... | collective-permute-start | bytes 786440 | tf_op jit(solution)/shard_map/ppermute | solution.py:298
  117.2 27.9 %collective-permute-start.14 = (bf16[1,256,1024]{2,1,0:T(8,128)(2,1)S(1)}, bf16[1,256,1024]{2,1,0:T(8,128)(2,1)S(1)}, u32[]{:S(2)}, u32[]{:S(2)}) collective-permute-start(bf16[1,256,1024]{2,1,0:T(8,128)(2,1)S(1)} %shard_map.18.refs_0_.own1), channel_id=1, source_target_pairs={{0,240},{8,24},{16,0},{24,40},{32,16},{40,56},{48,32},{56,72},{64,... | collective-permute-start | bytes 1572872 | tf_op jit(solution)/shard_map/ppermute | solution.py:303
  125.6 16.3 %collective-permute-start.10 = (f32[4,64,256]{2,1,0:T(8,128)S(1)}, f32[4,64,256]{2,1,0:T(8,128)S(1)}, u32[]{:S(2)}, u32[]{:S(2)}) collective-permute-start(f32[4,64,256]{2,1,0:T(8,128)S(1)} %get-tuple-element.32), channel_id=1, source_target_pairs={{0,8},{8,0},{16,24},{24,16},{32,40},{40,32},{48,56},{56,48},{64,72... | collective-permute-start | bytes 786440 | tf_op jit(solution)/shard_map/ppermute | solution.py:303
  145.5 1.6 collective-permute-start.16
  145.6 8.9 %collective-permute-start.12 = (f32[4,32,256]{2,1,0:T(8,128)S(1)}, f32[4,32,256]{2,1,0:T(8,128)S(1)}, u32[]{:S(2)}, u32[]{:S(2)}) collective-permute-start(f32[4,32,256]{2,1,0:T(8,128)S(1)} %get-tuple-element.35), channel_id=1, source_target_pairs={{0,16},{1,24},{2,18},{3,26},{4,20},{5,28},{6,22},{7,30},{8,25},{9,... | collective-permute-start | bytes 393224 | tf_op jit(solution)/shard_map/ppermute | solution.py:358
  147.1 4.8 %collective-permute-start.17 = (f32[64,256]{1,0:T(8,128)S(1)}, f32[64,256]{1,0:T(8,128)S(1)}, u32[]{:S(2)}, u32[]{:S(2)}) collective-permute-start(f32[64,256]{1,0:T(8,128)S(1)} %get-tuple-element.37), channel_id=1, source_target_pairs={{0,2},{1,3},{2,4},{3,5},{4,6},{5,7},{6,0},{7,1},{8,12},{9,13},{10,... | collective-permute-start | bytes 196616 | tf_op jit(solution)/shard_map/ppermute | solution.py:354
  148.5 4.3 %collective-permute-start.18 = (f32[64,256]{1,0:T(8,128)S(1)}, f32[64,256]{1,0:T(8,128)S(1)}, u32[]{:S(2)}, u32[]{:S(2)}) collective-permute-start(f32[64,256]{1,0:T(8,128)S(1)} %get-tuple-element.38), channel_id=1, source_target_pairs={{0,6},{1,7},{2,0},{3,1},{4,2},{5,3},{6,4},{7,5},{8,14},{9,15},{10,... | collective-permute-start | bytes 196616 | tf_op jit(solution)/shard_map/ppermute | solution.py:354
  149.2 8.3 %collective-permute-start.11 = (f32[4,32,256]{2,1,0:T(8,128)S(1)}, f32[4,32,256]{2,1,0:T(8,128)S(1)}, u32[]{:S(2)}, u32[]{:S(2)}) collective-permute-start(f32[4,32,256]{2,1,0:T(8,128)S(1)} %get-tuple-element.34.hidden), channel_id=1, source_target_pairs={{0,1},{1,0},{2,3},{3,2},{4,5},{5,4},{6,7},{7,6},{8,9},{9,8},{10,11... | collective-permute-start | bytes 393224 | tf_op jit(solution)/shard_map/ppermute | solution.py:338
  152.8 2.8 %collective-permute-start.19 = (f32[32,256]{1,0:T(8,128)S(1)}, f32[32,256]{1,0:T(8,128)S(1)}, u32[]{:S(2)}, u32[]{:S(2)}) collective-permute-start(f32[32,256]{1,0:T(8,128)S(1)} %get-tuple-element.40), channel_id=1, source_target_pairs={{0,8},{8,0},{16,24},{24,16},{32,40},{40,32},{48,56},{56,48},{64,72... | collective-permute-start | bytes 98312 | tf_op jit(solution)/shard_map/ppermute | solution.py:303
  154.4 3.1 %collective-permute-start.13 = (f32[2,32,256]{2,1,0:T(8,128)S(1)}, f32[2,32,256]{2,1,0:T(8,128)S(1)}, u32[]{:S(2)}, u32[]{:S(2)}) collective-permute-start(f32[2,32,256]{2,1,0:T(8,128)S(1)} %shard_map.26), channel_id=1, source_target_pairs={{0,8},{8,0},{16,24},{24,16},{32,40},{40,32},{48,56},{56,48},{64,72... | collective-permute-start | bytes 196616 | tf_op jit(solution)/shard_map/ppermute | solution.py:303
  155.6 6.8 %collective-permute-start.20 = (f32[32,256]{1,0:T(8,128)S(1)}, f32[32,256]{1,0:T(8,128)S(1)}, u32[]{:S(2)}, u32[]{:S(2)}) collective-permute-start(f32[32,256]{1,0:T(8,128)S(1)} %shard_map.31), channel_id=1, source_target_pairs={{0,8},{1,9},{2,10},{3,11},{4,12},{5,13},{6,14},{7,15},{8,17},{9,16... | collective-permute-start | bytes 98312 | tf_op jit(solution)/shard_map/ppermute | solution.py:360
  155.7 6.7 %collective-permute-start.21 = (f32[32,256]{1,0:T(8,128)S(1)}, f32[32,256]{1,0:T(8,128)S(1)}, u32[]{:S(2)}, u32[]{:S(2)}) collective-permute-start(f32[32,256]{1,0:T(8,128)S(1)} %shard_map.31), channel_id=1, source_target_pairs={{0,16},{1,17},{2,18},{3,19},{4,20},{5,21},{6,22},{7,23},{8,10},{9,... | collective-permute-start | bytes 98312 | tf_op jit(solution)/shard_map/ppermute | solution.py:360

commit v8 on v7

--- a/solution.py
+++ b/solution.py
@@ -267,7 +267,7 @@
     out[...] = a[...] + b[...]
 
 
-def hand_kernel(up, give):
+def hand_kernel(up, hidden, give):
     def even():
         give[0] = up[1]
         give[1] = up[3]
@@ -356,9 +356,9 @@
     ]
     keep, give = call(collect_kernel, [f32(32, ROWS)] * 2, parts[0], *moved)
     up = lax.ppermute(up, ("blk", "aux"), to_upper_chip())
-    last = call(join_kernel, f32(32, ROWS), keep, send(give, TO_MATE), hidden=(up,))
-    last = [lax.ppermute(last, ("blk", "aux"), to_upper_even(core)) for core in (1, 0)]
-    given = send(call(hand_kernel, f32(2, 32, ROWS), up), TO_MATE)
+    joined = call(join_kernel, f32(32, ROWS), keep, send(give, TO_MATE), hidden=(up,))
+    last = [lax.ppermute(joined, ("blk", "aux"), to_upper_even(core)) for core in (1, 0)]
+    given = send(call(hand_kernel, f32(2, 32, ROWS), up, hidden=(joined,)), TO_MATE)
     out = call(finish_kernel, f32(4, 32, ROWS), stay, come, up, given, *last)
     return out.transpose(2, 0, 1)
 

time: 163 us -> 163 us (level)
  no operation moved by 1% of the time
where the time goes in v8:
time: 163 us
  waiting for transfers between devices  120 us (74%)
  starting transfers between devices  23.4 us (14%)
  Pallas kernels  20 us (12%)
    ppermute x10, waiting for transfers between devices, send(): return lax.ppermute(value, 'blk', pairs)  83 us
    ppermute x6, waiting for transfers between devices, sum_along_y(): lax.ppermute(parts[d], 'aux', along_y(d))  27.5 us
    pallas_call x16, Pallas kernels, call(): pl.pallas_call(kernel, out_shape=out_shape, in_specs=(specs or [VMEM] * l...  20 us
    ppermute x10, starting transfers between devices, send(): return lax.ppermute(value, 'blk', pairs)  12.7 us
    ppermute x6, starting transfers between devices, sum_along_y(): lax.ppermute(parts[d], 'aux', along_y(d))  5.71 us
    ppermute x2, waiting for transfers between devices, local(): lax.ppermute(joined, ('blk', 'aux'), to_upper_even(core))  5.07 us
  transfers between devices with their start and end apart: 22, of which 14 were waited for; matrix products, arithmetic and copies ran while one was open for 0% of the time, Pallas kernels for 10%

profile of v8, /device:TPU:16, one launch (start us, length us, event | category | flops | bytes accessed | tf_op | source)
XLA Modules:
  0.0 163.3 jit_solution(15733031397628480202)
XLA Ops:
  0.0 2.2 %shard_map.17.refs_0_ = bf16[8,256,1024]{2,1,0:T(8,128)(2,1)S(1)} custom-call(bf16[16,256,1024]{2,1,0:T(8,128)(2,1)} %factors.5), custom_call_target="tpu_custom_call" | custom-call | bytes 8388608 | tf_op jit(solution)/shard_map/pallas_call | solution.py:76
  2.3 6.9 %collective-permute-start.4 = (bf16[8,256,1024]{2,1,0:T(8,128)(2,1)S(1)}, bf16[8,256,1024]{2,1,0:T(8,128)(2,1)S(1)}, u32[]{:S(2)}, u32[]{:S(2)}) collective-permute-start(bf16[8,256,1024]{2,1,0:T(8,128)(2,1)S(1)} %shard_map.17.refs_0_), channel_id=1, source_target_pairs={{0,248},{8,16},{16,8},{24,32},{32,24},{40,48},{48,40},{56,64},{64,... | collective-permute-start | bytes 12582920 | tf_op jit(solution)/shard_map/ppermute | solution.py:303
  9.2 1.0 shard_map.18.refs_0_.own1
  10.3 2.1 %shard_map.19.own0 = bf16[7,256,1024]{2,1,0:T(8,128)(2,1)S(1)} custom-call(bf16[16,256,1024]{2,1,0:T(8,128)(2,1)} %factors.5, bf16[1,256,1024]{2,1,0:T(8,128)(2,1)S(1)} %shard_map.18.refs_0_.own1), custom_call_target="tpu_custom_call" | custom-call | bytes 8388608 | tf_op jit(solution)/shard_map/pallas_call | solution.py:76
  12.4 4.1 %collective-permute-start.14 = (bf16[7,256,1024]{2,1,0:T(8,128)(2,1)S(1)}, bf16[7,256,1024]{2,1,0:T(8,128)(2,1)S(1)}, u32[]{:S(2)}, u32[]{:S(2)}) collective-permute-start(bf16[7,256,1024]{2,1,0:T(8,128)(2,1)S(1)} %shard_map.19.own0), channel_id=1, source_target_pairs={{0,240},{8,24},{16,0},{24,40},{32,16},{40,56},{48,32},{56,72},{64,... | collective-permute-start | bytes 11010056 | tf_op jit(solution)/shard_map/ppermute | solution.py:303
  16.6 5.0 %shard_map.20 = (f32[3,64,256]{2,1,0:T(8,128)S(1)}, f32[3,64,256]{2,1,0:T(8,128)S(1)}, f32[3,64,256]{2,1,0:T(8,128)S(1)}, f32[3,64,256]{2,1,0:T(8,128)S(1)}) custom-call(bf16[7,256,1024]{2,1,0:T(8,128)(2,1)S(1)} %shard_map.19.own0, bf16[1,256,1024]{2,1,0:T(8,128)(2,1)S(1)} %shard_map.18.refs_0_.own1, bf16[8,256,1024]{2,1,0:T(8,128)(2,1)S(1)} %collective-permute-done.mate0), custom_call_target="tpu_custom_call" | custom-call | flops 3221225472 | bytes 8388608 | tf_op jit(solution)/shard_map/pallas_call | solution.py:76
  21.5 1.4 collective-permute-start.1
  22.9 6.5 %collective-permute-done.1.b = f32[3,64,256]{2,1,0:T(8,128)S(1)} collective-permute-done((f32[3,64,256]{2,1,0:T(8,128)S(1)}, f32[3,64,256]{2,1,0:T(8,128)S(1)}, u32[]{:S(2)}, u32[]{:S(2)}) %collective-permute-start.1) | collective-permute-done | bytes 196640 | tf_op jit(solution)/shard_map/ppermute | solution.py:298
  29.5 7.0 %collective-permute-done.2.c = f32[3,64,256]{2,1,0:T(8,128)S(1)} collective-permute-done((f32[3,64,256]{2,1,0:T(8,128)S(1)}, f32[3,64,256]{2,1,0:T(8,128)S(1)}, u32[]{:S(2)}, u32[]{:S(2)}) %collective-permute-start.2) | collective-permute-done | bytes 196640 | tf_op jit(solution)/shard_map/ppermute | solution.py:298
  36.5 1.1 collective-permute-start.3
  37.7 5.6 %collective-permute-done.3.d = f32[3,64,256]{2,1,0:T(8,128)S(1)} collective-permute-done((f32[3,64,256]{2,1,0:T(8,128)S(1)}, f32[3,64,256]{2,1,0:T(8,128)S(1)}, u32[]{:S(2)}, u32[]{:S(2)}) %collective-permute-start.3) | collective-permute-done | bytes 196640 | tf_op jit(solution)/shard_map/ppermute | solution.py:298
  43.4 64.7 %collective-permute-done.6.far1 = bf16[1,256,1024]{2,1,0:T(8,128)(2,1)S(1)} collective-permute-done((bf16[1,256,1024]{2,1,0:T(8,128)(2,1)S(1)}, bf16[1,256,1024]{2,1,0:T(8,128)(2,1)S(1)}, u32[]{:S(2)}, u32[]{:S(2)}) %collective-permute-start.6) | collective-permute-done | bytes 524320 | tf_op jit(solution)/shard_map/ppermute | solution.py:303
  108.0 6.1 %shard_map.22 = (f32[4,64,256]{2,1,0:T(8,128)S(1)}, f32[4,64,256]{2,1,0:T(8,128)S(1)}, f32[4,64,256]{2,1,0:T(8,128)S(1)}, f32[4,64,256]{2,1,0:T(8,128)S(1)}) custom-call(bf16[7,256,1024]{2,1,0:T(8,128)(2,1)S(1)} %shard_map.19.own0, bf16[1,256,1024]{2,1,0:T(8,128)(2,1)S(1)} %shard_map.18.refs_0_.own1, bf16[8,256,1024]{2,1,0:T(8,128)(2,1)S(1)} %collective-permute-done.mate0, ...), custom_call_target="tpu_custom_call" | custom-call | flops 4294967296 | bytes 16777216 | tf_op jit(solution)/shard_map/pallas_call | solution.py:76
  114.1 1.4 collective-permute-start.7
  115.5 0.6 collective-permute-start.8
  116.1 1.1 collective-permute-start.9
  117.2 3.4 %collective-permute-done.7.b = f32[4,64,256]{2,1,0:T(8,128)S(1)} collective-permute-done((f32[4,64,256]{2,1,0:T(8,128)S(1)}, f32[4,64,256]{2,1,0:T(8,128)S(1)}, u32[]{:S(2)}, u32[]{:S(2)}) %collective-permute-start.7) | collective-permute-done | bytes 262176 | tf_op jit(solution)/shard_map/ppermute | solution.py:298
  120.6 2.8 %collective-permute-done.8.c = f32[4,64,256]{2,1,0:T(8,128)S(1)} collective-permute-done((f32[4,64,256]{2,1,0:T(8,128)S(1)}, f32[4,64,256]{2,1,0:T(8,128)S(1)}, u32[]{:S(2)}, u32[]{:S(2)}) %collective-permute-start.8) | collective-permute-done | bytes 262176 | tf_op jit(solution)/shard_map/ppermute | solution.py:298
  123.4 2.1 %collective-permute-done.9.d = f32[4,64,256]{2,1,0:T(8,128)S(1)} collective-permute-done((f32[4,64,256]{2,1,0:T(8,128)S(1)}, f32[4,64,256]{2,1,0:T(8,128)S(1)}, u32[]{:S(2)}, u32[]{:S(2)}) %collective-permute-start.9) | collective-permute-done | bytes 262176 | tf_op jit(solution)/shard_map/ppermute | solution.py:298
  125.7 13.8 %collective-permute-done.14.far0 = bf16[7,256,1024]{2,1,0:T(8,128)(2,1)S(1)} collective-permute-done((bf16[7,256,1024]{2,1,0:T(8,128)(2,1)S(1)}, bf16[7,256,1024]{2,1,0:T(8,128)(2,1)S(1)}, u32[]{:S(2)}, u32[]{:S(2)}) %collective-permute-start.14) | collective-permute-done | bytes 3670048 | tf_op jit(solution)/shard_map/ppermute | solution.py:303
  139.5 2.4 %shard_map.26.early = f32[1,256,256]{2,1,0:T(8,128)S(1)} custom-call(bf16[8,256,1024]{2,1,0:T(8,128)(2,1)S(1)} %collective-permute-done.4.near0, bf16[7,256,1024]{2,1,0:T(8,128)(2,1)S(1)} %collective-permute-done.14.far0), custom_call_target="tpu_custom_call" | custom-call | flops 939524096 | bytes 7864320 | tf_op jit(solution)/shard_map/pallas_call | solution.py:76
  142.0 3.1 %collective-permute-done.13.far1 = bf16[1,256,1024]{2,1,0:T(8,128)(2,1)S(1)} collective-permute-done((bf16[1,256,1024]{2,1,0:T(8,128)(2,1)S(1)}, bf16[1,256,1024]{2,1,0:T(8,128)(2,1)S(1)}, u32[]{:S(2)}, u32[]{:S(2)}) %collective-permute-start.13) | collective-permute-done | bytes 524320 | tf_op jit(solution)/shard_map/ppermute | solution.py:303
  145.7 1.4 collective-permute-done.15.given
  147.1 1.4 collective-permute-start.16
  148.5 0.7 collective-permute-start.17
  149.2 2.7 %collective-permute-start.11 = (f32[4,32,256]{2,1,0:T(8,128)S(1)}, f32[4,32,256]{2,1,0:T(8,128)S(1)}, u32[]{:S(2)}, u32[]{:S(2)}) collective-permute-start(f32[4,32,256]{2,1,0:T(8,128)S(1)} %get-tuple-element.34.hidden), channel_id=1, source_target_pairs={{0,1},{1,0},{2,3},{3,2},{4,5},{5,4},{6,7},{7,6},{8,9},{9,8},{10,11... | collective-permute-start | bytes 393224 | tf_op jit(solution)/shard_map/ppermute | solution.py:338
  152.0 0.8 collective-permute-done.17.second
  152.9 1.6 collective-permute-done.12.hidden.up
  154.5 1.2 collective-permute-start.19
  155.8 1.8 %collective-permute-done.11.come = f32[4,32,256]{2,1,0:T(8,128)S(1)} collective-permute-done((f32[4,32,256]{2,1,0:T(8,128)S(1)}, f32[4,32,256]{2,1,0:T(8,128)S(1)}, u32[]{:S(2)}, u32[]{:S(2)}) %collective-permute-start.11) | collective-permute-done | bytes 131104 | tf_op jit(solution)/shard_map/ppermute | solution.py:338
  157.6 5.1 %collective-permute-done.20.first = f32[32,256]{1,0:T(8,128)S(1)} collective-permute-done((f32[32,256]{1,0:T(8,128)S(1)}, f32[32,256]{1,0:T(8,128)S(1)}, u32[]{:S(2)}, u32[]{:S(2)}) %collective-permute-start.20) | collective-permute-done | bytes 32800 | tf_op jit(solution)/shard_map/ppermute | solution.py:360
  162.6 0.7 shard_map.32
  (28 shorter events, 1.5 us)
Async XLA Ops:
  2.2 14.3 %collective-permute-start = (bf16[8,256,1024]{2,1,0:T(8,128)(2,1)S(1)}, bf16[8,256,1024]{2,1,0:T(8,128)(2,1)S(1)}, u32[]{:S(2)}, u32[]{:S(2)}) collective-permute-start(bf16[8,256,1024]{2,1,0:T(8,128)(2,1)S(1)} %shard_map.17.refs_0_), channel_id=1, source_target_pairs={{0,8},{8,0},{16,24},{24,16},{32,40},{40,32},{48,56},{56,48},{64,72... | collective-permute-start | bytes 12582920 | tf_op jit(solution)/shard_map/ppermute | solution.py:303
  2.3 105.7 %collective-permute-start.4 = (bf16[8,256,1024]{2,1,0:T(8,128)(2,1)S(1)}, bf16[8,256,1024]{2,1,0:T(8,128)(2,1)S(1)}, u32[]{:S(2)}, u32[]{:S(2)}) collective-permute-start(bf16[8,256,1024]{2,1,0:T(8,128)(2,1)S(1)} %shard_map.17.refs_0_), channel_id=1, source_target_pairs={{0,248},{8,16},{16,8},{24,32},{32,24},{40,48},{48,40},{56,64},{64,... | collective-permute-start | bytes 12582920 | tf_op jit(solution)/shard_map/ppermute | solution.py:303
  12.3 95.7 %collective-permute-start.5 = (bf16[7,256,1024]{2,1,0:T(8,128)(2,1)S(1)}, bf16[7,256,1024]{2,1,0:T(8,128)(2,1)S(1)}, u32[]{:S(2)}, u32[]{:S(2)}) collective-permute-start(bf16[7,256,1024]{2,1,0:T(8,128)(2,1)S(1)} %shard_map.19.own0), channel_id=1, source_target_pairs={{0,16},{8,248},{16,32},{24,8},{32,48},{40,24},{48,64},{56,40},{64,... | collective-permute-start | bytes 11010056 | tf_op jit(solution)/shard_map/ppermute | solution.py:303
  12.4 127.1 %collective-permute-start.14 = (bf16[7,256,1024]{2,1,0:T(8,128)(2,1)S(1)}, bf16[7,256,1024]{2,1,0:T(8,128)(2,1)S(1)}, u32[]{:S(2)}, u32[]{:S(2)}) collective-permute-start(bf16[7,256,1024]{2,1,0:T(8,128)(2,1)S(1)} %shard_map.19.own0), channel_id=1, source_target_pairs={{0,240},{8,24},{16,0},{24,40},{32,16},{40,56},{48,32},{56,72},{64,... | collective-permute-start | bytes 11010056 | tf_op jit(solution)/shard_map/ppermute | solution.py:303
  21.5 7.9 %collective-permute-start.1 = (f32[3,64,256]{2,1,0:T(8,128)S(1)}, f32[3,64,256]{2,1,0:T(8,128)S(1)}, u32[]{:S(2)}, u32[]{:S(2)}) collective-permute-start(f32[3,64,256]{2,1,0:T(8,128)S(1)} %get-tuple-element.24), channel_id=1, source_target_pairs={{0,2},{1,3},{2,4},{3,5},{4,6},{5,7},{6,0},{7,1},{8,10},{9,11},{10,... | collective-permute-start | bytes 589832 | tf_op jit(solution)/shard_map/ppermute | solution.py:298
  22.9 85.2 %collective-permute-start.6 = (bf16[1,256,1024]{2,1,0:T(8,128)(2,1)S(1)}, bf16[1,256,1024]{2,1,0:T(8,128)(2,1)S(1)}, u32[]{:S(2)}, u32[]{:S(2)}) collective-permute-start(bf16[1,256,1024]{2,1,0:T(8,128)(2,1)S(1)} %shard_map.18.refs_0_.own1), channel_id=1, source_target_pairs={{0,16},{8,248},{16,32},{24,8},{32,48},{40,24},{48,64},{56,40},{64,... | collective-permute-start | bytes 1572872 | tf_op jit(solution)/shard_map/ppermute | solution.py:303
  29.4 7.2 %collective-permute-start.2 = (f32[3,64,256]{2,1,0:T(8,128)S(1)}, f32[3,64,256]{2,1,0:T(8,128)S(1)}, u32[]{:S(2)}, u32[]{:S(2)}) collective-permute-start(f32[3,64,256]{2,1,0:T(8,128)S(1)} %get-tuple-element.25), channel_id=1, source_target_pairs={{0,4},{1,5},{2,6},{3,7},{4,0},{5,1},{6,2},{7,3},{8,12},{9,13},{10,... | collective-permute-start | bytes 589832 | tf_op jit(solution)/shard_map/ppermute | solution.py:298
  36.5 6.8 %collective-permute-start.3 = (f32[3,64,256]{2,1,0:T(8,128)S(1)}, f32[3,64,256]{2,1,0:T(8,128)S(1)}, u32[]{:S(2)}, u32[]{:S(2)}) collective-permute-start(f32[3,64,256]{2,1,0:T(8,128)S(1)} %get-tuple-element.26), channel_id=1, source_target_pairs={{0,6},{1,7},{2,0},{3,1},{4,2},{5,3},{6,4},{7,5},{8,14},{9,15},{10,... | collective-permute-start | bytes 589832 | tf_op jit(solution)/shard_map/ppermute | solution.py:298
  114.1 6.5 %collective-permute-start.7 = (f32[4,64,256]{2,1,0:T(8,128)S(1)}, f32[4,64,256]{2,1,0:T(8,128)S(1)}, u32[]{:S(2)}, u32[]{:S(2)}) collective-permute-start(f32[4,64,256]{2,1,0:T(8,128)S(1)} %get-tuple-element.28), channel_id=1, source_target_pairs={{0,2},{1,3},{2,4},{3,5},{4,6},{5,7},{6,0},{7,1},{8,10},{9,11},{10,... | collective-permute-start | bytes 786440 | tf_op jit(solution)/shard_map/ppermute | solution.py:298
  115.5 7.9 %collective-permute-start.8 = (f32[4,64,256]{2,1,0:T(8,128)S(1)}, f32[4,64,256]{2,1,0:T(8,128)S(1)}, u32[]{:S(2)}, u32[]{:S(2)}) collective-permute-start(f32[4,64,256]{2,1,0:T(8,128)S(1)} %get-tuple-element.29), channel_id=1, source_target_pairs={{0,4},{1,5},{2,6},{3,7},{4,0},{5,1},{6,2},{7,3},{8,12},{9,13},{10,... | collective-permute-start | bytes 786440 | tf_op jit(solution)/shard_map/ppermute | solution.py:298
  116.1 9.4 %collective-permute-start.9 = (f32[4,64,256]{2,1,0:T(8,128)S(1)}, f32[4,64,256]{2,1,0:T(8,128)S(1)}, u32[]{:S(2)}, u32[]{:S(2)}) collective-permute-start(f32[4,64,256]{2,1,0:T(8,128)S(1)} %get-tuple-element.30), channel_id=1, source_target_pairs={{0,6},{1,7},{2,0},{3,1},{4,2},{5,3},{6,4},{7,5},{8,14},{9,15},{10,... | collective-permute-start | bytes 786440 | tf_op jit(solution)/shard_map/ppermute | solution.py:298
  117.2 27.9 %collective-permute-start.13 = (bf16[1,256,1024]{2,1,0:T(8,128)(2,1)S(1)}, bf16[1,256,1024]{2,1,0:T(8,128)(2,1)S(1)}, u32[]{:S(2)}, u32[]{:S(2)}) collective-permute-start(bf16[1,256,1024]{2,1,0:T(8,128)(2,1)S(1)} %shard_map.18.refs_0_.own1), channel_id=1, source_target_pairs={{0,240},{8,24},{16,0},{24,40},{32,16},{40,56},{48,32},{56,72},{64,... | collective-permute-start | bytes 1572872 | tf_op jit(solution)/shard_map/ppermute | solution.py:303
  125.6 16.3 %collective-permute-start.10 = (f32[4,64,256]{2,1,0:T(8,128)S(1)}, f32[4,64,256]{2,1,0:T(8,128)S(1)}, u32[]{:S(2)}, u32[]{:S(2)}) collective-permute-start(f32[4,64,256]{2,1,0:T(8,128)S(1)} %get-tuple-element.32), channel_id=1, source_target_pairs={{0,8},{8,0},{16,24},{24,16},{32,40},{40,32},{48,56},{56,48},{64,72... | collective-permute-start | bytes 786440 | tf_op jit(solution)/shard_map/ppermute | solution.py:303
  145.5 1.6 collective-permute-start.15
  145.6 8.9 %collective-permute-start.12 = (f32[4,32,256]{2,1,0:T(8,128)S(1)}, f32[4,32,256]{2,1,0:T(8,128)S(1)}, u32[]{:S(2)}, u32[]{:S(2)}) collective-permute-start(f32[4,32,256]{2,1,0:T(8,128)S(1)} %get-tuple-element.35), channel_id=1, source_target_pairs={{0,16},{1,24},{2,18},{3,26},{4,20},{5,28},{6,22},{7,30},{8,25},{9,... | collective-permute-start | bytes 393224 | tf_op jit(solution)/shard_map/ppermute | solution.py:358
  147.1 4.8 %collective-permute-start.16 = (f32[64,256]{1,0:T(8,128)S(1)}, f32[64,256]{1,0:T(8,128)S(1)}, u32[]{:S(2)}, u32[]{:S(2)}) collective-permute-start(f32[64,256]{1,0:T(8,128)S(1)} %get-tuple-element.37), channel_id=1, source_target_pairs={{0,2},{1,3},{2,4},{3,5},{4,6},{5,7},{6,0},{7,1},{8,12},{9,13},{10,... | collective-permute-start | bytes 196616 | tf_op jit(solution)/shard_map/ppermute | solution.py:354
  148.5 4.3 %collective-permute-start.17 = (f32[64,256]{1,0:T(8,128)S(1)}, f32[64,256]{1,0:T(8,128)S(1)}, u32[]{:S(2)}, u32[]{:S(2)}) collective-permute-start(f32[64,256]{1,0:T(8,128)S(1)} %get-tuple-element.38), channel_id=1, source_target_pairs={{0,6},{1,7},{2,0},{3,1},{4,2},{5,3},{6,4},{7,5},{8,14},{9,15},{10,... | collective-permute-start | bytes 196616 | tf_op jit(solution)/shard_map/ppermute | solution.py:354
  149.2 8.3 %collective-permute-start.11 = (f32[4,32,256]{2,1,0:T(8,128)S(1)}, f32[4,32,256]{2,1,0:T(8,128)S(1)}, u32[]{:S(2)}, u32[]{:S(2)}) collective-permute-start(f32[4,32,256]{2,1,0:T(8,128)S(1)} %get-tuple-element.34.hidden), channel_id=1, source_target_pairs={{0,1},{1,0},{2,3},{3,2},{4,5},{5,4},{6,7},{7,6},{8,9},{9,8},{10,11... | collective-permute-start | bytes 393224 | tf_op jit(solution)/shard_map/ppermute | solution.py:338
  152.8 1.7 %collective-permute-start.18 = (f32[32,256]{1,0:T(8,128)S(1)}, f32[32,256]{1,0:T(8,128)S(1)}, u32[]{:S(2)}, u32[]{:S(2)}) collective-permute-start(f32[32,256]{1,0:T(8,128)S(1)} %get-tuple-element.40), channel_id=1, source_target_pairs={{0,8},{8,0},{16,24},{24,16},{32,40},{40,32},{48,56},{56,48},{64,72... | collective-permute-start | bytes 98312 | tf_op jit(solution)/shard_map/ppermute | solution.py:303
  154.5 8.2 %collective-permute-start.19 = (f32[2,32,256]{2,1,0:T(8,128)S(1)}, f32[2,32,256]{2,1,0:T(8,128)S(1)}, u32[]{:S(2)}, u32[]{:S(2)}) collective-permute-start(f32[2,32,256]{2,1,0:T(8,128)S(1)} %shard_map.31), channel_id=1, source_target_pairs={{0,8},{8,0},{16,24},{24,16},{32,40},{40,32},{48,56},{56,48},{64,72... | collective-permute-start | bytes 196616 | tf_op jit(solution)/shard_map/ppermute | solution.py:303
  155.7 6.9 %collective-permute-start.20 = (f32[32,256]{1,0:T(8,128)S(1)}, f32[32,256]{1,0:T(8,128)S(1)}, u32[]{:S(2)}, u32[]{:S(2)}) collective-permute-start(f32[32,256]{1,0:T(8,128)S(1)} %shard_map.30.hidden), channel_id=1, source_target_pairs={{0,8},{1,9},{2,10},{3,11},{4,12},{5,13},{6,14},{7,15},{8,17},{9,16... | collective-permute-start | bytes 98312 | tf_op jit(solution)/shard_map/ppermute | solution.py:360
  155.8 6.8 %collective-permute-start.21 = (f32[32,256]{1,0:T(8,128)S(1)}, f32[32,256]{1,0:T(8,128)S(1)}, u32[]{:S(2)}, u32[]{:S(2)}) collective-permute-start(f32[32,256]{1,0:T(8,128)S(1)} %shard_map.30.hidden), channel_id=1, source_target_pairs={{0,16},{1,17},{2,18},{3,19},{4,20},{5,21},{6,22},{7,23},{8,10},{9,... | collective-permute-start | bytes 98312 | tf_op jit(solution)/shard_map/ppermute | solution.py:360
